TPU v7x, 32 devices: a whole 2x2x4 slice. The times are simulated.
32 devices in a mesh: ens: 1, lon: 16 (over z, y, x), lat: 2 (over core).
Axes of the slice: x: 2, y: 2, z: 4, core: 2. Of those that a mesh axis runs over, the one named last changes fastest.
Arguments:
- fields: bfloat16 [128, 64, 1024], P('lat', 'lon'), may hold values from -6 to 6
- land_mask: int32 [128, 64], P('lat', 'lon'), may hold values 0 or 1
- land_embed: float32 [1024], replicated, may hold values from -3 to 3
- column_gain: float32 [1024], replicated, may hold values from 0.1 to 1.9
- row_gain: float32 [1024], replicated, may hold values from 0.1 to 1.9
- column_slopes: float32 [8], replicated, may hold values from 0.02 to 0.3
- row_slopes: float32 [8], replicated, may hold values from 0.02 to 0.3
- column_project: bfloat16 [1024, 1536], P('lon', 'lat'), may hold values from -0.1875 to 0.1875
- column_output: bfloat16 [1024, 512], P('lon', 'lat'), may hold values from -0.5 to 0.5
- row_project: bfloat16 [1024, 1536], P('lon', 'lat'), may hold values from -0.1875 to 0.1875
- row_output: bfloat16 [1024, 512], P('lon', 'lat'), may hold values from -0.5 to 0.5
Outputs:
- block_output: bfloat16 [128, 64, 1024], P(('ens', 'lat'), 'lon')
All inputs are finite; a program needn't handle non-finite values. No bound on the sum of `land_mask` on one device may be relied on, other than what follows from the above.
Results may differ from a plain program's by a relative error of at most 0.012.
Values may be sent and summed in bfloat16 or wider, within the bound.
No kernel may reach another device: no remote copies, remote signals or barrier semaphores. Data moves between devices by JAX's collectives and lax.ppermute only.
A program may use at most 64 MiB of HBM per device.

v0:
```python
import math

import jax
import jax.numpy as jnp
from jax import lax
from jax.sharding import PartitionSpec as P

HS = 64


def passed_along(value, axis, by):
    length = lax.axis_size(axis)
    return lax.ppermute(value, axis, [(i, (i + by) % length) for i in range(length)])


def layer_norm(values, gain):
    center = values - jnp.mean(values, axis=-1, keepdims=True)
    spread = jnp.mean(center * center, axis=-1, keepdims=True)
    return center * lax.rsqrt(spread + 1e-05) * gain


def unit_rms(vectors):
    return vectors * lax.rsqrt(jnp.mean(vectors * vectors, axis=-1, keepdims=True) + 1e-06)


def head_split(projected):
    query = unit_rms(projected[..., 0, :]).astype(jnp.bfloat16)
    keyed = unit_rms(projected[..., 1, :]).astype(jnp.bfloat16)
    valued = projected[..., 2, :].astype(jnp.bfloat16)
    return (query, keyed, valued)


def gather_bands(normed):
    return lax.all_gather(normed, "lat", axis=0, tiled=True)


def sum_heads(partial_value):
    return lax.psum_scatter(
        partial_value.astype(jnp.bfloat16), "lat", scatter_dimension=0, tiled=True
    ).astype(jnp.float32)


def project_in(normed, weight):
    return jnp.dot(
        normed,
        lax.all_gather(weight, "lon", axis=0, tiled=True),
        preferred_element_type=jnp.float32,
    )


def project_out(mixed, weight):
    return lax.dot_general(
        mixed,
        lax.all_gather(weight, "lon", axis=0, tiled=True),
        (((1,), (1,)), ((), ())),
        preferred_element_type=jnp.float32,
    )


def column_attend(query, column_kv, far_kv, slopes):
    total_rows = column_kv.shape[0]
    keyed = jnp.concatenate([column_kv[..., :HS], far_kv[..., :HS]], axis=0)
    valued = jnp.concatenate([column_kv[..., HS:], far_kv[..., HS:]], axis=0)
    scores = jnp.einsum("rchd,schd->chrs", query, keyed, preferred_element_type=jnp.float32)
    rows_here = jnp.arange(query.shape[0], dtype=jnp.int32)
    key_rows = jnp.arange(total_rows, dtype=jnp.int32)
    near_dist = jnp.abs(rows_here[:, None] - key_rows[None, :])
    pair_sum = rows_here[:, None] + key_rows[None, :]
    far_dist = jnp.minimum(pair_sum + 1, 2 * total_rows - 1 - pair_sum)
    distance = jnp.concatenate([near_dist, far_dist], axis=1).astype(jnp.float32)
    weight = jnp.exp(scores * (1.0 / math.sqrt(HS)) - slopes[None, :, None, None] * distance)
    prob = (weight / jnp.sum(weight, axis=-1, keepdims=True)).astype(jnp.bfloat16)
    mixed = jnp.einsum("chrs,schd->rchd", prob, valued, preferred_element_type=jnp.float32)
    return mixed.astype(jnp.bfloat16).reshape(query.shape[0], query.shape[1], -1)


def shards(
    fields,
    land_mask,
    land_embed,
    column_gain,
    row_gain,
    column_slopes,
    row_slopes,
    column_project,
    column_output,
    row_project,
    row_output,
):
    lon_count = lax.axis_size("lon")
    lat_count = lax.axis_size("lat")
    band_rows, local_cols, width = fields.shape
    lat_place = lax.axis_index("lat")
    head_total = column_slopes.shape[0]
    head_share = head_total // lat_count
    first_head = lat_place * head_share
    start = fields.astype(jnp.float32) + land_mask.astype(jnp.float32)[..., None] * land_embed
    normed = layer_norm(start, column_gain).astype(jnp.bfloat16)
    whole = gather_bands(normed)
    projected = project_in(whole.reshape(-1, width), column_project)
    query, keyed, valued = head_split(
        projected.reshape(band_rows * lat_count, local_cols, head_share, 3, HS)
    )
    column_kv = jnp.concatenate([keyed, valued], axis=-1).reshape(
        band_rows * lat_count, local_cols, -1
    )
    slopes = lax.dynamic_slice_in_dim(column_slopes, first_head, head_share)
    far_kv = passed_along(column_kv, "lon", lon_count // 2)
    shaped = column_kv.shape[:2] + (head_share, 2 * HS)
    mixed = column_attend(query, column_kv.reshape(shaped), far_kv.reshape(shaped), slopes)
    partial_value = project_out(mixed.reshape(-1, head_share * HS), column_output)
    update = sum_heads(partial_value.reshape(band_rows * lat_count, local_cols, width))
    middle = start + update
    total_rows = band_rows * lat_count
    row_normed = layer_norm(middle, row_gain).astype(jnp.bfloat16)
    whole_rows = gather_bands(row_normed)
    projected = project_in(whole_rows.reshape(-1, width), row_project)
    query, keyed, valued = head_split(projected.reshape(total_rows, local_cols, head_share, 3, HS))
    packed = jnp.stack([query, keyed, valued], axis=3)
    parts = lax.all_to_all(packed, "lon", split_axis=0, concat_axis=1, tiled=True)
    few_rows, all_cols = (parts.shape[0], parts.shape[1])
    scores = jnp.einsum(
        "rchd,rehd->rhce", parts[..., 0, :], parts[..., 1, :], preferred_element_type=jnp.float32
    )
    cols_here = jnp.arange(all_cols, dtype=jnp.int32)
    gap = jnp.abs(cols_here[:, None] - cols_here[None, :])
    cycle_dist = jnp.minimum(gap, all_cols - gap).astype(jnp.float32)
    row_slope = lax.dynamic_slice_in_dim(row_slopes, first_head, head_share)
    weight = jnp.exp(scores * (1.0 / math.sqrt(HS)) - row_slope[None, :, None, None] * cycle_dist)
    prob = (weight / jnp.sum(weight, axis=-1, keepdims=True)).astype(jnp.bfloat16)
    row_mixed = jnp.einsum(
        "rhce,rehd->rchd", prob, parts[..., 2, :], preferred_element_type=jnp.float32
    )
    row_mixed = row_mixed.astype(jnp.bfloat16)
    back = lax.all_to_all(row_mixed, "lon", split_axis=1, concat_axis=0, tiled=True)
    partial_value = project_out(back.reshape(-1, head_share * HS), row_output)
    final_update = sum_heads(partial_value.reshape(total_rows, local_cols, width))
    return (middle + final_update).astype(jnp.bfloat16)


def solution(mesh):
    in_specs = (
        P("lat", "lon", None),
        P("lat", "lon"),
        P(),
        P(),
        P(),
        P(),
        P(),
        P("lon", "lat"),
        P("lon", "lat"),
        P("lon", "lat"),
        P("lon", "lat"),
    )
    out_specs = P(("ens", "lat"), "lon", None)
    return jax.shard_map(shards, mesh=mesh, in_specs=in_specs, out_specs=out_specs, check_vma=False)
```

profile of v0, /device:TPU:0, one launch (start us, length us, event | category | flops | bytes accessed | tf_op | source)
XLA Modules:
  0.0 326.6 jit_solution(141258692570913525)
XLA Ops:
  10.8 2.2 multiply_convert_fusion.1
  13.1 57.6 %all-gather.7.cloned.1.call-done = bf16[1024,768]{1,0:T(8,128)(2,1)} async-done(((bf16[64,768]{1,0:T(8,128)(2,1)}), bf16[1024,768]{1,0:T(8,128)(2,1)}) %all-gather.7.cloned.1.call-update) | async-done | bytes 1572880 | tf_op jit(solution)/shard_map/all_gather | solution.py:46
  70.7 2.6 copy.49
  73.3 6.8 %all-gather.5.cloned.1.call-done = bf16[128,4,1024]{2,0,1:T(8,128)(2,1)} async-done(((bf16[64,4,1024]{2,0,1:T(8,128)(2,1)}), bf16[128,4,1024]{2,0,1:T(8,128)(2,1)}) %all-gather.5.cloned.1.call-update) | async-done | bytes 1048592 | tf_op jit(solution)/shard_map/all_gather | solution.py:34
  80.1 2.7 fusion.6
  83.1 2.7 collective-permute-start
  86.1 51.6 %all_gather.20 = bf16[1024,256]{1,0:T(8,128)(2,1)S(1)} all-gather(bf16[64,256]{1,0:T(8,128)(2,1)S(1)} %copy-done.3), channel_id=1, replica_groups=mesh['ens'=1,'lon'=16,'lat'=2] {'lon'}, dimensions={0}, use_global_device_ids=true | all-gather | bytes 557056 | tf_op jit(solution)/shard_map/all_gather | solution.py:54
  139.1 1.5 convolution_convert_fusion.1
  141.2 7.4 %reduce-scatter.3.cloned.1.call-done = bf16[64,4,1024]{2,0,1:T(8,128)(2,1)} async-done(((bf16[128,4,1024]{2,0,1:T(8,128)(2,1)}), bf16[64,4,1024]{2,0,1:T(8,128)(2,1)}) %reduce-scatter.3.cloned.1.call-update) | async-done | bytes 524304 | tf_op jit(solution)/shard_map/reduce_scatter | solution.py:38
  148.6 1.5 fusion.21
  150.1 1.5 multiply_reduce_fusion
  152.9 57.8 %all-gather.11.cloned.1.call-done = bf16[1024,768]{1,0:T(8,128)(2,1)} async-done(((bf16[64,768]{1,0:T(8,128)(2,1)}), bf16[1024,768]{1,0:T(8,128)(2,1)}) %all-gather.11.cloned.1.call-update) | async-done | bytes 1572880 | tf_op jit(solution)/shard_map/all_gather | solution.py:46
  210.7 1.7 copy.52
  212.4 7.6 %all-gather.9.cloned.1.call-done = bf16[128,4,1024]{2,0,1:T(8,128)(2,1)} async-done(((bf16[64,4,1024]{2,0,1:T(8,128)(2,1)}), bf16[128,4,1024]{2,0,1:T(8,128)(2,1)}) %all-gather.9.cloned.1.call-update) | async-done | bytes 1048592 | tf_op jit(solution)/shard_map/all_gather | solution.py:34
  219.9 2.2 fusion.4
  222.6 1.8 copy.53
  224.4 1.9 reshape.142
  226.3 6.8 %all-to-all-start = ((bf16[16,2,12288]{2,1,0:T(2,128)(2,1)}), bf16[16,2,12288]{2,1,0:T(2,128)(2,1)S(1)}, u32[]{:S(2)}, u32[]{:S(2)}) async-start(bf16[16,2,12288]{2,1,0:T(2,128)(2,1)} %reshape.142), calls=%async_computation.1 | async-start | bytes 1572864 | tf_op jit(solution)/shard_map/all_to_all | solution.py:120
  233.3 19.9 %all-to-all-done = bf16[16,2,12288]{2,1,0:T(2,128)(2,1)S(1)} async-done(((bf16[16,2,12288]{2,1,0:T(2,128)(2,1)}), bf16[16,2,12288]{2,1,0:T(2,128)(2,1)S(1)}, u32[]{:S(2)}, u32[]{:S(2)}) %all-to-all-start) | async-done | bytes 786464 | tf_op jit(solution)/shard_map/all_to_all | solution.py:120
  257.2 1.9 fusion.3
  261.1 5.1 %all-to-all-start.1 = ((bf16[16,2,4096]{2,1,0:T(2,128)(2,1)}), bf16[16,2,4096]{2,1,0:T(2,128)(2,1)S(1)}, u32[]{:S(2)}, u32[]{:S(2)}) async-start(bf16[16,2,4096]{2,1,0:T(2,128)(2,1)} %reshape.144), calls=%async_computation.2 | async-start | bytes 524288 | tf_op jit(solution)/shard_map/all_to_all | solution.py:135
  266.2 43.8 %all_gather.23 = bf16[1024,256]{1,0:T(8,128)(2,1)S(1)} all-gather(bf16[64,256]{1,0:T(8,128)(2,1)S(1)} %copy-done.4), channel_id=1, replica_groups=mesh['ens'=1,'lon'=16,'lat'=2] {'lon'}, dimensions={0}, use_global_device_ids=true | all-gather | bytes 557056 | tf_op jit(solution)/shard_map/all_gather | solution.py:54
  312.5 4.6 %reduce-scatter.5.cloned.1.call-done = bf16[64,4,1024]{2,0,1:T(8,128)(2,1)} async-done(((bf16[128,4,1024]{2,0,1:T(8,128)(2,1)}), bf16[64,4,1024]{2,0,1:T(8,128)(2,1)}) %reduce-scatter.5.cloned.1.call-update) | async-done | bytes 524304 | tf_op jit(solution)/shard_map/reduce_scatter | solution.py:38
  317.1 1.4 add_convert_fusion
  (71 shorter events, 18.3 us)
Async XLA Ops:
  6.5 64.2 %all-gather.7.cloned.1.call-start = ((), (), s32[]{:S(2)}) async-start(), calls=%async_computation.5 | async-start | bytes 1671168 | tf_op jit(solution)/shard_map/all_gather | solution.py:46
  7.3 72.8 %all-gather.5.cloned.1.call-start = ((), (), s32[]{:S(2)}) async-start(), calls=%async_computation.4 | async-start | bytes 1572864 | tf_op jit(solution)/shard_map/all_gather | solution.py:34
  13.0 135.6 %reduce-scatter.3.cloned.1.call-start = ((), (), s32[]{:S(2)}) async-start(), calls=%async_computation.6 | async-start | bytes 1572864 | tf_op jit(solution)/shard_map/reduce_scatter | solution.py:38
  82.9 2.9 copy-start.6
  82.9 3.1 copy-start.3
  83.1 54.5 %collective-permute-start = (bf16[128,4,512]{0,2,1:T(8,128)(2,1)S(1)}, bf16[128,4,512]{0,2,1:T(8,128)(2,1)S(1)}, u32[]{:S(2)}, u32[]{:S(2)}) collective-permute-start(bf16[128,4,512]{0,2,1:T(8,128)(2,1)S(1)} %bitcast.90), channel_id=1, source_target_pairs={{0,16},{2,18},{4,20},{6,22},{8,24},{10,26},{12,28},{14,30},{16,0},... | collective-permute-start | bytes 1572872 | tf_op jit(solution)/shard_map/ppermute | solution.py:13
  139.1 9.5 %copy-start = (bf16[64,4,1024]{2,1,0:T(4,128)(2,1)S(1)}, bf16[64,4,1024]{2,1,0:T(4,128)(2,1)}, u32[]{:S(2)}) copy-start(bf16[64,4,1024]{2,1,0:T(4,128)(2,1)} %param.11) | copy-start | bytes 1572868
  139.1 9.5 %copy-start.2 = (f32[1024]{0:T(1024)S(1)}, f32[1024]{0:T(1024)}, u32[]{:S(2)}) copy-start(f32[1024]{0:T(1024)} %param.13) | copy-start | bytes 12292
  140.6 11.0 %copy-start.5 = (f32[1024]{0:T(1024)S(1)}, f32[1024]{0:T(1024)}, u32[]{:S(2)}) copy-start(f32[1024]{0:T(1024)} %param.15) | copy-start | bytes 12292
  140.6 70.0 %all-gather.11.cloned.1.call-start = ((), (), s32[]{:S(2)}) async-start(), calls=%async_computation.8 | async-start | bytes 1671168 | tf_op jit(solution)/shard_map/all_gather | solution.py:46
  141.2 78.7 %all-gather.9.cloned.1.call-start = ((), (), s32[]{:S(2)}) async-start(), calls=%async_computation.7 | async-start | bytes 1572864 | tf_op jit(solution)/shard_map/all_gather | solution.py:34
  148.6 3.0 copy-start.1
  224.4 8.7 %copy-start.7 = (f32[8]{0:T(128)S(1)}, f32[8]{0:T(128)}, u32[]{:S(2)}) copy-start(f32[8]{0:T(128)} %param.17) | copy-start | bytes 100
  226.3 26.9 %all-to-all-start = ((bf16[16,2,12288]{2,1,0:T(2,128)(2,1)}), bf16[16,2,12288]{2,1,0:T(2,128)(2,1)S(1)}, u32[]{:S(2)}, u32[]{:S(2)}) async-start(bf16[16,2,12288]{2,1,0:T(2,128)(2,1)} %reshape.142), calls=%async_computation.1 | async-start | bytes 1572864 | tf_op jit(solution)/shard_map/all_to_all | solution.py:120
  259.2 7.0 %copy-start.4 = (bf16[64,256]{1,0:T(8,128)(2,1)S(1)}, bf16[64,256]{1,0:T(8,128)(2,1)}, u32[]{:S(2)}) copy-start(bf16[64,256]{1,0:T(8,128)(2,1)} %param.21) | copy-start | bytes 98308
  261.1 49.0 %all-to-all-start.1 = ((bf16[16,2,4096]{2,1,0:T(2,128)(2,1)}), bf16[16,2,4096]{2,1,0:T(2,128)(2,1)S(1)}, u32[]{:S(2)}, u32[]{:S(2)}) async-start(bf16[16,2,4096]{2,1,0:T(2,128)(2,1)} %reshape.144), calls=%async_computation.2 | async-start | bytes 524288 | tf_op jit(solution)/shard_map/all_to_all | solution.py:135
  266.2 50.9 %reduce-scatter.5.cloned.1.call-start = ((), (), s32[]{:S(2)}) async-start(), calls=%async_computation.9 | async-start | bytes 1572864 | tf_op jit(solution)/shard_map/reduce_scatter | solution.py:38
Sparse Core Ops, SparseCore 0:
  10.1 60.5 all-gather.6
  72.3 7.7 all-gather.4
  140.7 7.8 reduce-scatter.2
  151.6 58.9 all-gather.10
  212.1 7.7 all-gather.8
  312.6 4.3 reduce-scatter.4
where the time goes:
time: 327 us
  waiting for transfers between devices  163 us (50%)
  blocking collectives  95.4 us (29%)
  local copies, waits for them, and re-layouts  15 us (5%)
  starting transfers between devices  14.8 us (5%)
  between operations  13.8 us (4%)
  matrix products  12.6 us (4%)
  other arithmetic  12.2 us (4%)
    all_gather x2, waiting for transfers between devices, project_in(): lax.all_gather(weight, 'lon', axis=0, tiled=True)  115 us
    all_gather x2, blocking collectives, project_out(): lax.all_gather(weight, 'lon', axis=0, tiled=True)  95.4 us
    all_to_all x1, waiting for transfers between devices, shards(): lax.all_to_all(packed, 'lon', split_axis=0, concat_axis=1, tiled=True)  19.9 us
    all_gather x2, waiting for transfers between devices, gather_bands(): return lax.all_gather(normed, 'lat', axis=0, tiled=True)  14.3 us
    reduce_scatter x2, waiting for transfers between devices, sum_heads(): lax.psum_scatter(partial_value.astype(jnp.bfloat16), 'lat', scatter_dimen...  11.9 us
    all_to_all x1, starting transfers between devices, shards(): lax.all_to_all(packed, 'lon', split_axis=0, concat_axis=1, tiled=True)  6.79 us
  transfers between devices with their start and end apart: 9, of which 7 were waited for; matrix products, arithmetic and copies ran while one was open for 4% of the time, Pallas kernels for 0%

commit v1 on v0

--- a/solution.py
+++ b/solution.py
@@ -1,11 +1,338 @@
+import functools
 import math
 
 import jax
 import jax.numpy as jnp
 from jax import lax
+from jax.experimental import pallas as pl
+from jax.experimental.pallas import tpu as pltpu
 from jax.sharding import PartitionSpec as P
 
 HS = 64
+PAIR = 2 * HS
+PLANE = 4
+NEVER = -1e30
+
+
+def at(place, length):
+    return [(i, place(i)) for i in range(length)]
+
+
+def swap_bands(value):
+    return lax.ppermute(value, "lat", at(lambda i: 1 - i, 2))
+
+
+def whole(shape, index=None):
+    return pl.BlockSpec(shape, lambda _: index or (0,) * len(shape))
+
+
+SCALARS = pl.BlockSpec(memory_space=pltpu.SMEM)
+
+
+def call(kernel, out, name, in_specs, scratch=(), cost=1e9):
+    return pl.pallas_call(
+        kernel,
+        grid=(1,),
+        out_shape=out,
+        in_specs=in_specs,
+        out_specs=jax.tree.map(lambda o: whole(o.shape), out),
+        scratch_shapes=scratch,
+        compiler_params=pltpu.CompilerParams(vmem_limit_bytes=40 * 2**20),
+        cost_estimate=pl.CostEstimate(flops=int(cost), bytes_accessed=4 * 2**20, transcendentals=2**19),
+        name=name,
+    )
+
+
+def dot(a, b):
+    return jnp.dot(a, b, preferred_element_type=jnp.float32)
+
+
+def dot_t(a, b):
+    return lax.dot_general(a, b, (((1,), (1,)), ((), ())), preferred_element_type=jnp.float32)
+
+
+def iota(shape, axis):
+    return lax.broadcasted_iota(jnp.int32, shape, axis)
+
+
+def by_kind(weight):
+    rows, cols = weight.shape
+    heads = cols // (3 * HS)
+    return weight.reshape(rows, heads, 3, HS).transpose(0, 2, 1, 3).reshape(rows, cols)
+
+
+def along_lines(weight, length):
+    lines = length // PLANE
+    parts = [weight]
+    for k in range(1, lines):
+        parts.append(lax.ppermute(weight, "lon", at(lambda i: (i + PLANE * k) % length, length)))
+    return jnp.concatenate(parts, axis=0)
+
+
+def across_plane(part, length):
+    return [part] + [lax.ppermute(part, "lon", at(lambda i: i ^ k, length)) for k in range(1, PLANE)]
+
+
+def put_in_order(target, pieces, place, rows):
+    lines = pieces[0].shape[0] // rows
+    line, spot = place[0] // PLANE, place[0] % PLANE
+    for j, piece in enumerate(pieces):
+        for k in range(lines):
+            owner = lax.rem(line - k + lines, lines) * PLANE + lax.bitwise_xor(spot, j)
+            target[pl.ds(pl.multiple_of(owner * rows, rows), rows), :] = piece[
+                k * rows : (k + 1) * rows, :
+            ]
+
+
+def norm(values, gain):
+    center = values - jnp.mean(values, axis=-1, keepdims=True)
+    spread = jnp.mean(center * center, axis=-1, keepdims=True)
+    return center * lax.rsqrt(spread + 1e-05) * gain
+
+
+def land_start(tokens_ref, mask_ref, embed_ref):
+    rows, cols = mask_ref.shape
+    total = rows * cols
+    row_of = (iota((total, rows), 0) // cols == iota((total, rows), 1)).astype(jnp.bfloat16)
+    spread = dot(row_of, mask_ref[...].astype(jnp.bfloat16))
+    own = iota((total, cols), 0) % cols == iota((total, cols), 1)
+    land = jnp.sum(jnp.where(own, spread, 0.0), axis=1, keepdims=True)
+    return tokens_ref[...].astype(jnp.float32) + land * embed_ref[...]
+
+
+def reorder(total, minor):
+    major = total // minor
+    d, t = iota((total, total), 0), iota((total, total), 1)
+    return (t == (d % major) * minor + d // major).astype(jnp.bfloat16)
+
+
+def start_kernel(tokens_ref, mask_ref, embed_ref, gain_ref, out_ref):
+    start = land_start(tokens_ref, mask_ref, embed_ref)
+    normed = norm(start, gain_ref[...]).astype(jnp.bfloat16)
+    cols = mask_ref.shape[1]
+    out_ref[...] = dot(reorder(normed.shape[0], cols), normed).astype(jnp.bfloat16)
+
+
+def unit_heads(vectors, scale=1.0):
+    width = vectors.shape[1]
+    same = (iota((width, width), 0) // HS == iota((width, width), 1) // HS).astype(jnp.bfloat16)
+    total = dot((vectors * vectors).astype(jnp.bfloat16), same)
+    return (vectors * (lax.rsqrt(total * (1.0 / HS) + 1e-06) * scale)).astype(jnp.bfloat16)
+
+
+def two_heads(query, keyed, valued, bias):
+    rows = query.shape[0]
+    first = iota(query.shape, 1) < HS
+    zero = jnp.zeros_like(query)
+    stacked = jnp.concatenate([jnp.where(first, query, zero), jnp.where(first, zero, query)], axis=0)
+    weight = jnp.exp(dot_t(stacked, keyed) + bias).astype(jnp.bfloat16)
+    widened = jnp.concatenate([valued, jnp.ones_like(valued)], axis=1)
+    mixed = dot(weight, widened)
+    mixed = mixed[:, :PAIR] / mixed[:, PAIR:]
+    return jnp.where(first, mixed[:rows], mixed[rows:]).astype(jnp.bfloat16)
+
+
+def column_kernel(
+    shard, cols, place, slopes, own, other, far_own, far_other, w0, w1, w2, w3, out_own, out_other, weight, qkv, far
+):
+    put_in_order(weight, (w0, w1, w2, w3), place, shard)
+    tokens = own.shape[0]
+    band = tokens // cols
+    width = weight.shape[1] // 3
+    for half, ref in enumerate((own, other)):
+        at_rows = slice(half * tokens, (half + 1) * tokens)
+        projected = dot(ref[...], weight[...])
+        qkv[at_rows, :width] = unit_heads(projected[:, :width], 1.0 / math.sqrt(HS))
+        qkv[at_rows, width : 2 * width] = unit_heads(projected[:, width : 2 * width])
+        qkv[at_rows, 2 * width :] = projected[:, 2 * width :].astype(jnp.bfloat16)
+    for half, ref in enumerate((far_own, far_other)):
+        at_rows = slice(half * tokens, (half + 1) * tokens)
+        projected = dot(ref[...], weight[:, width:])
+        far[at_rows, :width] = unit_heads(projected[:, :width])
+        far[at_rows, width:] = projected[:, width:].astype(jnp.bfloat16)
+    total = 2 * band
+    lat = place[1]
+    shape = (total, 2 * total)
+    spot_q, spot_k = iota(shape, 0), iota(shape, 1)
+    shift = lat * band
+    row_q = (spot_q + shift) % total
+    row_k = (spot_k % total + shift) % total
+    near = jnp.abs(row_q - row_k)
+    pair_sum = row_q + row_k
+    beyond = jnp.minimum(pair_sum + 1, 2 * total - 1 - pair_sum)
+    distance = jnp.where(spot_k < total, near, beyond).astype(jnp.float32)
+    mixed_own, mixed_other = [], []
+    for pair in range(width // PAIR):
+        bias = jnp.concatenate(
+            [distance * -slopes[2 * pair], distance * -slopes[2 * pair + 1]], axis=0
+        )
+        lanes = lambda kind: slice(kind * width + pair * PAIR, kind * width + (pair + 1) * PAIR)
+        got_own, got_other = [], []
+        for c in range(cols):
+            here = slice(c * band, (c + 1) * band)
+            there = slice(tokens + c * band, tokens + (c + 1) * band)
+            both = lambda ref, kind: [ref[here, lanes(kind)], ref[there, lanes(kind)]]
+            query = jnp.concatenate(both(qkv, 0), axis=0)
+            keyed = jnp.concatenate(both(qkv, 1) + both(far, 0), axis=0)
+            valued = jnp.concatenate(both(qkv, 2) + both(far, 1), axis=0)
+            mixed = two_heads(query, keyed, valued, bias)
+            got_own.append(mixed[:band])
+            got_other.append(mixed[band:])
+        mixed_own.append(jnp.concatenate(got_own, axis=0))
+        mixed_other.append(jnp.concatenate(got_other, axis=0))
+    back = reorder(tokens, band)
+    out_own[...] = dot(back, jnp.concatenate(mixed_own, axis=1)).astype(jnp.bfloat16)
+    out_other[...] = dot(back, jnp.concatenate(mixed_other, axis=1)).astype(jnp.bfloat16)
+
+
+def middle_kernel(
+    shard, place, tokens, mask, embed, gain, mine, theirs, w0, w1, w2, w3, u0, u1, u2, u3, middle, out, near, far
+):
+    put_in_order(near, (w0, w1, w2, w3), place, shard)
+    put_in_order(far, (u0, u1, u2, u3), place, shard)
+    update = dot_t(mine[...], near[...]) + dot_t(theirs[...], far[...])
+    value = land_start(tokens, mask, embed) + update
+    middle[...] = value
+    out[...] = norm(value, gain[...]).astype(jnp.bfloat16)
+
+
+def row_kernel(shard, cols, rows, place, slopes, tokens, w0, w1, w2, w3, u0, u1, u2, u3, out, near, far):
+    put_in_order(near, (w0, w1, w2, w3), place, shard)
+    put_in_order(far, (u0, u1, u2, u3), place, shard)
+    total = tokens.shape[0]
+    block = cols * rows
+    lon_count = total // block
+    circle = lon_count * cols
+    spot_q, spot_k = iota((total, total), 0), iota((total, total), 1)
+    lon_of = lambda spot: spot // block * cols + spot % cols
+    row_of = lambda spot: spot % block // cols
+    gap = jnp.abs(lon_of(spot_q) - lon_of(spot_k))
+    distance = jnp.minimum(gap, circle - gap).astype(jnp.float32)
+    same = row_of(spot_q) == row_of(spot_k)
+    width = near.shape[1] // 3
+    heads = width // HS
+    for half, ref in enumerate((near, far)):
+        projected = dot(tokens[...], ref[...])
+        query = unit_heads(projected[:, :width], 1.0 / math.sqrt(HS))
+        keyed = unit_heads(projected[:, width : 2 * width])
+        valued = projected[:, 2 * width :].astype(jnp.bfloat16)
+        for pair in range(width // PAIR):
+            lanes = slice(pair * PAIR, (pair + 1) * PAIR)
+            bias = jnp.concatenate(
+                [
+                    jnp.where(same, distance * -slopes[half * heads + 2 * pair + one], NEVER)
+                    for one in range(2)
+                ],
+                axis=0,
+            )
+            mixed = two_heads(query[:, lanes], keyed[:, lanes], valued[:, lanes], bias)
+            start = half * width + pair * PAIR
+            out[:, start : start + PAIR] = mixed
+
+
+def final_kernel(shard, place, middle, mixed, w0, w1, w2, w3, u0, u1, u2, u3, out, near, far):
+    put_in_order(near, (w0, w1, w2, w3), place, shard)
+    put_in_order(far, (u0, u1, u2, u3), place, shard)
+    width = near.shape[1]
+    update = dot_t(mixed[:, :width], near[...]) + dot_t(mixed[:, width:], far[...])
+    out[...] = (middle[...] + update).astype(jnp.bfloat16)
+
+
+def fast(
+    fields,
+    land_mask,
+    land_embed,
+    column_gain,
+    row_gain,
+    column_slopes,
+    row_slopes,
+    column_project,
+    column_output,
+    row_project,
+    row_output,
+):
+    lon_count = lax.axis_size("lon")
+    lat = lax.axis_index("lat")
+    lon = lax.axis_index("lon")
+    band, cols, width = fields.shape
+    tokens = band * cols
+    heads = column_slopes.shape[0]
+    half = heads // 2
+    attend = half * HS
+    shard = column_project.shape[0]
+    place = jnp.stack([lon, lat]).astype(jnp.int32)
+    embed, column_gain, row_gain = (v.reshape(1, width) for v in (land_embed, column_gain, row_gain))
+    own_slopes = lax.dynamic_slice_in_dim(column_slopes, lat * half, half)
+    turned = jnp.roll(row_slopes, -lat * half)
+
+    first = along_lines(by_kind(column_project), lon_count)
+    flat = fields.reshape(tokens, width)
+    bf16 = lambda *shape: jax.ShapeDtypeStruct(shape, jnp.bfloat16)
+    f32 = lambda *shape: jax.ShapeDtypeStruct(shape, jnp.float32)
+    token_block = whole((tokens, width))
+    mask_block = whole((band, cols))
+    row_block = whole((1, width))
+    normed = call(
+        start_kernel,
+        bf16(tokens, width),
+        "column_normed",
+        [token_block, mask_block, row_block, row_block],
+    )(flat, land_mask, embed, column_gain)
+    other = swap_bands(normed)
+    far_own = lax.ppermute(normed, "lon", at(lambda i: (i + lon_count // 2) % lon_count, lon_count))
+    pieces = across_plane(first, lon_count)
+    far_other = swap_bands(far_own)
+
+    rest = jnp.concatenate([by_kind(row_project), column_output, row_output], axis=1)
+    rest = along_lines(rest, lon_count)
+    rest_near = across_plane(rest, lon_count)
+    rest_far = [swap_bands(piece) for piece in rest_near]
+
+    part = rest.shape[0]
+    project_specs = [whole((part, 3 * attend))] * PLANE
+    column_out_specs = [whole((part, attend), (0, 3))] * PLANE
+    row_out_specs = [whole((part, attend), (0, 4))] * PLANE
+    wide = pltpu.VMEM((shard * lon_count, 3 * attend), jnp.bfloat16)
+    narrow = pltpu.VMEM((shard * lon_count, attend), jnp.bfloat16)
+
+    mixed_own, mixed_other = call(
+        functools.partial(column_kernel, shard, cols),
+        (bf16(tokens, attend), bf16(tokens, attend)),
+        "column_attention",
+        [SCALARS, SCALARS] + [token_block] * 4 + project_specs,
+        [
+            wide,
+            pltpu.VMEM((2 * tokens, 3 * attend), jnp.bfloat16),
+            pltpu.VMEM((2 * tokens, 2 * attend), jnp.bfloat16),
+        ],
+    )(place, own_slopes, normed, other, far_own, far_other, *pieces)
+    theirs = swap_bands(mixed_other)
+    mixed_block = whole((tokens, attend))
+    middle, row_normed = call(
+        functools.partial(middle_kernel, shard),
+        (f32(tokens, width), bf16(tokens, width)),
+        "middle",
+        [SCALARS, token_block, mask_block, row_block, row_block, mixed_block, mixed_block]
+        + column_out_specs * 2,
+        [narrow, narrow],
+    )(place, flat, land_mask, embed, row_gain, mixed_own, theirs, *rest_near, *rest_far)
+    spread = lax.all_to_all(row_normed, "lon", split_axis=0, concat_axis=0, tiled=True)
+    row_mixed = call(
+        functools.partial(row_kernel, shard, cols, band // lon_count),
+        bf16(tokens, 2 * attend),
+        "row_attention",
+        [SCALARS, SCALARS, token_block] + project_specs * 2,
+        [wide, wide],
+    )(place, turned, spread, *rest_near, *rest_far)
+    back = lax.all_to_all(row_mixed, "lon", split_axis=0, concat_axis=0, tiled=True)
+    out = call(
+        functools.partial(final_kernel, shard),
+        bf16(tokens, width),
+        "block_output",
+        [SCALARS, token_block, whole((tokens, 2 * attend))] + row_out_specs * 2,
+        [narrow, narrow],
+    )(place, middle, back, *rest_near, *rest_far)
+    return out.reshape(band, cols, width)
 
 
 def passed_along(value, axis, by):
@@ -74,7 +401,7 @@
     return mixed.astype(jnp.bfloat16).reshape(query.shape[0], query.shape[1], -1)
 
 
-def shards(
+def general(
     fields,
     land_mask,
     land_embed,
@@ -153,4 +480,10 @@
         P("lon", "lat"),
     )
     out_specs = P(("ens", "lat"), "lon", None)
+
+    def shards(fields, *rest):
+        length = lax.axis_size("lon")
+        suits = fields.shape[0] % length == 0 and length in (2 * PLANE, 4 * PLANE)
+        return (fast if suits else general)(fields, *rest)
+
     return jax.shard_map(shards, mesh=mesh, in_specs=in_specs, out_specs=out_specs, check_vma=False)

time: 327 us -> 131 us (0.40)
  waiting for transfers between devices: 163 us -> 52.8 us
  blocking collectives: 95.4 us -> 13 us
  starting transfers between devices: 14.8 us -> 35 us
  between operations: 13.8 us -> 0.32 us
  Pallas kernels: 0 us -> 12.8 us
  matrix products: 12.6 us -> 0 us
  other arithmetic: 12.2 us -> 0.19 us
    all_gather x4 -> x0, waiting for transfers between devices: 130 us -> none  [the longest x2 115 us: project_in(): lax.all_gather(weight, 'lon', axis=0, tiled=True)]
    all_gather x2 -> x0, blocking collectives: 95.4 us -> none  [project_out(): lax.all_gather(weight, 'lon', axis=0, tiled=True)]
    ppermute x1 -> x20, waiting for transfers between devices: 0.01 us -> 37.5 us  [the longest x1 22.3 us: fast(): lax.ppermute(normed, 'lon', at(lambda i: (i + lon_count // 2) % lon_count...]
    ppermute x1 -> x20, starting transfers between devices: 2.72 us -> 30.3 us  [the longest x6 18.9 us: along_lines(): lax.ppermute(weight, 'lon', at(lambda i: (i + PLANE * k) % length, length))]
    all_to_all x0 -> x1, blocking collectives: none -> 13 us  [fast(): lax.all_to_all(row_mixed, 'lon', split_axis=0, concat_axis=0, tiled=True)]
    pallas_call x0 -> x5, Pallas kernels: none -> 12.8 us  [the longest x1 4.38 us: fast(): call(functools.partial(column_kernel, shard, cols), (bf16(tokens, attend)...]
    dot_general x8 -> x0, matrix products: 12.6 us -> none  [the longest x2 4.97 us: project_in(): jnp.dot(normed, lax.all_gather(weight, 'lon', axis=0, tiled=True), prefer...]
    reduce_scatter x2 -> x0, waiting for transfers between devices: 11.9 us -> none  [sum_heads(): lax.psum_scatter(partial_value.astype(jnp.bfloat16), 'lat', scatter_dimen...]
  transfers between devices with their start and end apart: 9 -> 21, of which waited for: 7 -> 7; matrix products, arithmetic and copies ran while one was open for 4% -> 3% of each run, Pallas kernels for 0% -> 4%
where the time goes in v1:
time: 131 us
  waiting for transfers between devices  52.8 us (40%)
  starting transfers between devices  35 us (27%)
  local copies, waits for them, and re-layouts  16.6 us (13%)
  blocking collectives  13 us (10%)
  Pallas kernels  12.8 us (10%)
    ppermute x1, waiting for transfers between devices, fast(): lax.ppermute(normed, 'lon', at(lambda i: (i + lon_count // 2) % lon_count...  22.3 us
    ppermute x6, starting transfers between devices, along_lines(): lax.ppermute(weight, 'lon', at(lambda i: (i + PLANE * k) % length, length))  18.9 us
    all_to_all x1, waiting for transfers between devices, fast(): lax.all_to_all(row_normed, 'lon', split_axis=0, concat_axis=0, tiled=True)  15.3 us
    all_to_all x1, blocking collectives, fast(): lax.all_to_all(row_mixed, 'lon', split_axis=0, concat_axis=0, tiled=True)  13 us
    unnamed x54, local copies, waits for them, and re-layouts  11.8 us
    ppermute x6, waiting for transfers between devices, across_plane(): lax.ppermute(part, 'lon', at(lambda i: i ^ k, length))  11.8 us
    ppermute x6, starting transfers between devices, across_plane(): lax.ppermute(part, 'lon', at(lambda i: i ^ k, length))  8.05 us
    all_to_all x1, starting transfers between devices, fast(): lax.all_to_all(row_normed, 'lon', split_axis=0, concat_axis=0, tiled=True)  4.69 us
  transfers between devices with their start and end apart: 21, of which 7 were waited for; matrix products, arithmetic and copies ran while one was open for 3% of the time, Pallas kernels for 4%

profile of v1, /device:TPU:0, one launch (start us, length us, event | category | flops | bytes accessed | tf_op | source)
XLA Modules:
  0.0 130.7 jit_solution(12126876751806573279)
XLA Ops:
  0.0 1.1 reshape.35
  1.4 5.1 %collective-permute-start.5 = (bf16[64,768]{1,0:T(8,128)(2,1)S(1)}, bf16[64,768]{1,0:T(8,128)(2,1)S(1)}, u32[]{:S(2)}, u32[]{:S(2)}) collective-permute-start(bf16[64,768]{1,0:T(8,128)(2,1)S(1)} %reshape.36), channel_id=1, source_target_pairs={{0,24},{2,26},{4,28},{6,30},{8,0},{10,2},{12,4},{14,6},{16,8},{18,... | collective-permute-start | bytes 294920 | tf_op jit(solution)/shard_map/ppermute | solution.py:68
  8.1 2.9 %collective-permute-start.12 = (bf16[64,1280]{1,0:T(8,128)(2,1)S(1)}, bf16[64,1280]{1,0:T(8,128)(2,1)S(1)}, u32[]{:S(2)}, u32[]{:S(2)}) collective-permute-start(bf16[64,1280]{1,0:T(8,128)(2,1)S(1)} %constant_dynamic-update-slice_fusion.4), channel_id=1, source_target_pairs={{0,24},{2,26},{4,28},{6,30},{8,0},{10,2},{12,4},{14,6},{16,8},{18,... | collective-permute-start | bytes 491528 | tf_op jit(solution)/shard_map/ppermute | solution.py:68
  10.9 1.1 collective-permute-start.11
  12.7 2.1 %collective-permute-done.3 = bf16[64,768]{1,0:T(8,128)(2,1)S(1)} collective-permute-done((bf16[64,768]{1,0:T(8,128)(2,1)S(1)}, bf16[64,768]{1,0:T(8,128)(2,1)S(1)}, u32[]{:S(2)}, u32[]{:S(2)}) %collective-permute-start.3) | collective-permute-done | bytes 98336 | tf_op jit(solution)/shard_map/ppermute | solution.py:68
  14.8 8.7 %collective-permute-start.10 = (bf16[64,1280]{1,0:T(8,128)(2,1)S(1)}, bf16[64,1280]{1,0:T(8,128)(2,1)S(1)}, u32[]{:S(2)}, u32[]{:S(2)}) collective-permute-start(bf16[64,1280]{1,0:T(8,128)(2,1)S(1)} %constant_dynamic-update-slice_fusion.4), channel_id=1, source_target_pairs={{0,8},{2,10},{4,12},{6,14},{8,16},{10,18},{12,20},{14,22},{16,24},... | collective-permute-start | bytes 491528 | tf_op jit(solution)/shard_map/ppermute | solution.py:68
  25.5 2.4 %collective-permute-start.8 = (bf16[256,768]{1,0:T(8,128)(2,1)}, bf16[256,768]{1,0:T(8,128)(2,1)S(1)}, u32[]{:S(2)}, u32[]{:S(2)}) collective-permute-start(bf16[256,768]{1,0:T(8,128)(2,1)} %constant_dynamic-update-slice_fusion.w0), channel_id=1, source_target_pairs={{0,6},{2,4},{4,2},{6,0},{8,14},{10,12},{12,10},{14,8},{16,22},{18,... | collective-permute-start | bytes 1179656 | tf_op jit(solution)/shard_map/ppermute | solution.py:73
  29.4 2.5 %collective-permute-start.15 = (bf16[256,1280]{1,0:T(8,128)(2,1)S(1)}, bf16[256,1280]{1,0:T(8,128)(2,1)S(1)}, u32[]{:S(2)}, u32[]{:S(2)}) collective-permute-start(bf16[256,1280]{1,0:T(8,128)(2,1)S(1)} %pad_maximum_fusion.w0), channel_id=1, source_target_pairs={{0,6},{2,4},{4,2},{6,0},{8,14},{10,12},{12,10},{14,8},{16,22},{18,... | collective-permute-start | bytes 1966088 | tf_op jit(solution)/shard_map/ppermute | solution.py:73
  32.4 6.3 %collective-permute-done.8.w3 = bf16[256,768]{1,0:T(8,128)(2,1)S(1)} collective-permute-done((bf16[256,768]{1,0:T(8,128)(2,1)}, bf16[256,768]{1,0:T(8,128)(2,1)S(1)}, u32[]{:S(2)}, u32[]{:S(2)}) %collective-permute-start.8) | collective-permute-done | bytes 393248 | tf_op jit(solution)/shard_map/ppermute | solution.py:73
  39.4 1.5 %collective-permute-start.13 = (bf16[256,1280]{1,0:T(8,128)(2,1)S(1)}, bf16[256,1280]{1,0:T(8,128)(2,1)S(1)}, u32[]{:S(2)}, u32[]{:S(2)}) collective-permute-start(bf16[256,1280]{1,0:T(8,128)(2,1)S(1)} %pad_maximum_fusion.w0), channel_id=1, source_target_pairs={{0,2},{2,0},{4,6},{6,4},{8,10},{10,8},{12,14},{14,12},{16,18},{18,... | collective-permute-start | bytes 1966088 | tf_op jit(solution)/shard_map/ppermute | solution.py:73
  41.8 5.5 %collective-permute-done.7.w2 = bf16[256,768]{1,0:T(8,128)(2,1)} collective-permute-done((bf16[256,768]{1,0:T(8,128)(2,1)}, bf16[256,768]{1,0:T(8,128)(2,1)}, u32[]{:S(2)}, u32[]{:S(2)}) %collective-permute-start.7) | collective-permute-done | bytes 393248 | tf_op jit(solution)/shard_map/ppermute | solution.py:73
  47.3 1.9 %collective-permute-start.1 = (bf16[256,1024]{1,0:T(8,128)(2,1)S(1)}, bf16[256,1024]{1,0:T(8,128)(2,1)}, u32[]{:S(2)}, u32[]{:S(2)}) collective-permute-start(bf16[256,1024]{1,0:T(8,128)(2,1)S(1)} %column_normed.1.own), channel_id=1, source_target_pairs={{0,16},{2,18},{4,20},{6,22},{8,24},{10,26},{12,28},{14,30},{16,0},... | collective-permute-start | bytes 1572872 | tf_op jit(solution)/shard_map/ppermute | solution.py:282
  50.8 22.3 %collective-permute-done.1.far_own = bf16[256,1024]{1,0:T(8,128)(2,1)} collective-permute-done((bf16[256,1024]{1,0:T(8,128)(2,1)S(1)}, bf16[256,1024]{1,0:T(8,128)(2,1)}, u32[]{:S(2)}, u32[]{:S(2)}) %collective-permute-start.1) | collective-permute-done | bytes 524320 | tf_op jit(solution)/shard_map/ppermute | solution.py:282
  75.4 1.0 copy-done.9
  76.4 1.0 copy-done.11
  79.4 4.4 %column_attention.1 = (bf16[256,256]{1,0:T(8,128)(2,1)S(1)}, bf16[256,256]{1,0:T(8,128)(2,1)S(1)}) custom-call(s32[2]{0:T(128)S(1)} %pad_add_fusion.place, f32[4]{0:T(128)S(1)} %dynamic_slice.7.slopes, bf16[256,1024]{1,0:T(8,128)(2,1)S(1)} %copy-done.9, bf16[256,1024]{1,0:T(8,128)(2,1)S(1)} %copy-done.11, bf16[256,1024]{1,0:T(8,128)(2,1)} %collective-permute-done.1.far_own, ...), custom_call_target="tpu_custom_call" | custom-call | flops 1000000000 | bytes 4194304 | tf_op jit(solution)/shard_map/column_attention/pallas_call | solution.py:298
  84.2 1.0 collective-permute-done.9.theirs
  85.3 2.1 %middle.1 = (f32[256,1024]{1,0:T(8,128)S(1)}, bf16[256,1024]{1,0:T(8,128)(2,1)S(1)}) custom-call(s32[2]{0:T(128)S(1)} %pad_add_fusion.place, bf16[256,1024]{1,0:T(8,128)(2,1)S(1)} %copy-done.2, s32[64,4]{1,0:T(8,128)S(1)} %copy.19.mask_ref.mask, f32[1,1024]{1,0:T(1,128)S(1)} %bitcast.15, f32[1,1024]{1,0:T(1,128)S(1)} %bitcast.16, ...), custom_call_target="tpu_custom_call" | custom-call | flops 1000000000 | bytes 4194304 | tf_op jit(solution)/shard_map/middle/pallas_call | solution.py:311
  89.1 4.7 %all-to-all-start = ((bf16[16,16,1024]{2,1,0:T(8,128)(2,1)}), bf16[16,16,1024]{2,1,0:T(8,128)(2,1)}, u32[]{:S(2)}, u32[]{:S(2)}) async-start(bf16[16,16,1024]{2,1,0:T(8,128)(2,1)} %bitcast.13), calls=%async_computation | async-start | bytes 1048576 | tf_op jit(solution)/shard_map/all_to_all | solution.py:319
  94.0 15.3 %all-to-all-done = bf16[16,16,1024]{2,1,0:T(8,128)(2,1)} async-done(((bf16[16,16,1024]{2,1,0:T(8,128)(2,1)}), bf16[16,16,1024]{2,1,0:T(8,128)(2,1)}, u32[]{:S(2)}, u32[]{:S(2)}) %all-to-all-start) | async-done | bytes 524320 | tf_op jit(solution)/shard_map/all_to_all | solution.py:319
  109.4 3.9 %row_attention.1 = bf16[256,512]{1,0:T(8,128)(2,1)S(1)} custom-call(s32[2]{0:T(128)S(1)} %pad_add_fusion.place, f32[8]{0:T(128)S(1)} %dynamic_slice.8.slopes, bf16[256,1024]{1,0:T(8,128)(2,1)} %bitcast.8.tokens, bf16[256,1280]{1,0:T(8,128)(2,1)S(1)} %pad_maximum_fusion.w0, bf16[256,1280]{1,0:T(8,128)(2,1)S(1)} %collective-permute-done.13.w1, ...), custom_call_target="tpu_custom_call" | custom-call | flops 1000000000 | bytes 4194304 | tf_op jit(solution)/shard_map/row_attention/pallas_call | solution.py:320
  113.3 13.0 %all_to_all.22 = bf16[16,16,512]{2,1,0:T(8,128)(2,1)S(1)} all-to-all(bf16[16,16,512]{2,1,0:T(8,128)(2,1)S(1)} %bitcast.12), channel_id=1, replica_groups=mesh['ens'=1,'lon'=16,'lat'=2] {'lon'}, dimensions={0} | all-to-all | bytes 524288 | tf_op jit(solution)/shard_map/all_to_all | solution.py:327
  126.3 1.6 %block_output.1 = bf16[256,1024]{1,0:T(8,128)(2,1)S(1)} custom-call(s32[2]{0:T(128)S(1)} %pad_add_fusion.place, f32[256,1024]{1,0:T(8,128)S(1)} %copy-done.4, bf16[256,512]{1,0:T(8,128)(2,1)S(1)} %bitcast.11, bf16[256,1280]{1,0:T(8,128)(2,1)S(1)} %pad_maximum_fusion.w0, bf16[256,1280]{1,0:T(8,128)(2,1)S(1)} %collective-permute-done.13.w1, ...), custom_call_target="tpu_custom_call" | custom-call | flops 1000000000 | bytes 4194304 | tf_op jit(solution)/shard_map/block_output/pallas_call | solution.py:328
  128.7 2.0 %reshape.39 = bf16[64,4,1024]{2,1,0:T(4,128)(2,1)} reshape(bf16[256,1024]{1,0:T(8,128)(2,1)} %copy-done) | data formatting | bytes 1048576 | tf_op jit(solution)/shard_map/reshape | solution.py:335
  (93 shorter events, 16.7 us)
Async XLA Ops:
  1.4 27.0 %copy-start.21 = (s32[64,4]{0,1:T(4,128)S(1)}, s32[64,4]{0,1:T(4,128)}, u32[]{:S(2)}) copy-start(s32[64,4]{0,1:T(4,128)} %param.12) | copy-start | bytes 3076
  1.4 27.1 %copy-start.17 = (bf16[64,4,1024]{2,1,0:T(4,128)(2,1)S(1)}, bf16[64,4,1024]{2,1,0:T(4,128)(2,1)}, u32[]{:S(2)}) copy-start(bf16[64,4,1024]{2,1,0:T(4,128)(2,1)} %param.11) | copy-start | bytes 1572868
  1.4 23.4 %collective-permute-start.5 = (bf16[64,768]{1,0:T(8,128)(2,1)S(1)}, bf16[64,768]{1,0:T(8,128)(2,1)S(1)}, u32[]{:S(2)}, u32[]{:S(2)}) collective-permute-start(bf16[64,768]{1,0:T(8,128)(2,1)S(1)} %reshape.36), channel_id=1, source_target_pairs={{0,24},{2,26},{4,28},{6,30},{8,0},{10,2},{12,4},{14,6},{16,8},{18,... | collective-permute-start | bytes 294920 | tf_op jit(solution)/shard_map/ppermute | solution.py:68
  6.6 17.7 %collective-permute-start.4 = (bf16[64,768]{1,0:T(8,128)(2,1)S(1)}, bf16[64,768]{1,0:T(8,128)(2,1)S(1)}, u32[]{:S(2)}, u32[]{:S(2)}) collective-permute-start(bf16[64,768]{1,0:T(8,128)(2,1)S(1)} %reshape.36), channel_id=1, source_target_pairs={{0,16},{2,18},{4,20},{6,22},{8,24},{10,26},{12,28},{14,30},{16,0},... | collective-permute-start | bytes 294920 | tf_op jit(solution)/shard_map/ppermute | solution.py:68
  6.6 8.3 %collective-permute-start.3 = (bf16[64,768]{1,0:T(8,128)(2,1)S(1)}, bf16[64,768]{1,0:T(8,128)(2,1)S(1)}, u32[]{:S(2)}, u32[]{:S(2)}) collective-permute-start(bf16[64,768]{1,0:T(8,128)(2,1)S(1)} %reshape.36), channel_id=1, source_target_pairs={{0,8},{2,10},{4,12},{6,14},{8,16},{10,18},{12,20},{14,22},{16,24},... | collective-permute-start | bytes 294920 | tf_op jit(solution)/shard_map/ppermute | solution.py:68
  8.1 20.6 %collective-permute-start.12 = (bf16[64,1280]{1,0:T(8,128)(2,1)S(1)}, bf16[64,1280]{1,0:T(8,128)(2,1)S(1)}, u32[]{:S(2)}, u32[]{:S(2)}) collective-permute-start(bf16[64,1280]{1,0:T(8,128)(2,1)S(1)} %constant_dynamic-update-slice_fusion.4), channel_id=1, source_target_pairs={{0,24},{2,26},{4,28},{6,30},{8,0},{10,2},{12,4},{14,6},{16,8},{18,... | collective-permute-start | bytes 491528 | tf_op jit(solution)/shard_map/ppermute | solution.py:68
  10.9 18.4 %collective-permute-start.11 = (bf16[64,1280]{1,0:T(8,128)(2,1)S(1)}, bf16[64,1280]{1,0:T(8,128)(2,1)S(1)}, u32[]{:S(2)}, u32[]{:S(2)}) collective-permute-start(bf16[64,1280]{1,0:T(8,128)(2,1)S(1)} %constant_dynamic-update-slice_fusion.4), channel_id=1, source_target_pairs={{0,16},{2,18},{4,20},{6,22},{8,24},{10,26},{12,28},{14,30},{16,0},... | collective-permute-start | bytes 491528 | tf_op jit(solution)/shard_map/ppermute | solution.py:68
  14.8 14.5 %collective-permute-start.10 = (bf16[64,1280]{1,0:T(8,128)(2,1)S(1)}, bf16[64,1280]{1,0:T(8,128)(2,1)S(1)}, u32[]{:S(2)}, u32[]{:S(2)}) collective-permute-start(bf16[64,1280]{1,0:T(8,128)(2,1)S(1)} %constant_dynamic-update-slice_fusion.4), channel_id=1, source_target_pairs={{0,8},{2,10},{4,12},{6,14},{8,16},{10,18},{12,20},{14,22},{16,24},... | collective-permute-start | bytes 491528 | tf_op jit(solution)/shard_map/ppermute | solution.py:68
  25.5 13.2 %collective-permute-start.8 = (bf16[256,768]{1,0:T(8,128)(2,1)}, bf16[256,768]{1,0:T(8,128)(2,1)S(1)}, u32[]{:S(2)}, u32[]{:S(2)}) collective-permute-start(bf16[256,768]{1,0:T(8,128)(2,1)} %constant_dynamic-update-slice_fusion.w0), channel_id=1, source_target_pairs={{0,6},{2,4},{4,2},{6,0},{8,14},{10,12},{12,10},{14,8},{16,22},{18,... | collective-permute-start | bytes 1179656 | tf_op jit(solution)/shard_map/ppermute | solution.py:73
  27.9 19.3 %collective-permute-start.7 = (bf16[256,768]{1,0:T(8,128)(2,1)}, bf16[256,768]{1,0:T(8,128)(2,1)}, u32[]{:S(2)}, u32[]{:S(2)}) collective-permute-start(bf16[256,768]{1,0:T(8,128)(2,1)} %constant_dynamic-update-slice_fusion.w0), channel_id=1, source_target_pairs={{0,4},{2,6},{4,0},{6,2},{8,12},{10,14},{12,8},{14,10},{16,20},{18,... | collective-permute-start | bytes 1179656 | tf_op jit(solution)/shard_map/ppermute | solution.py:73
  28.7 20.5 %collective-permute-start.6 = (bf16[256,768]{1,0:T(8,128)(2,1)}, bf16[256,768]{1,0:T(8,128)(2,1)S(1)}, u32[]{:S(2)}, u32[]{:S(2)}) collective-permute-start(bf16[256,768]{1,0:T(8,128)(2,1)} %constant_dynamic-update-slice_fusion.w0), channel_id=1, source_target_pairs={{0,2},{2,0},{4,6},{6,4},{8,10},{10,8},{12,14},{14,12},{16,18},{18,... | collective-permute-start | bytes 1179656 | tf_op jit(solution)/shard_map/ppermute | solution.py:73
  29.4 45.0 %collective-permute-start.15 = (bf16[256,1280]{1,0:T(8,128)(2,1)S(1)}, bf16[256,1280]{1,0:T(8,128)(2,1)S(1)}, u32[]{:S(2)}, u32[]{:S(2)}) collective-permute-start(bf16[256,1280]{1,0:T(8,128)(2,1)S(1)} %pad_maximum_fusion.w0), channel_id=1, source_target_pairs={{0,6},{2,4},{4,2},{6,0},{8,14},{10,12},{12,10},{14,8},{16,22},{18,... | collective-permute-start | bytes 1966088 | tf_op jit(solution)/shard_map/ppermute | solution.py:73
  31.9 42.5 %collective-permute-start.14 = (bf16[256,1280]{1,0:T(8,128)(2,1)S(1)}, bf16[256,1280]{1,0:T(8,128)(2,1)S(1)}, u32[]{:S(2)}, u32[]{:S(2)}) collective-permute-start(bf16[256,1280]{1,0:T(8,128)(2,1)S(1)} %pad_maximum_fusion.w0), channel_id=1, source_target_pairs={{0,4},{2,6},{4,0},{6,2},{8,12},{10,14},{12,8},{14,10},{16,20},{18,... | collective-permute-start | bytes 1966088 | tf_op jit(solution)/shard_map/ppermute | solution.py:73
  39.4 35.5 %collective-permute-start.13 = (bf16[256,1280]{1,0:T(8,128)(2,1)S(1)}, bf16[256,1280]{1,0:T(8,128)(2,1)S(1)}, u32[]{:S(2)}, u32[]{:S(2)}) collective-permute-start(bf16[256,1280]{1,0:T(8,128)(2,1)S(1)} %pad_maximum_fusion.w0), channel_id=1, source_target_pairs={{0,2},{2,0},{4,6},{6,4},{8,10},{10,8},{12,14},{14,12},{16,18},{18,... | collective-permute-start | bytes 1966088 | tf_op jit(solution)/shard_map/ppermute | solution.py:73
  40.9 34.1 %copy-start.22 = (f32[8]{0:T(128)S(1)}, f32[8]{0:T(128)}, u32[]{:S(2)}) copy-start(f32[8]{0:T(128)} %param.16) | copy-start | bytes 100
  47.3 25.8 %collective-permute-start.1 = (bf16[256,1024]{1,0:T(8,128)(2,1)S(1)}, bf16[256,1024]{1,0:T(8,128)(2,1)}, u32[]{:S(2)}, u32[]{:S(2)}) collective-permute-start(bf16[256,1024]{1,0:T(8,128)(2,1)S(1)} %column_normed.1.own), channel_id=1, source_target_pairs={{0,16},{2,18},{4,20},{6,22},{8,24},{10,26},{12,28},{14,30},{16,0},... | collective-permute-start | bytes 1572872 | tf_op jit(solution)/shard_map/ppermute | solution.py:282
  50.0 23.1 %collective-permute-start = (bf16[256,1024]{1,0:T(8,128)(2,1)S(1)}, bf16[256,1024]{1,0:T(8,128)(2,1)S(1)}, u32[]{:S(2)}, u32[]{:S(2)}) collective-permute-start(bf16[256,1024]{1,0:T(8,128)(2,1)S(1)} %column_normed.1.own), channel_id=1, source_target_pairs={{0,1},{1,0},{2,3},{3,2},{4,5},{5,4},{6,7},{7,6},{8,9},{9,8},{10,11... | collective-permute-start | bytes 1572872 | tf_op jit(solution)/shard_map/ppermute | solution.py:22
  73.1 2.3 %collective-permute-start.2 = (bf16[256,1024]{1,0:T(8,128)(2,1)}, bf16[256,1024]{1,0:T(8,128)(2,1)}, u32[]{:S(2)}, u32[]{:S(2)}) collective-permute-start(bf16[256,1024]{1,0:T(8,128)(2,1)} %collective-permute-done.1.far_own), channel_id=1, source_target_pairs={{0,1},{1,0},{2,3},{3,2},{4,5},{5,4},{6,7},{7,6},{8,9},{9,8},{10,11... | collective-permute-start | bytes 1572872 | tf_op jit(solution)/shard_map/ppermute | solution.py:22
  73.9 10.3 %collective-permute-start.16 = (bf16[256,1280]{1,0:T(8,128)(2,1)S(1)}, bf16[256,1280]{1,0:T(8,128)(2,1)S(1)}, u32[]{:S(2)}, u32[]{:S(2)}) collective-permute-start(bf16[256,1280]{1,0:T(8,128)(2,1)S(1)} %pad_maximum_fusion.w0), channel_id=1, source_target_pairs={{0,1},{1,0},{2,3},{3,2},{4,5},{5,4},{6,7},{7,6},{8,9},{9,8},{10,11... | collective-permute-start | bytes 1966088 | tf_op jit(solution)/shard_map/ppermute | solution.py:22
  74.4 10.8 %collective-permute-start.19 = (bf16[256,1280]{1,0:T(8,128)(2,1)S(1)}, bf16[256,1280]{1,0:T(8,128)(2,1)}, u32[]{:S(2)}, u32[]{:S(2)}) collective-permute-start(bf16[256,1280]{1,0:T(8,128)(2,1)S(1)} %collective-permute-done.15.w3), channel_id=1, source_target_pairs={{0,1},{1,0},{2,3},{3,2},{4,5},{5,4},{6,7},{7,6},{8,9},{9,8},{10,11... | collective-permute-start | bytes 1966088 | tf_op jit(solution)/shard_map/ppermute | solution.py:22
  74.4 10.8 %collective-permute-start.18 = (bf16[256,1280]{1,0:T(8,128)(2,1)S(1)}, bf16[256,1280]{1,0:T(8,128)(2,1)}, u32[]{:S(2)}, u32[]{:S(2)}) collective-permute-start(bf16[256,1280]{1,0:T(8,128)(2,1)S(1)} %collective-permute-done.14.w2), channel_id=1, source_target_pairs={{0,1},{1,0},{2,3},{3,2},{4,5},{5,4},{6,7},{7,6},{8,9},{9,8},{10,11... | collective-permute-start | bytes 1966088 | tf_op jit(solution)/shard_map/ppermute | solution.py:22
  74.9 10.3 %collective-permute-start.17 = (bf16[256,1280]{1,0:T(8,128)(2,1)S(1)}, bf16[256,1280]{1,0:T(8,128)(2,1)}, u32[]{:S(2)}, u32[]{:S(2)}) collective-permute-start(bf16[256,1280]{1,0:T(8,128)(2,1)S(1)} %collective-permute-done.13.w1), channel_id=1, source_target_pairs={{0,1},{1,0},{2,3},{3,2},{4,5},{5,4},{6,7},{7,6},{8,9},{9,8},{10,11... | collective-permute-start | bytes 1966088 | tf_op jit(solution)/shard_map/ppermute | solution.py:22
  83.8 1.4 %collective-permute-start.9 = (bf16[256,256]{1,0:T(8,128)(2,1)S(1)}, bf16[256,256]{1,0:T(8,128)(2,1)S(1)}, u32[]{:S(2)}, u32[]{:S(2)}) collective-permute-start(bf16[256,256]{1,0:T(8,128)(2,1)S(1)} %get-tuple-element.10), channel_id=1, source_target_pairs={{0,1},{1,0},{2,3},{3,2},{4,5},{5,4},{6,7},{7,6},{8,9},{9,8},{10,11... | collective-permute-start | bytes 393224 | tf_op jit(solution)/shard_map/ppermute | solution.py:22
  89.1 20.2 %all-to-all-start = ((bf16[16,16,1024]{2,1,0:T(8,128)(2,1)}), bf16[16,16,1024]{2,1,0:T(8,128)(2,1)}, u32[]{:S(2)}, u32[]{:S(2)}) async-start(bf16[16,16,1024]{2,1,0:T(8,128)(2,1)} %bitcast.13), calls=%async_computation | async-start | bytes 1048576 | tf_op jit(solution)/shard_map/all_to_all | solution.py:319
  (21 other events, 110.7 us)

commit v2 on v0

--- a/solution.py
+++ b/solution.py
@@ -1,11 +1,482 @@
+import functools
 import math
 
 import jax
 import jax.numpy as jnp
 from jax import lax
+from jax.experimental import pallas as pl
+from jax.experimental.pallas import tpu as pltpu
 from jax.sharding import PartitionSpec as P
 
 HS = 64
+PAIR = 2 * HS
+PLANE = 4
+NEVER = -1e30
+EXTRA = 16
+
+
+def at(place, length):
+    return [(i, place(i)) for i in range(length)]
+
+
+def swap_bands(value):
+    return lax.ppermute(value, "lat", at(lambda i: 1 - i, 2))
+
+
+SCALARS = pl.BlockSpec(memory_space=pltpu.SMEM)
+
+
+def call(kernel, out, name, scalars, arrays, given=(), scratch=(), room=24, space=pltpu.VMEM):
+    return pl.pallas_call(
+        kernel,
+        out_shape=out,
+        in_specs=[SCALARS] * len(scalars)
+        + [pl.BlockSpec(memory_space=pltpu.VMEM)] * len(arrays)
+        + [pl.BlockSpec(memory_space=pltpu.HBM)] * len(given),
+        out_specs=jax.tree.map(lambda _: pl.BlockSpec(memory_space=space), out),
+        scratch_shapes=scratch,
+        compiler_params=pltpu.CompilerParams(vmem_limit_bytes=room * 2**20),
+        cost_estimate=pl.CostEstimate(flops=2**10, bytes_accessed=2**10, transcendentals=0),
+        name=name,
+    )(*scalars, *arrays, *given)
+
+
+def dot(a, b):
+    return jnp.dot(a, b, preferred_element_type=jnp.float32)
+
+
+def dot_t(a, b):
+    return lax.dot_general(a, b, (((1,), (1,)), ((), ())), preferred_element_type=jnp.float32)
+
+
+def iota(shape, axis):
+    return lax.broadcasted_iota(jnp.int32, shape, axis)
+
+
+def bring(pairs, sems):
+    copies = [pltpu.make_async_copy(ref, held, sems.at[i]) for i, (ref, held) in enumerate(pairs)]
+    for copy in copies:
+        copy.start()
+    return copies
+
+
+def wait(copies):
+    for copy in copies:
+        copy.wait()
+
+
+def along_lines(weight, length):
+    steps = range(PLANE, length, PLANE)
+    return jnp.concatenate(
+        [weight] + [lax.ppermute(weight, "lon", at(lambda i: i ^ k, length)) for k in steps], axis=0
+    )
+
+
+def doubled(weight, step, length):
+    got = lax.ppermute(weight, "lon", at(lambda i: i ^ step, length))
+    return jnp.concatenate([weight, got], axis=0)
+
+
+def across_plane(part, length):
+    return [part] + [lax.ppermute(part, "lon", at(lambda i: i ^ k, length)) for k in range(1, PLANE)]
+
+
+def pack_rows_kernel(project, output, out):
+    split = project.shape[1]
+    out[:, :split] = by_kind(project[...])
+    out[:, split:] = output[...]
+
+
+def by_kind(weight):
+    heads = weight.shape[1] // (3 * HS)
+    block = lambda kind, head: weight[:, (3 * head + kind) * HS : (3 * head + kind + 1) * HS]
+    return jnp.concatenate([block(kind, head) for kind in range(3) for head in range(heads)], axis=1)
+
+
+def places(shard, place, pieces):
+    line, spot = place[0] // PLANE, place[0] % PLANE
+    for j, piece in enumerate(pieces):
+        for k in range(piece.shape[0] // shard):
+            owner = lax.bitwise_xor(line, k) * PLANE + lax.bitwise_xor(spot, j)
+            there = pl.ds(pl.multiple_of(owner * shard, shard), shard)
+            yield piece, slice(k * shard, (k + 1) * shard), there
+
+
+def order_kernel(shard, sort, place, w0, w1, w2, w3, out):
+    for piece, here, there in places(shard, place, (w0, w1, w2, w3)):
+        out[there, :] = by_kind(piece[here, :]) if sort else piece[here, :]
+
+
+def bring_in_order(shard, place, pieces, lane, target, sems):
+    lanes = slice(lane, lane + target.shape[1])
+    return bring(
+        [
+            (piece.at[here, lanes], target.at[there, :])
+            for piece, here, there in places(shard, place, pieces)
+        ],
+        sems,
+    )
+
+
+def norm(values, gain):
+    center = values - jnp.mean(values, axis=-1, keepdims=True)
+    spread = jnp.mean(center * center, axis=-1, keepdims=True)
+    return center * lax.rsqrt(spread + 1e-05) * gain
+
+
+def land_start(tokens, mask, embed):
+    cols, rows = mask.shape
+    total = rows * cols
+    row_of = (iota((total, rows), 0) // cols == iota((total, rows), 1)).astype(jnp.bfloat16)
+    spread = dot_t(row_of, mask.astype(jnp.bfloat16))
+    own = iota((total, cols), 0) % cols == iota((total, cols), 1)
+    land = jnp.sum(jnp.where(own, spread, 0.0), axis=1, keepdims=True)
+    return tokens.astype(jnp.float32).reshape(total, tokens.shape[2]) + land * embed
+
+
+def packed_start(packed, embed):
+    total = packed.shape[0] - EXTRA
+    row = packed[total : total + 1, :total].astype(jnp.float32)
+    same = iota((total, total), 0) == iota((total, total), 1)
+    land = jnp.sum(jnp.where(same, row, 0.0), axis=1, keepdims=True)
+    return packed[:total, :].astype(jnp.float32) + land * embed
+
+
+def slots(cols, rows, side, inverse=False):
+    total = cols * rows
+    spot, grid = iota((total, total), int(inverse)), iota((total, total), int(not inverse))
+    column = lax.rem(spot // rows + side * (cols // 2), cols)
+    return (grid == lax.rem(spot, rows) * cols + column).astype(jnp.bfloat16)
+
+
+def pack_tokens_kernel(lons, place, tokens, mask, keep, send, *scratch):
+    *held, sems = scratch
+    wait(bring(zip((tokens, mask), held), sems))
+    tokens, mask = held
+    rows, cols, width = tokens.shape
+    half = rows * cols // 2
+    side = place[0] // (lons // 2)
+    flat = tokens[...].astype(jnp.float32).reshape(rows * cols, width).astype(jnp.bfloat16)
+    in_slots = dot(slots(cols, rows, side), flat).astype(jnp.bfloat16)
+    land = mask[...].astype(jnp.float32)
+    parts = [land[c : c + 1, :] for c in range(cols)]
+    halves = [jnp.concatenate(parts[: cols // 2], axis=1), jnp.concatenate(parts[cols // 2 :], axis=1)]
+    for k, out in enumerate((keep, send)):
+        out[:half, :] = in_slots[k * half : (k + 1) * half]
+        out[half:, :] = jnp.zeros((EXTRA, width), jnp.bfloat16)
+        row = jnp.where(side == k, halves[0], halves[1])
+        out[half:, :half] = jnp.broadcast_to(row, (EXTRA, half)).astype(jnp.bfloat16)
+
+
+def column_norm_kernel(own, other, far_own, far_other, embed, gain, out):
+    half = own.shape[0] - EXTRA
+    for k, ref in enumerate((own, other, far_own, far_other)):
+        normed = norm(packed_start(ref[...], embed[...]), gain[...])
+        out[k * half : (k + 1) * half, :] = normed.astype(jnp.bfloat16)
+
+
+def unit_heads(vectors, scale=1.0):
+    width = vectors.shape[1]
+    same = (iota((width, width), 0) // HS == iota((width, width), 1) // HS).astype(jnp.bfloat16)
+    total = dot((vectors * vectors).astype(jnp.bfloat16), same)
+    return (vectors * (lax.rsqrt(total * (1.0 / HS) + 1e-06) * scale)).astype(jnp.bfloat16)
+
+
+def two_heads(query, keyed, valued, bias):
+    rows = query.shape[0]
+    first = iota(query.shape, 1) < HS
+    zero = jnp.zeros_like(query)
+    stacked = jnp.concatenate([jnp.where(first, query, zero), jnp.where(first, zero, query)], axis=0)
+    weight = jnp.exp(dot_t(stacked, keyed) + bias).astype(jnp.bfloat16)
+    widened = jnp.concatenate([valued, jnp.ones_like(valued)], axis=1)
+    mixed = dot(weight, widened)
+    mixed = mixed[:, :PAIR] / mixed[:, PAIR:]
+    return jnp.where(first, mixed[:rows], mixed[rows:]).astype(jnp.bfloat16)
+
+
+def column_kernel(band, place, slopes, tokens, weight, out_own, out_other, qkv):
+    block = tokens.shape[0] // 4
+    loops = block // band
+    width = weight.shape[1] // 3
+    projected = dot(tokens[...], weight[...])
+    qkv[:, :width] = unit_heads(projected[:, :width], 1.0 / math.sqrt(HS))
+    qkv[:, width : 2 * width] = unit_heads(projected[:, width : 2 * width])
+    qkv[:, 2 * width :] = projected[:, 2 * width :].astype(jnp.bfloat16)
+    total = 2 * band
+    shape = (2 * total, 2 * total)
+    spot_q, spot_k = iota(shape, 0), iota(shape, 1)
+    shift = place[1] * band
+    row_q, row_k = lax.rem(spot_q + shift, total), lax.rem(spot_k + shift, total)
+    pair_sum = row_q + row_k
+    beyond = jnp.minimum(pair_sum + 1, 2 * total - 1 - pair_sum)
+    here = (spot_q < total) == (spot_k < total)
+    distance = jnp.where(here, jnp.abs(row_q - row_k), beyond).astype(jnp.float32)
+    first = place[1] * (width // HS)
+    for pair in range(width // PAIR):
+        bias = jnp.concatenate(
+            [distance * -slopes[first + 2 * pair + one] for one in range(2)], axis=0
+        )
+        lanes = slice(pair * PAIR, (pair + 1) * PAIR)
+        for loop in range(loops):
+            starts = [part * block + loop * band for part in range(4)]
+            query, keyed, valued = (
+                jnp.concatenate(
+                    [
+                        qkv[at : at + band, kind * width + lanes.start : kind * width + lanes.stop]
+                        for at in starts
+                    ],
+                    axis=0,
+                )
+                for kind in range(3)
+            )
+            mixed = two_heads(query, keyed, valued, bias)
+            for part in range(4):
+                out = (out_own, out_other)[part % 2]
+                slot = (part // 2) * loops + loop
+                out[slot * band : (slot + 1) * band, lanes] = mixed[part * band : (part + 1) * band]
+
+
+def middle_kernel(cols, mine, theirs, near, far, kept, got, embed, gain, out):
+    update = dot_t(mine[...], near[...]) + dot_t(theirs[...], far[...])
+    parts = [packed_start(ref[...], embed[...]) for ref in (kept, got)]
+    middle = jnp.concatenate(parts, axis=0) + update
+    normed = norm(middle, gain[...]).astype(jnp.bfloat16)
+    by_row = slots(cols, normed.shape[0] // cols, 0, True)
+    out[...] = dot(by_row, normed).astype(jnp.bfloat16)
+
+
+def home_kernel(lons, place, mine, theirs, back, near, far, tokens, mask, embed, out, *scratch):
+    *held, total, sems = scratch
+    coming = bring(zip((tokens, mask, embed), held), sems)
+    tokens, mask, embed = held
+    rows, cols, _ = tokens.shape
+    half, width = rows * cols // 2, near.shape[1]
+    to_grid = slots(cols, rows, place[0] // (lons // 2), True)
+    update = 0.0
+    for lane, (kept, weight) in enumerate(((mine, near), (theirs, far))):
+        mixed = dot(to_grid[:, :half], kept[:half, :])
+        mixed += dot(to_grid[:, half:], back[:, lane * width : (lane + 1) * width])
+        update += dot_t(mixed.astype(jnp.bfloat16), weight[...])
+    wait(coming)
+    total[...] = land_start(tokens[...], mask[...], embed[...]) + update
+    wait(bring([(total, out)], sems))
+
+
+def row_kernel(shard, cols, rows, place, slopes, tokens, *refs):
+    pieces, (out, weight, sems) = refs[:-3], refs[-3:]
+    coming = [
+        bring_in_order(
+            shard, place, pieces[half * PLANE : (half + 1) * PLANE], 0, weight.at[half], sems.at[half]
+        )
+        for half in range(2)
+    ]
+    total = tokens.shape[0]
+    block = cols * rows
+    lon_count = total // block
+    circle = lon_count * cols
+    turn, part = lon_count // 2, cols // 2
+    spot_q, spot_k = iota((total, total), 0), iota((total, total), 1)
+
+    def lon_of(spot):
+        device, slot = spot // block, lax.rem(spot, cols)
+        side = device // turn
+        holder = lax.rem(device + (slot // part) * turn, lon_count)
+        return holder * cols + side * part + lax.rem(slot, part)
+
+    row_of = lambda spot: lax.rem(spot, block) // cols
+    gap = jnp.abs(lon_of(spot_q) - lon_of(spot_k))
+    distance = jnp.minimum(gap, circle - gap).astype(jnp.float32)
+    column = lax.rem(spot_q, cols)
+    away = (column // part != spot_q // block // turn).astype(jnp.int32)
+    home = lax.rem(spot_q // block + away * turn, lon_count) * block
+    home = home + row_of(spot_q) * cols + away * part + lax.rem(column, part)
+    homeward = (spot_k == home).astype(jnp.bfloat16)
+    same = row_of(spot_q) == row_of(spot_k)
+    width = weight.shape[2] // 3
+    heads = width // HS
+    for half in range(2):
+        first = lax.rem(place[1] + half, 2) * heads
+        wait(coming[half])
+        projected = dot(tokens[...], weight[half])
+        query = unit_heads(projected[:, :width], 1.0 / math.sqrt(HS))
+        keyed = unit_heads(projected[:, width : 2 * width])
+        valued = projected[:, 2 * width :].astype(jnp.bfloat16)
+        for pair in range(width // PAIR):
+            lanes = slice(pair * PAIR, (pair + 1) * PAIR)
+            bias = jnp.concatenate(
+                [
+                    jnp.where(same, distance * -slopes[first + 2 * pair + one], NEVER)
+                    for one in range(2)
+                ],
+                axis=0,
+            )
+            mixed = two_heads(query[:, lanes], keyed[:, lanes], valued[:, lanes], bias)
+            start = half * width + pair * PAIR
+            out[:, start : start + PAIR] = dot(homeward, mixed).astype(jnp.bfloat16)
+
+
+def final_kernel(shard, place, mixed, *refs):
+    pieces, middle, out, weight, total, sems, total_sems = refs[:-6], *refs[-6:]
+    width = weight.shape[2]
+    lane = pieces[0].shape[1] - width
+    coming = [
+        bring_in_order(
+            shard, place, pieces[half * PLANE : (half + 1) * PLANE], lane, weight.at[half], sems.at[half]
+        )
+        for half in range(2)
+    ]
+    rows = total.shape[0] // 4
+    cut = [slice(i * rows, (i + 1) * rows) for i in range(4)]
+    last = bring([(middle.at[here, :], total.at[here, :]) for here in cut], total_sems)
+    update = 0.0
+    for half in range(2):
+        wait(coming[half])
+        update += dot_t(mixed[:, half * width : (half + 1) * width], weight[half])
+    wait(last)
+    out[...] = (total[...] + update).reshape(out.shape).astype(jnp.bfloat16)
+
+
+def fast(
+    fields,
+    land_mask,
+    land_embed,
+    column_gain,
+    row_gain,
+    column_slopes,
+    row_slopes,
+    column_project,
+    column_output,
+    row_project,
+    row_output,
+):
+    lon_count = lax.axis_size("lon")
+    lat = lax.axis_index("lat")
+    lon = lax.axis_index("lon")
+    band, cols, width = fields.shape
+    tokens = band * cols
+    heads = column_slopes.shape[0]
+    half = heads // 2
+    attend = half * HS
+    shard = column_project.shape[0]
+    place = jnp.stack([lon, lat]).astype(jnp.int32)
+    embed, column_gain, row_gain = (v.reshape(1, width) for v in (land_embed, column_gain, row_gain))
+    bf16 = lambda *shape: jax.ShapeDtypeStruct(shape, jnp.bfloat16)
+    f32 = lambda *shape: jax.ShapeDtypeStruct(shape, jnp.float32)
+    rows = shard * lon_count
+    weights = (bf16(rows, 3 * attend), bf16(rows, attend))
+
+    order = lambda pieces, name, sort, out: call(
+        functools.partial(order_kernel, shard, sort), out, name, (place,), pieces
+    )
+    project_shape, output_shape = weights
+    antipode = lambda value: lax.ppermute(
+        value, "lon", at(lambda i: (i + lon_count // 2) % lon_count, lon_count)
+    )
+    packed = bf16(tokens // 2 + EXTRA, width)
+    mask = land_mask.T
+    held = [pltpu.VMEM(fields.shape, fields.dtype), pltpu.VMEM(mask.shape, mask.dtype)]
+
+    first = along_lines(column_project, lon_count)
+    keep, send = call(
+        functools.partial(pack_tokens_kernel, lon_count),
+        (packed, packed),
+        "loop_tokens",
+        (place,),
+        (),
+        (fields, mask),
+        held + [pltpu.SemaphoreType.DMA((2,))],
+        room=60,
+    )
+    second = column_output
+    third = bf16(shard, row_project.shape[1] + row_output.shape[1])
+    third = call(pack_rows_kernel, third, "row_shards", (), (row_project, row_output))
+    if lon_count > PLANE:
+        second = doubled(second, PLANE, lon_count)
+        third = doubled(third, PLANE, lon_count)
+    keep_other = swap_bands(keep)
+    first, second, third, send = lax.optimization_barrier((first, second, third, send))
+    far = antipode(send)
+    pieces = across_plane(first, lon_count)
+    if lon_count > 2 * PLANE:
+        second = doubled(second, 2 * PLANE, lon_count)
+    far_other = swap_bands(far)
+    normed = call(
+        column_norm_kernel,
+        bf16(2 * tokens, width),
+        "column_normed",
+        (),
+        (keep, keep_other, far, far_other, embed, column_gain),
+    )
+    normed, pieces, second = lax.optimization_barrier((normed, pieces, second))
+    third, _ = lax.optimization_barrier((third, far))
+    project = order(pieces, "column_project", True, project_shape)
+    second = across_plane(second, lon_count)
+    if lon_count > 2 * PLANE:
+        third = doubled(third, 2 * PLANE, lon_count)
+
+    mixed_own, mixed_other = call(
+        functools.partial(column_kernel, band),
+        (bf16(tokens, attend), bf16(tokens, attend)),
+        "column_attention",
+        (place, column_slopes),
+        (normed, project),
+        (),
+        [pltpu.VMEM((2 * tokens, 3 * attend), jnp.bfloat16)],
+    )
+    theirs = swap_bands(mixed_other)
+    second, third, mixed_own = lax.optimization_barrier((second, third, mixed_own))
+    output = order(second, "column_output", False, output_shape)
+    output_far = swap_bands(output)
+    third = across_plane(third, lon_count)
+    back = antipode(jnp.concatenate([mixed_own[tokens // 2 :], theirs[tokens // 2 :]], axis=1))
+    row_normed = call(
+        functools.partial(middle_kernel, cols),
+        bf16(tokens, width),
+        "row_normed",
+        (),
+        (mixed_own, theirs, output, output_far, keep, far, embed, row_gain),
+    )
+    spread = lax.all_to_all(row_normed, "lon", split_axis=0, concat_axis=0, tiled=True)
+    third, back = lax.optimization_barrier((third, back))
+    third_far = [swap_bands(piece) for piece in third]
+    middle = call(
+        functools.partial(home_kernel, lon_count),
+        f32(tokens, width),
+        "middle",
+        (place,),
+        (mixed_own, theirs, back, output, output_far),
+        (fields, mask, embed),
+        held + [pltpu.VMEM(embed.shape, embed.dtype), pltpu.VMEM((tokens, width), jnp.float32)]
+        + [pltpu.SemaphoreType.DMA((3,))],
+        space=pltpu.HBM,
+    )
+    sems = pltpu.SemaphoreType.DMA((2, lon_count))
+    row_mixed = call(
+        functools.partial(row_kernel, shard, cols, band // lon_count),
+        bf16(tokens, 2 * attend),
+        "row_attention",
+        (place, row_slopes),
+        (spread,),
+        (*third, *third_far),
+        [pltpu.VMEM((2, *project_shape.shape), jnp.bfloat16), sems],
+        room=60,
+    )
+    back = lax.all_to_all(row_mixed, "lon", split_axis=0, concat_axis=0, tiled=True)
+    return call(
+        functools.partial(final_kernel, shard),
+        bf16(band, cols, width),
+        "block_output",
+        (place,),
+        (back,),
+        (*third, *third_far, middle),
+        [
+            pltpu.VMEM((2, *output_shape.shape), jnp.bfloat16),
+            pltpu.VMEM((tokens, width), jnp.float32),
+            sems,
+            pltpu.SemaphoreType.DMA((4,)),
+        ],
+        room=60,
+    )
 
 
 def passed_along(value, axis, by):
@@ -74,7 +545,7 @@
     return mixed.astype(jnp.bfloat16).reshape(query.shape[0], query.shape[1], -1)
 
 
-def shards(
+def general(
     fields,
     land_mask,
     land_embed,
@@ -153,4 +624,10 @@
         P("lon", "lat"),
     )
     out_specs = P(("ens", "lat"), "lon", None)
+
+    def shards(fields, *rest):
+        length = lax.axis_size("lon")
+        suits = fields.shape[0] % length == 0 and length in (2 * PLANE, 4 * PLANE)
+        return (fast if suits else general)(fields, *rest)
+
     return jax.shard_map(shards, mesh=mesh, in_specs=in_specs, out_specs=out_specs, check_vma=False)

time: 327 us -> 119 us (0.36)
  waiting for transfers between devices: 163 us -> 53.3 us
  blocking collectives: 95.4 us -> 0 us
  Pallas kernels: 0 us -> 22.4 us
  starting transfers between devices: 14.8 us -> 35.4 us
  between operations: 13.8 us -> 0.36 us
  matrix products: 12.6 us -> 0 us
  local copies, waits for them, and re-layouts: 15 us -> 4.25 us
  other arithmetic: 12.2 us -> 2.38 us
    all_gather x4 -> x0, waiting for transfers between devices: 130 us -> none  [the longest x2 115 us: project_in(): lax.all_gather(weight, 'lon', axis=0, tiled=True)]
    all_gather x2 -> x0, blocking collectives: 95.4 us -> none  [project_out(): lax.all_gather(weight, 'lon', axis=0, tiled=True)]
    ppermute x1 -> x26, waiting for transfers between devices: 0.01 us -> 45.9 us  [the longest x2 16.5 us: fast(): lax.ppermute(value, 'lon', at(lambda i: (i + lon_count // 2) % lon_count,...]
    ppermute x1 -> x26, starting transfers between devices: 2.72 us -> 26.9 us  [the longest x9 11.7 us: across_plane(): lax.ppermute(part, 'lon', at(lambda i: i ^ k, length))]
    pallas_call x0 -> x10, Pallas kernels: none -> 22.4 us  [call(): pl.pallas_call(kernel, out_shape=out, in_specs=[SCALARS] * len(scalars) +...]
    dot_general x8 -> x0, matrix products: 12.6 us -> none  [the longest x2 4.97 us: project_in(): jnp.dot(normed, lax.all_gather(weight, 'lon', axis=0, tiled=True), prefer...]
    all_to_all x2, waiting for transfers between devices: 19.9 us -> 7.36 us  [the longest x1 7.36 us: fast(): lax.all_to_all(row_mixed, 'lon', split_axis=0, concat_axis=0, tiled=True)]
    reduce_scatter x2 -> x0, waiting for transfers between devices: 11.9 us -> none  [sum_heads(): lax.psum_scatter(partial_value.astype(jnp.bfloat16), 'lat', scatter_dimen...]
  transfers between devices with their start and end apart: 9 -> 28, of which waited for: 7 -> 13; matrix products, arithmetic and copies ran while one was open for 4% -> 2% of each run, Pallas kernels for 0% -> 9%
where the time goes in v2:
time: 119 us; the launch traced here: 118 us
  waiting for transfers between devices  53.3 us (45%)
  starting transfers between devices  35.4 us (30%)
  Pallas kernels  22.4 us (19%)
  local copies, waits for them, and re-layouts  4.25 us (4%)
  other arithmetic  2.38 us (2%)
    pallas_call x10, Pallas kernels, call(): pl.pallas_call(kernel, out_shape=out, in_specs=[SCALARS] * len(scalars) +...  22.4 us
    ppermute x2, waiting for transfers between devices, fast(): lax.ppermute(value, 'lon', at(lambda i: (i + lon_count // 2) % lon_count,...  16.5 us
    ppermute x4, waiting for transfers between devices, doubled(): got = lax.ppermute(weight, 'lon', at(lambda i: i ^ step, length))  16.2 us
    ppermute x9, starting transfers between devices, across_plane(): lax.ppermute(part, 'lon', at(lambda i: i ^ k, length))  11.7 us
    ppermute x9, waiting for transfers between devices, across_plane(): lax.ppermute(part, 'lon', at(lambda i: i ^ k, length))  8.65 us
    all_to_all x1, waiting for transfers between devices, fast(): lax.all_to_all(row_mixed, 'lon', split_axis=0, concat_axis=0, tiled=True)  7.36 us
    ppermute x3, starting transfers between devices, along_lines(): lax.ppermute(weight, 'lon', at(lambda i: i ^ k, length))  5.62 us
    ppermute x2, starting transfers between devices, fast(): lax.ppermute(value, 'lon', at(lambda i: (i + lon_count // 2) % lon_count,...  4.9 us
  transfers between devices with their start and end apart: 28, of which 13 were waited for; matrix products, arithmetic and copies ran while one was open for 2% of the time, Pallas kernels for 9%

profile of v2, /device:TPU:0, one launch (start us, length us, event | category | flops | bytes accessed | tf_op | source)
XLA Modules:
  0.0 118.1 jit_solution(14854854868000175375)
XLA Ops:
  0.0 4.0 %collective-permute-start.2 = (bf16[64,768]{1,0:T(8,128)(2,1)}, bf16[64,768]{1,0:T(8,128)(2,1)S(1)}, u32[]{:S(2)}, u32[]{:S(2)}) collective-permute-start(bf16[64,768]{1,0:T(8,128)(2,1)} %param.18), channel_id=1, source_target_pairs={{0,16},{2,18},{4,20},{6,22},{8,24},{10,26},{12,28},{14,30},{16,0},... | collective-permute-start | bytes 294920 | tf_op jit(solution)/shard_map/ppermute | solution.py:71
  4.0 1.6 %collective-permute-start.1 = (bf16[64,768]{1,0:T(8,128)(2,1)}, bf16[64,768]{1,0:T(8,128)(2,1)S(1)}, u32[]{:S(2)}, u32[]{:S(2)}) collective-permute-start(bf16[64,768]{1,0:T(8,128)(2,1)} %param.18), channel_id=1, source_target_pairs={{0,8},{2,10},{4,12},{6,14},{8,0},{10,2},{12,4},{14,6},{16,24},{18,... | collective-permute-start | bytes 294920 | tf_op jit(solution)/shard_map/ppermute | solution.py:71
  10.0 2.9 %loop_tokens.1 = (bf16[144,1024]{1,0:T(8,128)(2,1)}, bf16[144,1024]{1,0:T(8,128)(2,1)}) custom-call(s32[2]{0:T(128)} %pad_add_fusion.place, bf16[64,4,1024]{2,1,0:T(4,128)(2,1)} %tokens.3, s32[4,64]{1,0:T(4,128)} %bitcast.13), custom_call_target="tpu_custom_call" | custom-call | flops 1024 | bytes 1024 | tf_op jit(solution)/shard_map/loop_tokens/pallas_call | solution.py:30
  15.1 2.1 %collective-permute-start.6 = (bf16[144,1024]{1,0:T(8,128)(2,1)}, bf16[144,1024]{1,0:T(8,128)(2,1)S(1)}, u32[]{:S(2)}, u32[]{:S(2)}) collective-permute-start(bf16[144,1024]{1,0:T(8,128)(2,1)} %get-tuple-element.33), channel_id=1, source_target_pairs={{0,16},{2,18},{4,20},{6,22},{8,24},{10,26},{12,28},{14,30},{16,0},... | collective-permute-start | bytes 884744 | tf_op jit(solution)/shard_map/ppermute | solution.py:372
  18.1 2.5 %collective-permute-start.10 = (bf16[256,768]{1,0:T(8,128)(2,1)S(1)}, bf16[256,768]{1,0:T(8,128)(2,1)S(1)}, u32[]{:S(2)}, u32[]{:S(2)}) collective-permute-start(bf16[256,768]{1,0:T(8,128)(2,1)S(1)} %pad_maximum_fusion.1.w0), channel_id=1, source_target_pairs={{0,6},{2,4},{4,2},{6,0},{8,14},{10,12},{12,10},{14,8},{16,22},{18,... | collective-permute-start | bytes 1179656 | tf_op jit(solution)/shard_map/ppermute | solution.py:81
  21.1 12.9 %collective-permute-done.11 = bf16[128,256]{1,0:T(8,128)(2,1)S(1)} collective-permute-done((bf16[128,256]{1,0:T(8,128)(2,1)S(1)}, bf16[128,256]{1,0:T(8,128)(2,1)S(1)}, u32[]{:S(2)}, u32[]{:S(2)}) %collective-permute-start.11) | collective-permute-done | bytes 65568 | tf_op jit(solution)/shard_map/ppermute | solution.py:76
  34.0 1.7 %collective-permute-start.8 = (bf16[256,768]{1,0:T(8,128)(2,1)S(1)}, bf16[256,768]{1,0:T(8,128)(2,1)S(1)}, u32[]{:S(2)}, u32[]{:S(2)}) collective-permute-start(bf16[256,768]{1,0:T(8,128)(2,1)S(1)} %pad_maximum_fusion.1.w0), channel_id=1, source_target_pairs={{0,2},{2,0},{4,6},{6,4},{8,10},{10,8},{12,14},{14,12},{16,18},{18,... | collective-permute-start | bytes 1179656 | tf_op jit(solution)/shard_map/ppermute | solution.py:81
  35.8 1.5 %collective-permute-done.7.far_other = bf16[144,1024]{1,0:T(8,128)(2,1)S(1)} collective-permute-done((bf16[144,1024]{1,0:T(8,128)(2,1)S(1)}, bf16[144,1024]{1,0:T(8,128)(2,1)S(1)}, u32[]{:S(2)}, u32[]{:S(2)}) %collective-permute-start.7) | collective-permute-done | bytes 294944 | tf_op jit(solution)/shard_map/ppermute | solution.py:23
  38.7 5.8 %collective-permute-done.8.w1 = bf16[256,768]{1,0:T(8,128)(2,1)S(1)} collective-permute-done((bf16[256,768]{1,0:T(8,128)(2,1)S(1)}, bf16[256,768]{1,0:T(8,128)(2,1)S(1)}, u32[]{:S(2)}, u32[]{:S(2)}) %collective-permute-start.8) | collective-permute-done | bytes 393248 | tf_op jit(solution)/shard_map/ppermute | solution.py:81
  44.5 2.7 %collective-permute-start.14 = (bf16[256,256]{1,0:T(8,128)(2,1)S(1)}, bf16[256,256]{1,0:T(8,128)(2,1)S(1)}, u32[]{:S(2)}, u32[]{:S(2)}) collective-permute-start(bf16[256,256]{1,0:T(8,128)(2,1)S(1)} %pad_maximum_fusion.3.w0), channel_id=1, source_target_pairs={{0,6},{2,4},{4,2},{6,0},{8,14},{10,12},{12,10},{14,8},{16,22},{18,... | collective-permute-start | bytes 393224 | tf_op jit(solution)/shard_map/ppermute | solution.py:81
  48.0 2.9 %collective-permute-done.15 = bf16[128,1024]{1,0:T(8,128)(2,1)S(1)} collective-permute-done((bf16[128,1024]{1,0:T(8,128)(2,1)S(1)}, bf16[128,1024]{1,0:T(8,128)(2,1)S(1)}, u32[]{:S(2)}, u32[]{:S(2)}) %collective-permute-start.15) | collective-permute-done | bytes 262176 | tf_op jit(solution)/shard_map/ppermute | solution.py:76
  51.9 2.5 %column_attention.1 = (bf16[256,256]{1,0:T(8,128)(2,1)S(1)}, bf16[256,256]{1,0:T(8,128)(2,1)S(1)}) custom-call(s32[2]{0:T(128)S(1)} %copy-done.6, f32[8]{0:T(128)S(1)} %copy-done.11, bf16[512,1024]{1,0:T(8,128)(2,1)S(1)} %column_normed.1.tokens, bf16[1024,768]{1,0:T(8,128)(2,1)S(1)} %column_project.1.weight), custom_call_target="tpu_custom_call" | custom-call | flops 1024 | bytes 1024 | tf_op jit(solution)/shard_map/column_attention/pallas_call | solution.py:30
  55.6 1.5 %collective-permute-start.20 = (bf16[256,1024]{1,0:T(8,128)(2,1)S(1)}, bf16[256,1024]{1,0:T(8,128)(2,1)S(1)}, u32[]{:S(2)}, u32[]{:S(2)}) collective-permute-start(bf16[256,1024]{1,0:T(8,128)(2,1)S(1)} %pad_maximum_fusion.refs_0_), channel_id=1, source_target_pairs={{0,6},{2,4},{4,2},{6,0},{8,14},{10,12},{12,10},{14,8},{16,22},{18,... | collective-permute-start | bytes 1572872 | tf_op jit(solution)/shard_map/ppermute | solution.py:81
  57.4 1.7 %collective-permute-start.18 = (bf16[256,1024]{1,0:T(8,128)(2,1)S(1)}, bf16[256,1024]{1,0:T(8,128)(2,1)S(1)}, u32[]{:S(2)}, u32[]{:S(2)}) collective-permute-start(bf16[256,1024]{1,0:T(8,128)(2,1)S(1)} %pad_maximum_fusion.refs_0_), channel_id=1, source_target_pairs={{0,2},{2,0},{4,6},{6,4},{8,10},{10,8},{12,14},{14,12},{16,18},{18,... | collective-permute-start | bytes 1572872 | tf_op jit(solution)/shard_map/ppermute | solution.py:81
  59.1 1.8 %row_normed.1 = bf16[256,1024]{1,0:T(8,128)(2,1)} custom-call(bf16[256,256]{1,0:T(8,128)(2,1)S(1)} %get-tuple-element.45.mine, bf16[256,256]{1,0:T(8,128)(2,1)S(1)} %collective-permute-done.16.theirs, bf16[1024,256]{1,0:T(8,128)(2,1)S(1)} %column_output.1.near, bf16[1024,256]{1,0:T(8,128)(2,1)S(1)} %collective-permute-done.17.far, ...), custom_call_target="tpu_custom_call" | custom-call | flops 1024 | bytes 1024 | tf_op jit(solution)/shard_map/row_normed/pallas_call | solution.py:30
  60.9 4.6 %all-to-all-start = ((bf16[16,16,1024]{2,1,0:T(8,128)(2,1)}), bf16[16,16,1024]{2,1,0:T(8,128)(2,1)}, u32[]{:S(2)}, u32[]{:S(2)}) async-start(bf16[16,16,1024]{2,1,0:T(8,128)(2,1)} %bitcast.6), calls=%async_computation | async-start | bytes 1048576 | tf_op jit(solution)/shard_map/all_to_all | solution.py:439
  65.6 2.8 %collective-permute-start.21 = (bf16[128,512]{1,0:T(8,128)(2,1)S(1)}, bf16[128,512]{1,0:T(8,128)(2,1)S(1)}, u32[]{:S(2)}, u32[]{:S(2)}) collective-permute-start(bf16[128,512]{1,0:T(8,128)(2,1)S(1)} %pad_maximum_fusion.4), channel_id=1, source_target_pairs={{0,16},{2,18},{4,20},{6,22},{8,24},{10,26},{12,28},{14,30},{16,0},... | collective-permute-start | bytes 393224 | tf_op jit(solution)/shard_map/ppermute | solution.py:372
  68.4 16.5 %collective-permute-done.21.back = bf16[128,512]{1,0:T(8,128)(2,1)S(1)} collective-permute-done((bf16[128,512]{1,0:T(8,128)(2,1)S(1)}, bf16[128,512]{1,0:T(8,128)(2,1)S(1)}, u32[]{:S(2)}, u32[]{:S(2)}) %collective-permute-start.21) | collective-permute-done | bytes 131104 | tf_op jit(solution)/shard_map/ppermute | solution.py:372
  89.1 1.5 %collective-permute-done.23.refs_5_ = bf16[256,1024]{1,0:T(8,128)(2,1)S(1)} collective-permute-done((bf16[256,1024]{1,0:T(8,128)(2,1)S(1)}, bf16[256,1024]{1,0:T(8,128)(2,1)S(1)}, u32[]{:S(2)}, u32[]{:S(2)}) %collective-permute-start.23) | collective-permute-done | bytes 524320 | tf_op jit(solution)/shard_map/ppermute | solution.py:23
  92.2 6.9 %row_attention.1 = bf16[256,512]{1,0:T(8,128)(2,1)} custom-call(s32[2]{0:T(128)} %pad_add_fusion.place, f32[8]{0:T(128)} %slopes.3, bf16[256,1024]{1,0:T(8,128)(2,1)} %bitcast.7.tokens, bf16[256,1024]{1,0:T(8,128)(2,1)} %copy-done.12, bf16[256,1024]{1,0:T(8,128)(2,1)} %copy-done.15, bf16[256,1024]{1,0:T(8,128)(2,1)} %copy-done.14, ...), custom_call_target="tpu_custom_call" | custom-call | flops 1024 | bytes 1024 | tf_op jit(solution)/shard_map/row_attention/pallas_call | solution.py:30
  99.2 3.9 %all-to-all-start.1 = ((bf16[16,16,512]{2,1,0:T(8,128)(2,1)}), bf16[16,16,512]{2,1,0:T(8,128)(2,1)S(1)}, u32[]{:S(2)}, u32[]{:S(2)}) async-start(bf16[16,16,512]{2,1,0:T(8,128)(2,1)} %bitcast.18), calls=%async_computation.1 | async-start | bytes 524288 | tf_op jit(solution)/shard_map/all_to_all | solution.py:464
  103.1 1.8 %middle.1.refs_8_ = f32[256,1024]{1,0:T(8,128)S(1)} custom-call(s32[2]{0:T(128)S(1)} %copy-done.7, bf16[256,256]{1,0:T(8,128)(2,1)S(1)} %get-tuple-element.45.mine, bf16[256,256]{1,0:T(8,128)(2,1)S(1)} %collective-permute-done.16.theirs, bf16[128,512]{1,0:T(8,128)(2,1)S(1)} %collective-permute-done.21.back, bf16[1024,256]{1,0:T(8,128)(2,1)S(1)} %column_output.1.near, ...), custom_call_target="tpu_custom_call" | custom-call | flops 1024 | bytes 1024 | tf_op jit(solution)/shard_map/middle/pallas_call | solution.py:30
  105.9 7.4 %all-to-all-done.1 = bf16[16,16,512]{2,1,0:T(8,128)(2,1)S(1)} async-done(((bf16[16,16,512]{2,1,0:T(8,128)(2,1)}), bf16[16,16,512]{2,1,0:T(8,128)(2,1)S(1)}, u32[]{:S(2)}, u32[]{:S(2)}) %all-to-all-start.1) | async-done | bytes 262176 | tf_op jit(solution)/shard_map/all_to_all | solution.py:464
  113.9 4.2 %block_output.1 = bf16[64,4,1024]{2,1,0:T(4,128)(2,1)} custom-call(s32[2]{0:T(128)} %pad_add_fusion.place, bf16[256,512]{1,0:T(8,128)(2,1)} %bitcast.17, bf16[256,1024]{1,0:T(8,128)(2,1)} %copy-done.12, bf16[256,1024]{1,0:T(8,128)(2,1)} %copy-done.15, bf16[256,1024]{1,0:T(8,128)(2,1)} %copy-done.14, bf16[256,1024]{1,0:T(8,128)(2,1)} %copy-done.13, ...), custom_call_target="tpu_custom_call" | custom-call | flops 1024 | bytes 1024 | tf_op jit(solution)/shard_map/block_output/pallas_call | solution.py:30
  (91 shorter events, 20.2 us)
Async XLA Ops:
  0.0 13.7 %collective-permute-start.2 = (bf16[64,768]{1,0:T(8,128)(2,1)}, bf16[64,768]{1,0:T(8,128)(2,1)S(1)}, u32[]{:S(2)}, u32[]{:S(2)}) collective-permute-start(bf16[64,768]{1,0:T(8,128)(2,1)} %param.18), channel_id=1, source_target_pairs={{0,16},{2,18},{4,20},{6,22},{8,24},{10,26},{12,28},{14,30},{16,0},... | collective-permute-start | bytes 294920 | tf_op jit(solution)/shard_map/ppermute | solution.py:71
  4.0 9.7 %collective-permute-start.1 = (bf16[64,768]{1,0:T(8,128)(2,1)}, bf16[64,768]{1,0:T(8,128)(2,1)S(1)}, u32[]{:S(2)}, u32[]{:S(2)}) collective-permute-start(bf16[64,768]{1,0:T(8,128)(2,1)} %param.18), channel_id=1, source_target_pairs={{0,8},{2,10},{4,12},{6,14},{8,0},{10,2},{12,4},{14,6},{16,24},{18,... | collective-permute-start | bytes 294920 | tf_op jit(solution)/shard_map/ppermute | solution.py:71
  5.6 8.1 %collective-permute-start.3 = (bf16[64,768]{1,0:T(8,128)(2,1)}, bf16[64,768]{1,0:T(8,128)(2,1)S(1)}, u32[]{:S(2)}, u32[]{:S(2)}) collective-permute-start(bf16[64,768]{1,0:T(8,128)(2,1)} %param.18), channel_id=1, source_target_pairs={{0,24},{2,26},{4,28},{6,30},{8,16},{10,18},{12,20},{14,22},{16,8},... | collective-permute-start | bytes 294920 | tf_op jit(solution)/shard_map/ppermute | solution.py:71
  5.6 7.3 %collective-permute-start.4 = (bf16[64,256]{1,0:T(8,128)(2,1)}, bf16[64,256]{1,0:T(8,128)(2,1)S(1)}, u32[]{:S(2)}, u32[]{:S(2)}) collective-permute-start(bf16[64,256]{1,0:T(8,128)(2,1)} %param.19), channel_id=1, source_target_pairs={{0,8},{2,10},{4,12},{6,14},{8,0},{10,2},{12,4},{14,6},{16,24},{18,... | collective-permute-start | bytes 98312 | tf_op jit(solution)/shard_map/ppermute | solution.py:76
  8.3 6.8 %collective-permute-start.5 = (bf16[64,1024]{1,0:T(8,128)(2,1)S(1)}, bf16[64,1024]{1,0:T(8,128)(2,1)S(1)}, u32[]{:S(2)}, u32[]{:S(2)}) collective-permute-start(bf16[64,1024]{1,0:T(8,128)(2,1)S(1)} %row_shards.1), channel_id=1, source_target_pairs={{0,8},{2,10},{4,12},{6,14},{8,0},{10,2},{12,4},{14,6},{16,24},{18,... | collective-permute-start | bytes 393224 | tf_op jit(solution)/shard_map/ppermute | solution.py:76
  15.1 20.6 %collective-permute-start.6 = (bf16[144,1024]{1,0:T(8,128)(2,1)}, bf16[144,1024]{1,0:T(8,128)(2,1)S(1)}, u32[]{:S(2)}, u32[]{:S(2)}) collective-permute-start(bf16[144,1024]{1,0:T(8,128)(2,1)} %get-tuple-element.33), channel_id=1, source_target_pairs={{0,16},{2,18},{4,20},{6,22},{8,24},{10,26},{12,28},{14,30},{16,0},... | collective-permute-start | bytes 884744 | tf_op jit(solution)/shard_map/ppermute | solution.py:372
  17.2 18.5 %collective-permute-start = (bf16[144,1024]{1,0:T(8,128)(2,1)}, bf16[144,1024]{1,0:T(8,128)(2,1)S(1)}, u32[]{:S(2)}, u32[]{:S(2)}) collective-permute-start(bf16[144,1024]{1,0:T(8,128)(2,1)} %get-tuple-element.31.own.kept), channel_id=1, source_target_pairs={{0,1},{1,0},{2,3},{3,2},{4,5},{5,4},{6,7},{7,6},{8,9},{9,8},{10,11... | collective-permute-start | bytes 884744 | tf_op jit(solution)/shard_map/ppermute | solution.py:23
  17.2 16.8 %collective-permute-start.11 = (bf16[128,256]{1,0:T(8,128)(2,1)S(1)}, bf16[128,256]{1,0:T(8,128)(2,1)S(1)}, u32[]{:S(2)}, u32[]{:S(2)}) collective-permute-start(bf16[128,256]{1,0:T(8,128)(2,1)S(1)} %pad_maximum_fusion.5), channel_id=1, source_target_pairs={{0,16},{2,18},{4,20},{6,22},{8,24},{10,26},{12,28},{14,30},{16,0},... | collective-permute-start | bytes 196616 | tf_op jit(solution)/shard_map/ppermute | solution.py:76
  18.1 20.0 %collective-permute-start.10 = (bf16[256,768]{1,0:T(8,128)(2,1)S(1)}, bf16[256,768]{1,0:T(8,128)(2,1)S(1)}, u32[]{:S(2)}, u32[]{:S(2)}) collective-permute-start(bf16[256,768]{1,0:T(8,128)(2,1)S(1)} %pad_maximum_fusion.1.w0), channel_id=1, source_target_pairs={{0,6},{2,4},{4,2},{6,0},{8,14},{10,12},{12,10},{14,8},{16,22},{18,... | collective-permute-start | bytes 1179656 | tf_op jit(solution)/shard_map/ppermute | solution.py:81
  20.6 18.0 %collective-permute-start.9 = (bf16[256,768]{1,0:T(8,128)(2,1)S(1)}, bf16[256,768]{1,0:T(8,128)(2,1)S(1)}, u32[]{:S(2)}, u32[]{:S(2)}) collective-permute-start(bf16[256,768]{1,0:T(8,128)(2,1)S(1)} %pad_maximum_fusion.1.w0), channel_id=1, source_target_pairs={{0,4},{2,6},{4,0},{6,2},{8,12},{10,14},{12,8},{14,10},{16,20},{18,... | collective-permute-start | bytes 1179656 | tf_op jit(solution)/shard_map/ppermute | solution.py:81
  34.0 10.5 %collective-permute-start.8 = (bf16[256,768]{1,0:T(8,128)(2,1)S(1)}, bf16[256,768]{1,0:T(8,128)(2,1)S(1)}, u32[]{:S(2)}, u32[]{:S(2)}) collective-permute-start(bf16[256,768]{1,0:T(8,128)(2,1)S(1)} %pad_maximum_fusion.1.w0), channel_id=1, source_target_pairs={{0,2},{2,0},{4,6},{6,4},{8,10},{10,8},{12,14},{14,12},{16,18},{18,... | collective-permute-start | bytes 1179656 | tf_op jit(solution)/shard_map/ppermute | solution.py:81
  35.7 15.2 %collective-permute-start.15 = (bf16[128,1024]{1,0:T(8,128)(2,1)S(1)}, bf16[128,1024]{1,0:T(8,128)(2,1)S(1)}, u32[]{:S(2)}, u32[]{:S(2)}) collective-permute-start(bf16[128,1024]{1,0:T(8,128)(2,1)S(1)} %pad_maximum_fusion.2), channel_id=1, source_target_pairs={{0,16},{2,18},{4,20},{6,22},{8,24},{10,26},{12,28},{14,30},{16,0},... | collective-permute-start | bytes 786440 | tf_op jit(solution)/shard_map/ppermute | solution.py:76
  44.5 9.9 %collective-permute-start.14 = (bf16[256,256]{1,0:T(8,128)(2,1)S(1)}, bf16[256,256]{1,0:T(8,128)(2,1)S(1)}, u32[]{:S(2)}, u32[]{:S(2)}) collective-permute-start(bf16[256,256]{1,0:T(8,128)(2,1)S(1)} %pad_maximum_fusion.3.w0), channel_id=1, source_target_pairs={{0,6},{2,4},{4,2},{6,0},{8,14},{10,12},{12,10},{14,8},{16,22},{18,... | collective-permute-start | bytes 393224 | tf_op jit(solution)/shard_map/ppermute | solution.py:81
  47.2 7.2 %collective-permute-start.13 = (bf16[256,256]{1,0:T(8,128)(2,1)S(1)}, bf16[256,256]{1,0:T(8,128)(2,1)S(1)}, u32[]{:S(2)}, u32[]{:S(2)}) collective-permute-start(bf16[256,256]{1,0:T(8,128)(2,1)S(1)} %pad_maximum_fusion.3.w0), channel_id=1, source_target_pairs={{0,4},{2,6},{4,0},{6,2},{8,12},{10,14},{12,8},{14,10},{16,20},{18,... | collective-permute-start | bytes 393224 | tf_op jit(solution)/shard_map/ppermute | solution.py:81
  47.7 6.7 %collective-permute-start.12 = (bf16[256,256]{1,0:T(8,128)(2,1)S(1)}, bf16[256,256]{1,0:T(8,128)(2,1)S(1)}, u32[]{:S(2)}, u32[]{:S(2)}) collective-permute-start(bf16[256,256]{1,0:T(8,128)(2,1)S(1)} %pad_maximum_fusion.3.w0), channel_id=1, source_target_pairs={{0,2},{2,0},{4,6},{6,4},{8,10},{10,8},{12,14},{14,12},{16,18},{18,... | collective-permute-start | bytes 393224 | tf_op jit(solution)/shard_map/ppermute | solution.py:81
  55.0 4.1 %collective-permute-start.17 = (bf16[1024,256]{1,0:T(8,128)(2,1)S(1)}, bf16[1024,256]{1,0:T(8,128)(2,1)S(1)}, u32[]{:S(2)}, u32[]{:S(2)}) collective-permute-start(bf16[1024,256]{1,0:T(8,128)(2,1)S(1)} %column_output.1.near), channel_id=1, source_target_pairs={{0,1},{1,0},{2,3},{3,2},{4,5},{5,4},{6,7},{7,6},{8,9},{9,8},{10,11... | collective-permute-start | bytes 1572872 | tf_op jit(solution)/shard_map/ppermute | solution.py:23
  55.1 4.0 %collective-permute-start.16 = (bf16[256,256]{1,0:T(8,128)(2,1)S(1)}, bf16[256,256]{1,0:T(8,128)(2,1)S(1)}, u32[]{:S(2)}, u32[]{:S(2)}) collective-permute-start(bf16[256,256]{1,0:T(8,128)(2,1)S(1)} %get-tuple-element.46), channel_id=1, source_target_pairs={{0,1},{1,0},{2,3},{3,2},{4,5},{5,4},{6,7},{7,6},{8,9},{9,8},{10,11... | collective-permute-start | bytes 393224 | tf_op jit(solution)/shard_map/ppermute | solution.py:23
  55.6 29.3 %collective-permute-start.20 = (bf16[256,1024]{1,0:T(8,128)(2,1)S(1)}, bf16[256,1024]{1,0:T(8,128)(2,1)S(1)}, u32[]{:S(2)}, u32[]{:S(2)}) collective-permute-start(bf16[256,1024]{1,0:T(8,128)(2,1)S(1)} %pad_maximum_fusion.refs_0_), channel_id=1, source_target_pairs={{0,6},{2,4},{4,2},{6,0},{8,14},{10,12},{12,10},{14,8},{16,22},{18,... | collective-permute-start | bytes 1572872 | tf_op jit(solution)/shard_map/ppermute | solution.py:81
  57.1 29.2 %collective-permute-start.19 = (bf16[256,1024]{1,0:T(8,128)(2,1)S(1)}, bf16[256,1024]{1,0:T(8,128)(2,1)S(1)}, u32[]{:S(2)}, u32[]{:S(2)}) collective-permute-start(bf16[256,1024]{1,0:T(8,128)(2,1)S(1)} %pad_maximum_fusion.refs_0_), channel_id=1, source_target_pairs={{0,4},{2,6},{4,0},{6,2},{8,12},{10,14},{12,8},{14,10},{16,20},{18,... | collective-permute-start | bytes 1572872 | tf_op jit(solution)/shard_map/ppermute | solution.py:81
  57.4 29.7 %collective-permute-start.18 = (bf16[256,1024]{1,0:T(8,128)(2,1)S(1)}, bf16[256,1024]{1,0:T(8,128)(2,1)S(1)}, u32[]{:S(2)}, u32[]{:S(2)}) collective-permute-start(bf16[256,1024]{1,0:T(8,128)(2,1)S(1)} %pad_maximum_fusion.refs_0_), channel_id=1, source_target_pairs={{0,2},{2,0},{4,6},{6,4},{8,10},{10,8},{12,14},{14,12},{16,18},{18,... | collective-permute-start | bytes 1572872 | tf_op jit(solution)/shard_map/ppermute | solution.py:81
  60.9 31.3 %all-to-all-start = ((bf16[16,16,1024]{2,1,0:T(8,128)(2,1)}), bf16[16,16,1024]{2,1,0:T(8,128)(2,1)}, u32[]{:S(2)}, u32[]{:S(2)}) async-start(bf16[16,16,1024]{2,1,0:T(8,128)(2,1)} %bitcast.6), calls=%async_computation | async-start | bytes 1048576 | tf_op jit(solution)/shard_map/all_to_all | solution.py:439
  65.6 19.3 %collective-permute-start.21 = (bf16[128,512]{1,0:T(8,128)(2,1)S(1)}, bf16[128,512]{1,0:T(8,128)(2,1)S(1)}, u32[]{:S(2)}, u32[]{:S(2)}) collective-permute-start(bf16[128,512]{1,0:T(8,128)(2,1)S(1)} %pad_maximum_fusion.4), channel_id=1, source_target_pairs={{0,16},{2,18},{4,20},{6,22},{8,24},{10,26},{12,28},{14,30},{16,0},... | collective-permute-start | bytes 393224 | tf_op jit(solution)/shard_map/ppermute | solution.py:372
  87.8 4.4 %collective-permute-start.25 = (bf16[256,1024]{1,0:T(8,128)(2,1)S(1)}, bf16[256,1024]{1,0:T(8,128)(2,1)}, u32[]{:S(2)}, u32[]{:S(2)}) collective-permute-start(bf16[256,1024]{1,0:T(8,128)(2,1)S(1)} %collective-permute-done.20.refs_3_), channel_id=1, source_target_pairs={{0,1},{1,0},{2,3},{3,2},{4,5},{5,4},{6,7},{7,6},{8,9},{9,8},{10,11... | collective-permute-start | bytes 1572872 | tf_op jit(solution)/shard_map/ppermute | solution.py:23
  99.2 14.1 %all-to-all-start.1 = ((bf16[16,16,512]{2,1,0:T(8,128)(2,1)}), bf16[16,16,512]{2,1,0:T(8,128)(2,1)S(1)}, u32[]{:S(2)}, u32[]{:S(2)}) async-start(bf16[16,16,512]{2,1,0:T(8,128)(2,1)} %bitcast.18), calls=%async_computation.1 | async-start | bytes 524288 | tf_op jit(solution)/shard_map/all_to_all | solution.py:464
  (24 other events, 209.0 us)

commit v3 on v2

--- a/solution.py
+++ b/solution.py
@@ -26,7 +26,7 @@
 SCALARS = pl.BlockSpec(memory_space=pltpu.SMEM)
 
 
-def call(kernel, out, name, scalars, arrays, given=(), scratch=(), room=24, space=pltpu.VMEM):
+def call(kernel, out, name, scalars, arrays, given=(), scratch=(), cost=2**10, room=24, space=pltpu.VMEM):
     return pl.pallas_call(
         kernel,
         out_shape=out,
@@ -36,7 +36,7 @@
         out_specs=jax.tree.map(lambda _: pl.BlockSpec(memory_space=space), out),
         scratch_shapes=scratch,
         compiler_params=pltpu.CompilerParams(vmem_limit_bytes=room * 2**20),
-        cost_estimate=pl.CostEstimate(flops=2**10, bytes_accessed=2**10, transcendentals=0),
+        cost_estimate=pl.CostEstimate(flops=2**10, bytes_accessed=cost, transcendentals=0),
         name=name,
     )(*scalars, *arrays, *given)
 
@@ -81,10 +81,11 @@
     return [part] + [lax.ppermute(part, "lon", at(lambda i: i ^ k, length)) for k in range(1, PLANE)]
 
 
-def pack_rows_kernel(project, output, out):
-    split = project.shape[1]
-    out[:, :split] = by_kind(project[...])
-    out[:, split:] = output[...]
+def relayed_plane(part, length):
+    half = part.shape[0] // 2
+    step = lambda value, k: lax.ppermute(value, "lon", at(lambda i: i ^ k, length))
+    first, second = step(part, 1), step(part, 2)
+    return [part, first, second], [step(second[:half], 1), step(first[half:], 2)]
 
 
 def by_kind(weight):
@@ -95,11 +96,13 @@
 
 def places(shard, place, pieces):
     line, spot = place[0] // PLANE, place[0] % PLANE
-    for j, piece in enumerate(pieces):
-        for k in range(piece.shape[0] // shard):
-            owner = lax.bitwise_xor(line, k) * PLANE + lax.bitwise_xor(spot, j)
-            there = pl.ds(pl.multiple_of(owner * shard, shard), shard)
-            yield piece, slice(k * shard, (k + 1) * shard), there
+    lines = pieces[0].shape[0] // shard
+    blocks = [(piece, k) for piece in pieces for k in range(piece.shape[0] // shard)]
+    for number, (piece, k) in enumerate(blocks):
+        owner = lax.bitwise_xor(line, number % lines) * PLANE
+        owner += lax.bitwise_xor(spot, number // lines)
+        there = pl.ds(pl.multiple_of(owner * shard, shard), shard)
+        yield piece, slice(k * shard, (k + 1) * shard), there
 
 
 def order_kernel(shard, sort, place, w0, w1, w2, w3, out):
@@ -149,15 +152,17 @@
     return (grid == lax.rem(spot, rows) * cols + column).astype(jnp.bfloat16)
 
 
-def pack_tokens_kernel(lons, place, tokens, mask, keep, send, *scratch):
+def first_kernel(lons, place, tokens, mask, project, output, keep, send, packed, *scratch):
     *held, sems = scratch
-    wait(bring(zip((tokens, mask), held), sems))
-    tokens, mask = held
+    coming = bring(zip((tokens, mask, project, output), held), sems)
+    tokens, mask, project, output = held
     rows, cols, width = tokens.shape
     half = rows * cols // 2
     side = place[0] // (lons // 2)
+    to_slots = slots(cols, rows, side)
+    wait(coming[:2])
     flat = tokens[...].astype(jnp.float32).reshape(rows * cols, width).astype(jnp.bfloat16)
-    in_slots = dot(slots(cols, rows, side), flat).astype(jnp.bfloat16)
+    in_slots = dot(to_slots, flat).astype(jnp.bfloat16)
     land = mask[...].astype(jnp.float32)
     parts = [land[c : c + 1, :] for c in range(cols)]
     halves = [jnp.concatenate(parts[: cols // 2], axis=1), jnp.concatenate(parts[cols // 2 :], axis=1)]
@@ -166,6 +171,10 @@
         out[half:, :] = jnp.zeros((EXTRA, width), jnp.bfloat16)
         row = jnp.where(side == k, halves[0], halves[1])
         out[half:, :half] = jnp.broadcast_to(row, (EXTRA, half)).astype(jnp.bfloat16)
+    wait(coming[2:])
+    split = project.shape[1]
+    packed[:, :split] = by_kind(project[...])
+    packed[:, split:] = output[...]
 
 
 def column_norm_kernel(own, other, far_own, far_other, embed, gain, out):
@@ -245,9 +254,15 @@
     out[...] = dot(by_row, normed).astype(jnp.bfloat16)
 
 
-def home_kernel(lons, place, mine, theirs, back, near, far, tokens, mask, embed, out, *scratch):
-    *held, total, sems = scratch
+def home_kernel(shard, lons, place, mine, theirs, back, near, far, *refs):
+    pieces, (tokens, mask, embed, out, out_weight, *held, weight_sems, sems) = refs[:-10], refs[-10:]
+    lane = pieces[0].shape[1] - out_weight.shape[2]
     coming = bring(zip((tokens, mask, embed), held), sems)
+    count = len(pieces) // 2
+    later = []
+    for half in range(2):
+        mine_of = pieces[half * count : (half + 1) * count]
+        later += bring_in_order(shard, place, mine_of, lane, out_weight.at[half], weight_sems.at[half])
     tokens, mask, embed = held
     rows, cols, _ = tokens.shape
     half, width = rows * cols // 2, near.shape[1]
@@ -258,15 +273,15 @@
         mixed += dot(to_grid[:, half:], back[:, lane * width : (lane + 1) * width])
         update += dot_t(mixed.astype(jnp.bfloat16), weight[...])
     wait(coming)
-    total[...] = land_start(tokens[...], mask[...], embed[...]) + update
-    wait(bring([(total, out)], sems))
+    out[...] = land_start(tokens[...], mask[...], embed[...]) + update
+    wait(later)
 
 
 def row_kernel(shard, cols, rows, place, slopes, tokens, *refs):
     pieces, (out, weight, sems) = refs[:-3], refs[-3:]
     coming = [
         bring_in_order(
-            shard, place, pieces[half * PLANE : (half + 1) * PLANE], 0, weight.at[half], sems.at[half]
+            shard, place, pieces[half * len(pieces) // 2 : (half + 1) * len(pieces) // 2], 0, weight.at[half], sems.at[half]
         )
         for half in range(2)
     ]
@@ -315,25 +330,10 @@
             out[:, start : start + PAIR] = dot(homeward, mixed).astype(jnp.bfloat16)
 
 
-def final_kernel(shard, place, mixed, *refs):
-    pieces, middle, out, weight, total, sems, total_sems = refs[:-6], *refs[-6:]
+def final_kernel(middle, mixed, weight, out):
     width = weight.shape[2]
-    lane = pieces[0].shape[1] - width
-    coming = [
-        bring_in_order(
-            shard, place, pieces[half * PLANE : (half + 1) * PLANE], lane, weight.at[half], sems.at[half]
-        )
-        for half in range(2)
-    ]
-    rows = total.shape[0] // 4
-    cut = [slice(i * rows, (i + 1) * rows) for i in range(4)]
-    last = bring([(middle.at[here, :], total.at[here, :]) for here in cut], total_sems)
-    update = 0.0
-    for half in range(2):
-        wait(coming[half])
-        update += dot_t(mixed[:, half * width : (half + 1) * width], weight[half])
-    wait(last)
-    out[...] = (total[...] + update).reshape(out.shape).astype(jnp.bfloat16)
+    update = dot_t(mixed[:, :width], weight[0]) + dot_t(mixed[:, width:], weight[1])
+    out[...] = (middle[...] + update).reshape(out.shape).astype(jnp.bfloat16)
 
 
 def fast(
@@ -374,28 +374,27 @@
     )
     packed = bf16(tokens // 2 + EXTRA, width)
     mask = land_mask.T
-    held = [pltpu.VMEM(fields.shape, fields.dtype), pltpu.VMEM(mask.shape, mask.dtype)]
 
     first = along_lines(column_project, lon_count)
-    keep, send = call(
-        functools.partial(pack_tokens_kernel, lon_count),
-        (packed, packed),
+    third = bf16(shard, row_project.shape[1] + row_output.shape[1])
+    given = (fields, mask, row_project, row_output)
+    keep, send, third = call(
+        functools.partial(first_kernel, lon_count),
+        (packed, packed, third),
         "loop_tokens",
         (place,),
         (),
-        (fields, mask),
-        held + [pltpu.SemaphoreType.DMA((2,))],
+        given,
+        [pltpu.VMEM(v.shape, v.dtype) for v in given] + [pltpu.SemaphoreType.DMA((4,))],
         room=60,
     )
     second = column_output
-    third = bf16(shard, row_project.shape[1] + row_output.shape[1])
-    third = call(pack_rows_kernel, third, "row_shards", (), (row_project, row_output))
     if lon_count > PLANE:
         second = doubled(second, PLANE, lon_count)
         third = doubled(third, PLANE, lon_count)
     keep_other = swap_bands(keep)
-    first, second, third, send = lax.optimization_barrier((first, second, third, send))
     far = antipode(send)
+    first, second, third, keep_other = lax.optimization_barrier((first, second, third, keep_other))
     pieces = across_plane(first, lon_count)
     if lon_count > 2 * PLANE:
         second = doubled(second, 2 * PLANE, lon_count)
@@ -407,9 +406,9 @@
         (),
         (keep, keep_other, far, far_other, embed, column_gain),
     )
-    normed, pieces, second = lax.optimization_barrier((normed, pieces, second))
+    project = order(pieces, "column_project", True, project_shape)
+    normed, project, second = lax.optimization_barrier((normed, project, second))
     third, _ = lax.optimization_barrier((third, far))
-    project = order(pieces, "column_project", True, project_shape)
     second = across_plane(second, lon_count)
     if lon_count > 2 * PLANE:
         third = doubled(third, 2 * PLANE, lon_count)
@@ -422,13 +421,14 @@
         (normed, project),
         (),
         [pltpu.VMEM((2 * tokens, 3 * attend), jnp.bfloat16)],
+        cost=1 * 2**18,
     )
     theirs = swap_bands(mixed_other)
     second, third, mixed_own = lax.optimization_barrier((second, third, mixed_own))
     output = order(second, "column_output", False, output_shape)
     output_far = swap_bands(output)
-    third = across_plane(third, lon_count)
-    back = antipode(jnp.concatenate([mixed_own[tokens // 2 :], theirs[tokens // 2 :]], axis=1))
+    third, late = relayed_plane(third, lon_count)
+    to_home = jnp.concatenate([mixed_own[tokens // 2 :], theirs[tokens // 2 :]], axis=1)
     row_normed = call(
         functools.partial(middle_kernel, cols),
         bf16(tokens, width),
@@ -437,19 +437,10 @@
         (mixed_own, theirs, output, output_far, keep, far, embed, row_gain),
     )
     spread = lax.all_to_all(row_normed, "lon", split_axis=0, concat_axis=0, tiled=True)
-    third, back = lax.optimization_barrier((third, back))
+    home = antipode(to_home)
+    third = third + late
     third_far = [swap_bands(piece) for piece in third]
-    middle = call(
-        functools.partial(home_kernel, lon_count),
-        f32(tokens, width),
-        "middle",
-        (place,),
-        (mixed_own, theirs, back, output, output_far),
-        (fields, mask, embed),
-        held + [pltpu.VMEM(embed.shape, embed.dtype), pltpu.VMEM((tokens, width), jnp.float32)]
-        + [pltpu.SemaphoreType.DMA((3,))],
-        space=pltpu.HBM,
-    )
+    spread, home = lax.optimization_barrier((spread, home))
     sems = pltpu.SemaphoreType.DMA((2, lon_count))
     row_mixed = call(
         functools.partial(row_kernel, shard, cols, band // lon_count),
@@ -462,20 +453,19 @@
         room=60,
     )
     back = lax.all_to_all(row_mixed, "lon", split_axis=0, concat_axis=0, tiled=True)
+    given = (*third, *third_far, fields, mask, embed)
+    middle, row_out = call(
+        functools.partial(home_kernel, shard, lon_count),
+        (f32(tokens, width), bf16(2, *output_shape.shape)),
+        "middle",
+        (place,),
+        (mixed_own, theirs, home, output, output_far),
+        given,
+        [pltpu.VMEM(v.shape, v.dtype) for v in given[-3:]] + [sems, pltpu.SemaphoreType.DMA((3,))],
+        room=56,
+    )
     return call(
-        functools.partial(final_kernel, shard),
-        bf16(band, cols, width),
-        "block_output",
-        (place,),
-        (back,),
-        (*third, *third_far, middle),
-        [
-            pltpu.VMEM((2, *output_shape.shape), jnp.bfloat16),
-            pltpu.VMEM((tokens, width), jnp.float32),
-            sems,
-            pltpu.SemaphoreType.DMA((4,)),
-        ],
-        room=60,
+        final_kernel, bf16(band, cols, width), "block_output", (), (middle, back, row_out)
     )
 
 

time: 119 us -> 109 us (0.916)
  waiting for transfers between devices: 53.3 us -> 40.3 us
  starting transfers between devices: 35.4 us -> 38.3 us
    ppermute x4, waiting for transfers between devices: 16.2 us -> 7.09 us  [doubled(): got = lax.ppermute(weight, 'lon', at(lambda i: i ^ step, length))]
    ppermute x0 -> x4, starting transfers between devices: none -> 6.23 us  [relayed_plane(): lax.ppermute(value, 'lon', at(lambda i: i ^ k, length))]
    ppermute x0 -> x4, waiting for transfers between devices: none -> 6.19 us  [relayed_plane(): lax.ppermute(value, 'lon', at(lambda i: i ^ k, length))]
    ppermute x9 -> x6, waiting for transfers between devices: 8.65 us -> 3.26 us  [across_plane(): lax.ppermute(part, 'lon', at(lambda i: i ^ k, length))]
    ppermute x9 -> x6, starting transfers between devices: 11.7 us -> 7.11 us  [across_plane(): lax.ppermute(part, 'lon', at(lambda i: i ^ k, length))]
    ppermute x4, starting transfers between devices: 3.09 us -> 5.45 us  [doubled(): got = lax.ppermute(weight, 'lon', at(lambda i: i ^ step, length))]
    all_to_all x1, waiting for transfers between devices: 7.36 us -> 5.16 us  [fast(): lax.all_to_all(row_mixed, 'lon', split_axis=0, concat_axis=0, tiled=True)]
    ppermute x8 -> x9, waiting for transfers between devices: 4.62 us -> 2.94 us  [swap_bands(): return lax.ppermute(value, 'lat', at(lambda i: 1 - i, 2))]
  transfers between devices with their start and end apart: 28 -> 30, of which waited for: 13 -> 13; matrix products, arithmetic and copies ran while one was open for 2% -> 3% of each run, Pallas kernels for 9% -> 13%
where the time goes in v3:
time: 109 us; the launch traced here: 108 us
  waiting for transfers between devices  40.3 us (37%)
  starting transfers between devices  38.3 us (35%)
  Pallas kernels  22.7 us (21%)
  other arithmetic  3.3 us (3%)
  local copies, waits for them, and re-layouts  3.13 us (3%)
    pallas_call x9, Pallas kernels, call(): pl.pallas_call(kernel, out_shape=out, in_specs=[SCALARS] * len(scalars) +...  22.7 us
    ppermute x2, waiting for transfers between devices, fast(): lax.ppermute(value, 'lon', at(lambda i: (i + lon_count // 2) % lon_count,...  15.7 us
    ppermute x6, starting transfers between devices, across_plane(): lax.ppermute(part, 'lon', at(lambda i: i ^ k, length))  7.11 us
    ppermute x4, waiting for transfers between devices, doubled(): got = lax.ppermute(weight, 'lon', at(lambda i: i ^ step, length))  7.09 us
    ppermute x4, starting transfers between devices, relayed_plane(): lax.ppermute(value, 'lon', at(lambda i: i ^ k, length))  6.23 us
    ppermute x4, waiting for transfers between devices, relayed_plane(): lax.ppermute(value, 'lon', at(lambda i: i ^ k, length))  6.19 us
    ppermute x3, starting transfers between devices, along_lines(): lax.ppermute(weight, 'lon', at(lambda i: i ^ k, length))  5.62 us
    ppermute x4, starting transfers between devices, doubled(): got = lax.ppermute(weight, 'lon', at(lambda i: i ^ step, length))  5.45 us
  transfers between devices with their start and end apart: 30, of which 13 were waited for; matrix products, arithmetic and copies ran while one was open for 3% of the time, Pallas kernels for 13%

profile of v3, /device:TPU:0, one launch (start us, length us, event | category | flops | bytes accessed | tf_op | source)
XLA Modules:
  0.0 108.1 jit_solution(57982646799703020)
XLA Ops:
  0.0 4.0 %collective-permute-start.1 = (bf16[64,768]{1,0:T(8,128)(2,1)}, bf16[64,768]{1,0:T(8,128)(2,1)S(1)}, u32[]{:S(2)}, u32[]{:S(2)}) collective-permute-start(bf16[64,768]{1,0:T(8,128)(2,1)} %param.18), channel_id=1, source_target_pairs={{0,16},{2,18},{4,20},{6,22},{8,24},{10,26},{12,28},{14,30},{16,0},... | collective-permute-start | bytes 294920 | tf_op jit(solution)/shard_map/ppermute | solution.py:71
  4.0 1.6 %collective-permute-start = (bf16[64,768]{1,0:T(8,128)(2,1)}, bf16[64,768]{1,0:T(8,128)(2,1)S(1)}, u32[]{:S(2)}, u32[]{:S(2)}) collective-permute-start(bf16[64,768]{1,0:T(8,128)(2,1)} %param.18), channel_id=1, source_target_pairs={{0,8},{2,10},{4,12},{6,14},{8,0},{10,2},{12,4},{14,6},{16,24},{18,... | collective-permute-start | bytes 294920 | tf_op jit(solution)/shard_map/ppermute | solution.py:71
  7.2 2.9 %loop_tokens.1 = (bf16[144,1024]{1,0:T(8,128)(2,1)}, bf16[144,1024]{1,0:T(8,128)(2,1)}, bf16[64,1024]{1,0:T(8,128)(2,1)}) custom-call(s32[2]{0:T(128)} %pad_add_fusion.place, bf16[64,4,1024]{2,1,0:T(4,128)(2,1)} %refs_10_.1, s32[4,64]{1,0:T(4,128)} %bitcast.18, bf16[64,768]{1,0:T(8,128)(2,1)} %project.1, bf16[64,256]{1,0:T(8,128)(2,1)} %output.1), custom_call_target="tpu_custom_call" | custom-call | flops 1024 | bytes 1024 | tf_op jit(solution)/shard_map/loop_tokens/pallas_call | solution.py:30
  12.8 1.7 %collective-permute-start.6 = (bf16[144,1024]{1,0:T(8,128)(2,1)}, bf16[144,1024]{1,0:T(8,128)(2,1)S(1)}, u32[]{:S(2)}, u32[]{:S(2)}) collective-permute-start(bf16[144,1024]{1,0:T(8,128)(2,1)} %get-tuple-element.31), channel_id=1, source_target_pairs={{0,16},{2,18},{4,20},{6,22},{8,24},{10,26},{12,28},{14,30},{16,0},... | collective-permute-start | bytes 884744 | tf_op jit(solution)/shard_map/ppermute | solution.py:372
  16.4 2.5 %collective-permute-start.10 = (bf16[256,768]{1,0:T(8,128)(2,1)S(1)}, bf16[256,768]{1,0:T(8,128)(2,1)S(1)}, u32[]{:S(2)}, u32[]{:S(2)}) collective-permute-start(bf16[256,768]{1,0:T(8,128)(2,1)S(1)} %pad_maximum_fusion.1.w0), channel_id=1, source_target_pairs={{0,6},{2,4},{4,2},{6,0},{8,14},{10,12},{12,10},{14,8},{16,22},{18,... | collective-permute-start | bytes 1179656 | tf_op jit(solution)/shard_map/ppermute | solution.py:81
  20.0 3.4 %collective-permute-start.11 = (bf16[128,256]{1,0:T(8,128)(2,1)S(1)}, bf16[128,256]{1,0:T(8,128)(2,1)S(1)}, u32[]{:S(2)}, u32[]{:S(2)}) collective-permute-start(bf16[128,256]{1,0:T(8,128)(2,1)S(1)} %pad_maximum_fusion.5), channel_id=1, source_target_pairs={{0,16},{2,18},{4,20},{6,22},{8,24},{10,26},{12,28},{14,30},{16,0},... | collective-permute-start | bytes 196616 | tf_op jit(solution)/shard_map/ppermute | solution.py:76
  23.3 8.1 %collective-permute-done.6.far_own.got = bf16[144,1024]{1,0:T(8,128)(2,1)S(1)} collective-permute-done((bf16[144,1024]{1,0:T(8,128)(2,1)}, bf16[144,1024]{1,0:T(8,128)(2,1)S(1)}, u32[]{:S(2)}, u32[]{:S(2)}) %collective-permute-start.6) | collective-permute-done | bytes 294944 | tf_op jit(solution)/shard_map/ppermute | solution.py:372
  33.9 3.1 %collective-permute-done.9.w2 = bf16[256,768]{1,0:T(8,128)(2,1)S(1)} collective-permute-done((bf16[256,768]{1,0:T(8,128)(2,1)S(1)}, bf16[256,768]{1,0:T(8,128)(2,1)S(1)}, u32[]{:S(2)}, u32[]{:S(2)}) %collective-permute-start.9) | collective-permute-done | bytes 393248 | tf_op jit(solution)/shard_map/ppermute | solution.py:81
  38.0 1.7 %collective-permute-start.14 = (bf16[256,256]{1,0:T(8,128)(2,1)S(1)}, bf16[256,256]{1,0:T(8,128)(2,1)S(1)}, u32[]{:S(2)}, u32[]{:S(2)}) collective-permute-start(bf16[256,256]{1,0:T(8,128)(2,1)S(1)} %pad_maximum_fusion.3.w0), channel_id=1, source_target_pairs={{0,6},{2,4},{4,2},{6,0},{8,14},{10,12},{12,10},{14,8},{16,22},{18,... | collective-permute-start | bytes 393224 | tf_op jit(solution)/shard_map/ppermute | solution.py:81
  41.6 5.3 %collective-permute-done.15 = bf16[128,1024]{1,0:T(8,128)(2,1)S(1)} collective-permute-done((bf16[128,1024]{1,0:T(8,128)(2,1)S(1)}, bf16[128,1024]{1,0:T(8,128)(2,1)S(1)}, u32[]{:S(2)}, u32[]{:S(2)}) %collective-permute-start.15) | collective-permute-done | bytes 262176 | tf_op jit(solution)/shard_map/ppermute | solution.py:76
  47.0 2.5 %column_attention.1 = (bf16[256,256]{1,0:T(8,128)(2,1)S(1)}, bf16[256,256]{1,0:T(8,128)(2,1)S(1)}) custom-call(s32[2]{0:T(128)S(1)} %copy-done.8, f32[8]{0:T(128)S(1)} %copy-done.11, bf16[512,1024]{1,0:T(8,128)(2,1)S(1)} %column_normed.1.tokens, bf16[1024,768]{1,0:T(8,128)(2,1)S(1)} %column_project.1.weight), custom_call_target="tpu_custom_call" | custom-call | flops 1024 | bytes 262144 | tf_op jit(solution)/shard_map/column_attention/pallas_call | solution.py:30
  50.7 1.5 %collective-permute-start.20 = (bf16[256,1024]{1,0:T(8,128)(2,1)S(1)}, bf16[256,1024]{1,0:T(8,128)(2,1)S(1)}, u32[]{:S(2)}, u32[]{:S(2)}) collective-permute-start(bf16[256,1024]{1,0:T(8,128)(2,1)S(1)} %pad_maximum_fusion.refs_0_), channel_id=1, source_target_pairs={{0,4},{2,6},{4,0},{6,2},{8,12},{10,14},{12,8},{14,10},{16,20},{18,... | collective-permute-start | bytes 1572872 | tf_op jit(solution)/shard_map/ppermute | solution.py:86
  52.3 1.5 %collective-permute-start.19 = (bf16[256,1024]{1,0:T(8,128)(2,1)S(1)}, bf16[256,1024]{1,0:T(8,128)(2,1)S(1)}, u32[]{:S(2)}, u32[]{:S(2)}) collective-permute-start(bf16[256,1024]{1,0:T(8,128)(2,1)S(1)} %pad_maximum_fusion.refs_0_), channel_id=1, source_target_pairs={{0,2},{2,0},{4,6},{6,4},{8,10},{10,8},{12,14},{14,12},{16,18},{18,... | collective-permute-start | bytes 1572872 | tf_op jit(solution)/shard_map/ppermute | solution.py:86
  53.8 1.8 %row_normed.1 = bf16[256,1024]{1,0:T(8,128)(2,1)} custom-call(bf16[256,256]{1,0:T(8,128)(2,1)S(1)} %get-tuple-element.40.mine, bf16[256,256]{1,0:T(8,128)(2,1)S(1)} %collective-permute-done.16.theirs, bf16[1024,256]{1,0:T(8,128)(2,1)S(1)} %column_output.1.near, bf16[1024,256]{1,0:T(8,128)(2,1)S(1)} %collective-permute-done.17.far, ...), custom_call_target="tpu_custom_call" | custom-call | flops 1024 | bytes 1024 | tf_op jit(solution)/shard_map/row_normed/pallas_call | solution.py:30
  55.6 3.6 %all-to-all-start = ((bf16[16,16,1024]{2,1,0:T(8,128)(2,1)}), bf16[16,16,1024]{2,1,0:T(8,128)(2,1)S(1)}, u32[]{:S(2)}, u32[]{:S(2)}) async-start(bf16[16,16,1024]{2,1,0:T(8,128)(2,1)} %bitcast.6), calls=%async_computation | async-start | bytes 1048576 | tf_op jit(solution)/shard_map/all_to_all | solution.py:439
  59.2 2.8 %collective-permute-start.18 = (bf16[128,512]{1,0:T(8,128)(2,1)S(1)}, bf16[128,512]{1,0:T(8,128)(2,1)S(1)}, u32[]{:S(2)}, u32[]{:S(2)}) collective-permute-start(bf16[128,512]{1,0:T(8,128)(2,1)S(1)} %pad_maximum_fusion.4), channel_id=1, source_target_pairs={{0,16},{2,18},{4,20},{6,22},{8,24},{10,26},{12,28},{14,30},{16,0},... | collective-permute-start | bytes 393224 | tf_op jit(solution)/shard_map/ppermute | solution.py:372
  62.0 5.7 %collective-permute-done.20.refs_2_ = bf16[256,1024]{1,0:T(8,128)(2,1)S(1)} collective-permute-done((bf16[256,1024]{1,0:T(8,128)(2,1)S(1)}, bf16[256,1024]{1,0:T(8,128)(2,1)S(1)}, u32[]{:S(2)}, u32[]{:S(2)}) %collective-permute-start.20) | collective-permute-done | bytes 524320 | tf_op jit(solution)/shard_map/ppermute | solution.py:86
  69.5 2.0 %collective-permute-start.22 = (bf16[128,1024]{1,0:T(8,128)(2,1)S(1)}, bf16[128,1024]{1,0:T(8,128)(2,1)}, u32[]{:S(2)}, u32[]{:S(2)}) collective-permute-start(bf16[128,1024]{1,0:T(8,128)(2,1)S(1)} %slice.18), channel_id=1, source_target_pairs={{0,4},{2,6},{4,0},{6,2},{8,12},{10,14},{12,8},{14,10},{16,20},{18,... | collective-permute-start | bytes 786440 | tf_op jit(solution)/shard_map/ppermute | solution.py:86
  71.5 7.5 %collective-permute-done.18.back = bf16[128,512]{1,0:T(8,128)(2,1)S(1)} collective-permute-done((bf16[128,512]{1,0:T(8,128)(2,1)S(1)}, bf16[128,512]{1,0:T(8,128)(2,1)S(1)}, u32[]{:S(2)}, u32[]{:S(2)}) %collective-permute-start.18) | collective-permute-done | bytes 131104 | tf_op jit(solution)/shard_map/ppermute | solution.py:372
  79.7 2.2 %collective-permute-done.26.refs_8_ = bf16[128,1024]{1,0:T(8,128)(2,1)} collective-permute-done((bf16[128,1024]{1,0:T(8,128)(2,1)S(1)}, bf16[128,1024]{1,0:T(8,128)(2,1)}, u32[]{:S(2)}, u32[]{:S(2)}) %collective-permute-start.26) | collective-permute-done | bytes 262176 | tf_op jit(solution)/shard_map/ppermute | solution.py:23
  82.7 6.8 %row_attention.1 = bf16[256,512]{1,0:T(8,128)(2,1)} custom-call(s32[2]{0:T(128)} %pad_add_fusion.place, f32[8]{0:T(128)} %slopes.3, bf16[256,1024]{1,0:T(8,128)(2,1)} %bitcast.16, bf16[256,1024]{1,0:T(8,128)(2,1)} %copy-done.12, bf16[256,1024]{1,0:T(8,128)(2,1)} %copy-done.14, bf16[256,1024]{1,0:T(8,128)(2,1)} %copy-done.13, bf16[128,1024]{1,0:T(8,128)(2,1)} %copy-done.18, ...), custom_call_target="tpu_custom_call" | custom-call | flops 1024 | bytes 1024 | tf_op jit(solution)/shard_map/row_attention/pallas_call | solution.py:30
  89.5 4.6 %all-to-all-start.1 = ((bf16[16,16,512]{2,1,0:T(8,128)(2,1)}), bf16[16,16,512]{2,1,0:T(8,128)(2,1)S(1)}, u32[]{:S(2)}, u32[]{:S(2)}) async-start(bf16[16,16,512]{2,1,0:T(8,128)(2,1)} %bitcast.17), calls=%async_computation.1 | async-start | bytes 524288 | tf_op jit(solution)/shard_map/all_to_all | solution.py:455
  94.2 5.0 %middle.1 = (f32[256,1024]{1,0:T(8,128)}, bf16[2,1024,256]{2,1,0:T(8,128)(2,1)}) custom-call(s32[2]{0:T(128)} %pad_add_fusion.place, bf16[256,256]{1,0:T(8,128)(2,1)} %copy-done.5, bf16[256,256]{1,0:T(8,128)(2,1)} %copy-done.6, bf16[128,512]{1,0:T(8,128)(2,1)} %copy-done.19, bf16[1024,256]{1,0:T(8,128)(2,1)} %copy-done, bf16[1024,256]{1,0:T(8,128)(2,1)} %copy-done.1, ...), custom_call_target="tpu_custom_call" | custom-call | flops 1024 | bytes 1024 | tf_op jit(solution)/shard_map/middle/pallas_call | solution.py:30
  99.2 5.2 %all-to-all-done.1 = bf16[16,16,512]{2,1,0:T(8,128)(2,1)S(1)} async-done(((bf16[16,16,512]{2,1,0:T(8,128)(2,1)}), bf16[16,16,512]{2,1,0:T(8,128)(2,1)S(1)}, u32[]{:S(2)}, u32[]{:S(2)}) %all-to-all-start.1) | async-done | bytes 262176 | tf_op jit(solution)/shard_map/all_to_all | solution.py:455
  (96 shorter events, 20.5 us)
Async XLA Ops:
  0.0 12.8 %collective-permute-start.1 = (bf16[64,768]{1,0:T(8,128)(2,1)}, bf16[64,768]{1,0:T(8,128)(2,1)S(1)}, u32[]{:S(2)}, u32[]{:S(2)}) collective-permute-start(bf16[64,768]{1,0:T(8,128)(2,1)} %param.18), channel_id=1, source_target_pairs={{0,16},{2,18},{4,20},{6,22},{8,24},{10,26},{12,28},{14,30},{16,0},... | collective-permute-start | bytes 294920 | tf_op jit(solution)/shard_map/ppermute | solution.py:71
  4.0 10.5 %collective-permute-start = (bf16[64,768]{1,0:T(8,128)(2,1)}, bf16[64,768]{1,0:T(8,128)(2,1)S(1)}, u32[]{:S(2)}, u32[]{:S(2)}) collective-permute-start(bf16[64,768]{1,0:T(8,128)(2,1)} %param.18), channel_id=1, source_target_pairs={{0,8},{2,10},{4,12},{6,14},{8,0},{10,2},{12,4},{14,6},{16,24},{18,... | collective-permute-start | bytes 294920 | tf_op jit(solution)/shard_map/ppermute | solution.py:71
  5.6 8.9 %collective-permute-start.2 = (bf16[64,768]{1,0:T(8,128)(2,1)}, bf16[64,768]{1,0:T(8,128)(2,1)S(1)}, u32[]{:S(2)}, u32[]{:S(2)}) collective-permute-start(bf16[64,768]{1,0:T(8,128)(2,1)} %param.18), channel_id=1, source_target_pairs={{0,24},{2,26},{4,28},{6,30},{8,16},{10,18},{12,20},{14,22},{16,8},... | collective-permute-start | bytes 294920 | tf_op jit(solution)/shard_map/ppermute | solution.py:71
  5.6 6.4 %collective-permute-start.3 = (bf16[64,256]{1,0:T(8,128)(2,1)}, bf16[64,256]{1,0:T(8,128)(2,1)S(1)}, u32[]{:S(2)}, u32[]{:S(2)}) collective-permute-start(bf16[64,256]{1,0:T(8,128)(2,1)} %param.19), channel_id=1, source_target_pairs={{0,8},{2,10},{4,12},{6,14},{8,0},{10,2},{12,4},{14,6},{16,24},{18,... | collective-permute-start | bytes 98312 | tf_op jit(solution)/shard_map/ppermute | solution.py:76
  10.1 5.4 %collective-permute-start.4 = (bf16[64,1024]{1,0:T(8,128)(2,1)}, bf16[64,1024]{1,0:T(8,128)(2,1)S(1)}, u32[]{:S(2)}, u32[]{:S(2)}) collective-permute-start(bf16[64,1024]{1,0:T(8,128)(2,1)} %get-tuple-element.29), channel_id=1, source_target_pairs={{0,8},{2,10},{4,12},{6,14},{8,0},{10,2},{12,4},{14,6},{16,24},{18,... | collective-permute-start | bytes 393224 | tf_op jit(solution)/shard_map/ppermute | solution.py:76
  12.0 4.4 %collective-permute-start.5 = (bf16[144,1024]{1,0:T(8,128)(2,1)}, bf16[144,1024]{1,0:T(8,128)(2,1)S(1)}, u32[]{:S(2)}, u32[]{:S(2)}) collective-permute-start(bf16[144,1024]{1,0:T(8,128)(2,1)} %get-tuple-element.28.own.kept), channel_id=1, source_target_pairs={{0,1},{1,0},{2,3},{3,2},{4,5},{5,4},{6,7},{7,6},{8,9},{9,8},{10,11... | collective-permute-start | bytes 884744 | tf_op jit(solution)/shard_map/ppermute | solution.py:23
  12.8 18.6 %collective-permute-start.6 = (bf16[144,1024]{1,0:T(8,128)(2,1)}, bf16[144,1024]{1,0:T(8,128)(2,1)S(1)}, u32[]{:S(2)}, u32[]{:S(2)}) collective-permute-start(bf16[144,1024]{1,0:T(8,128)(2,1)} %get-tuple-element.31), channel_id=1, source_target_pairs={{0,16},{2,18},{4,20},{6,22},{8,24},{10,26},{12,28},{14,30},{16,0},... | collective-permute-start | bytes 884744 | tf_op jit(solution)/shard_map/ppermute | solution.py:372
  16.4 17.5 %collective-permute-start.10 = (bf16[256,768]{1,0:T(8,128)(2,1)S(1)}, bf16[256,768]{1,0:T(8,128)(2,1)S(1)}, u32[]{:S(2)}, u32[]{:S(2)}) collective-permute-start(bf16[256,768]{1,0:T(8,128)(2,1)S(1)} %pad_maximum_fusion.1.w0), channel_id=1, source_target_pairs={{0,6},{2,4},{4,2},{6,0},{8,14},{10,12},{12,10},{14,8},{16,22},{18,... | collective-permute-start | bytes 1179656 | tf_op jit(solution)/shard_map/ppermute | solution.py:81
  18.9 18.1 %collective-permute-start.9 = (bf16[256,768]{1,0:T(8,128)(2,1)S(1)}, bf16[256,768]{1,0:T(8,128)(2,1)S(1)}, u32[]{:S(2)}, u32[]{:S(2)}) collective-permute-start(bf16[256,768]{1,0:T(8,128)(2,1)S(1)} %pad_maximum_fusion.1.w0), channel_id=1, source_target_pairs={{0,4},{2,6},{4,0},{6,2},{8,12},{10,14},{12,8},{14,10},{16,20},{18,... | collective-permute-start | bytes 1179656 | tf_op jit(solution)/shard_map/ppermute | solution.py:81
  19.4 17.7 %collective-permute-start.8 = (bf16[256,768]{1,0:T(8,128)(2,1)S(1)}, bf16[256,768]{1,0:T(8,128)(2,1)S(1)}, u32[]{:S(2)}, u32[]{:S(2)}) collective-permute-start(bf16[256,768]{1,0:T(8,128)(2,1)S(1)} %pad_maximum_fusion.1.w0), channel_id=1, source_target_pairs={{0,2},{2,0},{4,6},{6,4},{8,10},{10,8},{12,14},{14,12},{16,18},{18,... | collective-permute-start | bytes 1179656 | tf_op jit(solution)/shard_map/ppermute | solution.py:81
  20.0 12.5 %collective-permute-start.11 = (bf16[128,256]{1,0:T(8,128)(2,1)S(1)}, bf16[128,256]{1,0:T(8,128)(2,1)S(1)}, u32[]{:S(2)}, u32[]{:S(2)}) collective-permute-start(bf16[128,256]{1,0:T(8,128)(2,1)S(1)} %pad_maximum_fusion.5), channel_id=1, source_target_pairs={{0,16},{2,18},{4,20},{6,22},{8,24},{10,26},{12,28},{14,30},{16,0},... | collective-permute-start | bytes 196616 | tf_op jit(solution)/shard_map/ppermute | solution.py:76
  32.5 14.5 %collective-permute-start.15 = (bf16[128,1024]{1,0:T(8,128)(2,1)S(1)}, bf16[128,1024]{1,0:T(8,128)(2,1)S(1)}, u32[]{:S(2)}, u32[]{:S(2)}) collective-permute-start(bf16[128,1024]{1,0:T(8,128)(2,1)S(1)} %pad_maximum_fusion.2), channel_id=1, source_target_pairs={{0,16},{2,18},{4,20},{6,22},{8,24},{10,26},{12,28},{14,30},{16,0},... | collective-permute-start | bytes 786440 | tf_op jit(solution)/shard_map/ppermute | solution.py:76
  38.0 11.5 %collective-permute-start.14 = (bf16[256,256]{1,0:T(8,128)(2,1)S(1)}, bf16[256,256]{1,0:T(8,128)(2,1)S(1)}, u32[]{:S(2)}, u32[]{:S(2)}) collective-permute-start(bf16[256,256]{1,0:T(8,128)(2,1)S(1)} %pad_maximum_fusion.3.w0), channel_id=1, source_target_pairs={{0,6},{2,4},{4,2},{6,0},{8,14},{10,12},{12,10},{14,8},{16,22},{18,... | collective-permute-start | bytes 393224 | tf_op jit(solution)/shard_map/ppermute | solution.py:81
  39.8 9.8 %collective-permute-start.13 = (bf16[256,256]{1,0:T(8,128)(2,1)S(1)}, bf16[256,256]{1,0:T(8,128)(2,1)S(1)}, u32[]{:S(2)}, u32[]{:S(2)}) collective-permute-start(bf16[256,256]{1,0:T(8,128)(2,1)S(1)} %pad_maximum_fusion.3.w0), channel_id=1, source_target_pairs={{0,4},{2,6},{4,0},{6,2},{8,12},{10,14},{12,8},{14,10},{16,20},{18,... | collective-permute-start | bytes 393224 | tf_op jit(solution)/shard_map/ppermute | solution.py:81
  41.1 8.5 %collective-permute-start.12 = (bf16[256,256]{1,0:T(8,128)(2,1)S(1)}, bf16[256,256]{1,0:T(8,128)(2,1)S(1)}, u32[]{:S(2)}, u32[]{:S(2)}) collective-permute-start(bf16[256,256]{1,0:T(8,128)(2,1)S(1)} %pad_maximum_fusion.3.w0), channel_id=1, source_target_pairs={{0,2},{2,0},{4,6},{6,4},{8,10},{10,8},{12,14},{14,12},{16,18},{18,... | collective-permute-start | bytes 393224 | tf_op jit(solution)/shard_map/ppermute | solution.py:81
  50.7 17.0 %collective-permute-start.20 = (bf16[256,1024]{1,0:T(8,128)(2,1)S(1)}, bf16[256,1024]{1,0:T(8,128)(2,1)S(1)}, u32[]{:S(2)}, u32[]{:S(2)}) collective-permute-start(bf16[256,1024]{1,0:T(8,128)(2,1)S(1)} %pad_maximum_fusion.refs_0_), channel_id=1, source_target_pairs={{0,4},{2,6},{4,0},{6,2},{8,12},{10,14},{12,8},{14,10},{16,20},{18,... | collective-permute-start | bytes 1572872 | tf_op jit(solution)/shard_map/ppermute | solution.py:86
  52.3 17.2 %collective-permute-start.19 = (bf16[256,1024]{1,0:T(8,128)(2,1)S(1)}, bf16[256,1024]{1,0:T(8,128)(2,1)S(1)}, u32[]{:S(2)}, u32[]{:S(2)}) collective-permute-start(bf16[256,1024]{1,0:T(8,128)(2,1)S(1)} %pad_maximum_fusion.refs_0_), channel_id=1, source_target_pairs={{0,2},{2,0},{4,6},{6,4},{8,10},{10,8},{12,14},{14,12},{16,18},{18,... | collective-permute-start | bytes 1572872 | tf_op jit(solution)/shard_map/ppermute | solution.py:86
  55.6 24.1 %all-to-all-start = ((bf16[16,16,1024]{2,1,0:T(8,128)(2,1)}), bf16[16,16,1024]{2,1,0:T(8,128)(2,1)S(1)}, u32[]{:S(2)}, u32[]{:S(2)}) async-start(bf16[16,16,1024]{2,1,0:T(8,128)(2,1)} %bitcast.6), calls=%async_computation | async-start | bytes 1048576 | tf_op jit(solution)/shard_map/all_to_all | solution.py:439
  59.2 19.8 %collective-permute-start.18 = (bf16[128,512]{1,0:T(8,128)(2,1)S(1)}, bf16[128,512]{1,0:T(8,128)(2,1)S(1)}, u32[]{:S(2)}, u32[]{:S(2)}) collective-permute-start(bf16[128,512]{1,0:T(8,128)(2,1)S(1)} %pad_maximum_fusion.4), channel_id=1, source_target_pairs={{0,16},{2,18},{4,20},{6,22},{8,24},{10,26},{12,28},{14,30},{16,0},... | collective-permute-start | bytes 393224 | tf_op jit(solution)/shard_map/ppermute | solution.py:372
  62.0 17.6 %collective-permute-start.23 = (bf16[256,1024]{1,0:T(8,128)(2,1)S(1)}, bf16[256,1024]{1,0:T(8,128)(2,1)S(1)}, u32[]{:S(2)}, u32[]{:S(2)}) collective-permute-start(bf16[256,1024]{1,0:T(8,128)(2,1)S(1)} %pad_maximum_fusion.refs_0_), channel_id=1, source_target_pairs={{0,1},{1,0},{2,3},{3,2},{4,5},{5,4},{6,7},{7,6},{8,9},{9,8},{10,11... | collective-permute-start | bytes 1572872 | tf_op jit(solution)/shard_map/ppermute | solution.py:23
  67.8 11.3 %collective-permute-start.21 = (bf16[128,1024]{1,0:T(8,128)(2,1)S(1)}, bf16[128,1024]{1,0:T(8,128)(2,1)S(1)}, u32[]{:S(2)}, u32[]{:S(2)}) collective-permute-start(bf16[128,1024]{1,0:T(8,128)(2,1)S(1)} %slice.17), channel_id=1, source_target_pairs={{0,2},{2,0},{4,6},{6,4},{8,10},{10,8},{12,14},{14,12},{16,18},{18,... | collective-permute-start | bytes 786440 | tf_op jit(solution)/shard_map/ppermute | solution.py:86
  69.5 10.1 %collective-permute-start.22 = (bf16[128,1024]{1,0:T(8,128)(2,1)S(1)}, bf16[128,1024]{1,0:T(8,128)(2,1)}, u32[]{:S(2)}, u32[]{:S(2)}) collective-permute-start(bf16[128,1024]{1,0:T(8,128)(2,1)S(1)} %slice.18), channel_id=1, source_target_pairs={{0,4},{2,6},{4,0},{6,2},{8,12},{10,14},{12,8},{14,10},{16,20},{18,... | collective-permute-start | bytes 786440 | tf_op jit(solution)/shard_map/ppermute | solution.py:86
  71.5 10.3 %collective-permute-start.25 = (bf16[256,1024]{1,0:T(8,128)(2,1)S(1)}, bf16[256,1024]{1,0:T(8,128)(2,1)S(1)}, u32[]{:S(2)}, u32[]{:S(2)}) collective-permute-start(bf16[256,1024]{1,0:T(8,128)(2,1)S(1)} %collective-permute-done.20.refs_2_), channel_id=1, source_target_pairs={{0,1},{1,0},{2,3},{3,2},{4,5},{5,4},{6,7},{7,6},{8,9},{9,8},{10,11... | collective-permute-start | bytes 1572872 | tf_op jit(solution)/shard_map/ppermute | solution.py:23
  89.5 14.8 %all-to-all-start.1 = ((bf16[16,16,512]{2,1,0:T(8,128)(2,1)}), bf16[16,16,512]{2,1,0:T(8,128)(2,1)S(1)}, u32[]{:S(2)}, u32[]{:S(2)}) async-start(bf16[16,16,512]{2,1,0:T(8,128)(2,1)} %bitcast.17), calls=%async_computation.1 | async-start | bytes 524288 | tf_op jit(solution)/shard_map/all_to_all | solution.py:455
  (26 other events, 238.1 us)

commit v4 on v3

--- a/solution.py
+++ b/solution.py
@@ -13,6 +13,7 @@
 PLANE = 4
 NEVER = -1e30
 EXTRA = 16
+CHUNKS = 4
 
 
 def at(place, length):
@@ -26,7 +27,18 @@
 SCALARS = pl.BlockSpec(memory_space=pltpu.SMEM)
 
 
-def call(kernel, out, name, scalars, arrays, given=(), scratch=(), cost=2**10, room=24, space=pltpu.VMEM):
+def call(
+    kernel,
+    out,
+    name,
+    arrays=(),
+    scalars=(),
+    given=(),
+    scratch=(),
+    cost=2**10,
+    room=24,
+    space=pltpu.VMEM,
+):
     return pl.pallas_call(
         kernel,
         out_shape=out,
@@ -41,6 +53,10 @@
     )(*scalars, *arrays, *given)
 
 
+def own_place():
+    return lax.axis_index("lon"), lax.axis_index("lat")
+
+
 def dot(a, b):
     return jnp.dot(a, b, preferred_element_type=jnp.float32)
 
@@ -67,14 +83,13 @@
 
 def along_lines(weight, length):
     steps = range(PLANE, length, PLANE)
-    return jnp.concatenate(
-        [weight] + [lax.ppermute(weight, "lon", at(lambda i: i ^ k, length)) for k in steps], axis=0
-    )
+    return [lax.ppermute(weight, "lon", at(lambda i: i ^ k, length)) for k in steps]
 
 
 def doubled(weight, step, length):
     got = lax.ppermute(weight, "lon", at(lambda i: i ^ step, length))
-    return jnp.concatenate([weight, got], axis=0)
+    half = weight.shape[0] // 2
+    return jnp.concatenate([weight[:half], got[:half], weight[half:], got[half:]], axis=0)
 
 
 def across_plane(part, length):
@@ -105,7 +120,8 @@
         yield piece, slice(k * shard, (k + 1) * shard), there
 
 
-def order_kernel(shard, sort, place, w0, w1, w2, w3, out):
+def order_kernel(shard, sort, w0, w1, w2, w3, out):
+    place = own_place()
     for piece, here, there in places(shard, place, (w0, w1, w2, w3)):
         out[there, :] = by_kind(piece[here, :]) if sort else piece[here, :]
 
@@ -152,7 +168,8 @@
     return (grid == lax.rem(spot, rows) * cols + column).astype(jnp.bfloat16)
 
 
-def first_kernel(lons, place, tokens, mask, project, output, keep, send, packed, *scratch):
+def first_kernel(lons, tokens, mask, project, output, keep, send, packed, *scratch):
+    place = own_place()
     *held, sems = scratch
     coming = bring(zip((tokens, mask, project, output), held), sems)
     tokens, mask, project, output = held
@@ -177,9 +194,9 @@
     packed[:, split:] = output[...]
 
 
-def column_norm_kernel(own, other, far_own, far_other, embed, gain, out):
+def column_norm_kernel(own, other, embed, gain, out):
     half = own.shape[0] - EXTRA
-    for k, ref in enumerate((own, other, far_own, far_other)):
+    for k, ref in enumerate((own, other)):
         normed = norm(packed_start(ref[...], embed[...]), gain[...])
         out[k * half : (k + 1) * half, :] = normed.astype(jnp.bfloat16)
 
@@ -203,14 +220,17 @@
     return jnp.where(first, mixed[:rows], mixed[rows:]).astype(jnp.bfloat16)
 
 
-def column_kernel(band, place, slopes, tokens, weight, out_own, out_other, qkv):
-    block = tokens.shape[0] // 4
+def column_kernel(band, slopes, tokens, far_tokens, weight, out_own, out_other, qkv):
+    place = own_place()
+    block = tokens.shape[0] // 2
     loops = block // band
     width = weight.shape[1] // 3
-    projected = dot(tokens[...], weight[...])
-    qkv[:, :width] = unit_heads(projected[:, :width], 1.0 / math.sqrt(HS))
-    qkv[:, width : 2 * width] = unit_heads(projected[:, width : 2 * width])
-    qkv[:, 2 * width :] = projected[:, 2 * width :].astype(jnp.bfloat16)
+    for half, ref in enumerate((tokens, far_tokens)):
+        projected = dot(ref[...], weight[...])
+        at_rows = slice(half * 2 * block, (half + 1) * 2 * block)
+        qkv[at_rows, :width] = unit_heads(projected[:, :width], 1.0 / math.sqrt(HS))
+        qkv[at_rows, width : 2 * width] = unit_heads(projected[:, width : 2 * width])
+        qkv[at_rows, 2 * width :] = projected[:, 2 * width :].astype(jnp.bfloat16)
     total = 2 * band
     shape = (2 * total, 2 * total)
     spot_q, spot_k = iota(shape, 0), iota(shape, 1)
@@ -254,7 +274,8 @@
     out[...] = dot(by_row, normed).astype(jnp.bfloat16)
 
 
-def home_kernel(shard, lons, place, mine, theirs, back, near, far, *refs):
+def home_kernel(shard, lons, mine, theirs, back, near, far, *refs):
+    place = own_place()
     pieces, (tokens, mask, embed, out, out_weight, *held, weight_sems, sems) = refs[:-10], refs[-10:]
     lane = pieces[0].shape[1] - out_weight.shape[2]
     coming = bring(zip((tokens, mask, embed), held), sems)
@@ -277,14 +298,16 @@
     wait(later)
 
 
-def row_kernel(shard, cols, rows, place, slopes, tokens, *refs):
-    pieces, (out, weight, sems) = refs[:-3], refs[-3:]
-    coming = [
-        bring_in_order(
-            shard, place, pieces[half * len(pieces) // 2 : (half + 1) * len(pieces) // 2], 0, weight.at[half], sems.at[half]
-        )
-        for half in range(2)
-    ]
+def row_kernel(shard, cols, rows, slopes, spread, *refs):
+    place = own_place()
+    pieces, (out, tokens, weight, sems, token_sem) = refs[:-5], refs[-5:]
+    count = len(pieces) // 2
+    fetch = lambda half: bring_in_order(
+        shard, place, pieces[half * count : (half + 1) * count], 0, weight.at[half], sems.at[half]
+    )
+    first_copy = bring([(spread, tokens)], token_sem)
+    coming = fetch(0)
+    wait(first_copy)
     total = tokens.shape[0]
     block = cols * rows
     lon_count = total // block
@@ -311,7 +334,9 @@
     heads = width // HS
     for half in range(2):
         first = lax.rem(place[1] + half, 2) * heads
-        wait(coming[half])
+        wait(coming)
+        if half == 0:
+            coming = fetch(1)
         projected = dot(tokens[...], weight[half])
         query = unit_heads(projected[:, :width], 1.0 / math.sqrt(HS))
         keyed = unit_heads(projected[:, width : 2 * width])
@@ -330,10 +355,27 @@
             out[:, start : start + PAIR] = dot(homeward, mixed).astype(jnp.bfloat16)
 
 
-def final_kernel(middle, mixed, weight, out):
-    width = weight.shape[2]
-    update = dot_t(mixed[:, :width], weight[0]) + dot_t(mixed[:, width:], weight[1])
-    out[...] = (middle[...] + update).reshape(out.shape).astype(jnp.bfloat16)
+def final_kernel(mixed, middle, weight, out, mixed_held, total, held, staged, sems, out_sems):
+    width = held.shape[2]
+    step = total.shape[1] // CHUNKS
+    cut = [slice(i * step, (i + 1) * step) for i in range(CHUNKS)]
+    pairs = [(mixed, mixed_held)]
+    for at_cols in cut:
+        pairs += [(weight.at[half, at_cols, :], held.at[half, at_cols, :]) for half in range(2)]
+        pairs += [(middle.at[:, at_cols], total.at[:, at_cols])]
+    coming = bring(pairs, sems)
+    coming[0].wait()
+    going = []
+    for i, at_cols in enumerate(cut):
+        wait(coming[1 + 3 * i : 4 + 3 * i])
+        update = total[:, at_cols]
+        for half in range(2):
+            update += dot_t(mixed_held[:, half * width : (half + 1) * width], held[half, at_cols, :])
+        staged[:, :, at_cols] = update.reshape(*out.shape[:2], step).astype(jnp.bfloat16)
+        copy = pltpu.make_async_copy(staged.at[:, :, at_cols], out.at[:, :, at_cols], out_sems.at[i])
+        copy.start()
+        going.append(copy)
+    wait(going)
 
 
 def fast(
@@ -350,122 +392,122 @@
     row_output,
 ):
     lon_count = lax.axis_size("lon")
-    lat = lax.axis_index("lat")
-    lon = lax.axis_index("lon")
     band, cols, width = fields.shape
     tokens = band * cols
-    heads = column_slopes.shape[0]
-    half = heads // 2
-    attend = half * HS
+    attend = column_slopes.shape[0] // 2 * HS
     shard = column_project.shape[0]
-    place = jnp.stack([lon, lat]).astype(jnp.int32)
     embed, column_gain, row_gain = (v.reshape(1, width) for v in (land_embed, column_gain, row_gain))
+    mask = land_mask.T
     bf16 = lambda *shape: jax.ShapeDtypeStruct(shape, jnp.bfloat16)
     f32 = lambda *shape: jax.ShapeDtypeStruct(shape, jnp.float32)
-    rows = shard * lon_count
-    weights = (bf16(rows, 3 * attend), bf16(rows, attend))
-
-    order = lambda pieces, name, sort, out: call(
-        functools.partial(order_kernel, shard, sort), out, name, (place,), pieces
-    )
-    project_shape, output_shape = weights
+    vmem = lambda *arrays: [pltpu.VMEM(v.shape, v.dtype) for v in arrays]
+    sems = lambda *shape: [pltpu.SemaphoreType.DMA(shape)]
+    after = lax.optimization_barrier
+    project_shape = bf16(shard * lon_count, 3 * attend)
+    output_shape = bf16(shard * lon_count, attend)
     antipode = lambda value: lax.ppermute(
         value, "lon", at(lambda i: (i + lon_count // 2) % lon_count, lon_count)
     )
+    two_lines = lambda value: lax.ppermute(value, "lon", at(lambda i: i ^ (2 * PLANE), lon_count))
+
+    given = (fields, mask, row_project, row_output)
     packed = bf16(tokens // 2 + EXTRA, width)
-    mask = land_mask.T
-
-    first = along_lines(column_project, lon_count)
-    third = bf16(shard, row_project.shape[1] + row_output.shape[1])
-    given = (fields, mask, row_project, row_output)
-    keep, send, third = call(
+    keep, send, row_weights = call(
         functools.partial(first_kernel, lon_count),
-        (packed, packed, third),
+        (packed, packed, bf16(shard, 4 * attend)),
         "loop_tokens",
-        (place,),
-        (),
-        given,
-        [pltpu.VMEM(v.shape, v.dtype) for v in given] + [pltpu.SemaphoreType.DMA((4,))],
+        given=given,
+        scratch=vmem(*given) + sems(4),
         room=60,
     )
-    second = column_output
-    if lon_count > PLANE:
-        second = doubled(second, PLANE, lon_count)
-        third = doubled(third, PLANE, lon_count)
+    lines = along_lines(column_project, lon_count)
+    output_got, row_got = two_lines(column_output), two_lines(row_weights)
     keep_other = swap_bands(keep)
+    *lines, send = after((*lines, send))
     far = antipode(send)
-    first, second, third, keep_other = lax.optimization_barrier((first, second, third, keep_other))
-    pieces = across_plane(first, lon_count)
-    if lon_count > 2 * PLANE:
-        second = doubled(second, 2 * PLANE, lon_count)
+    project = jnp.concatenate([column_project, *lines], axis=0)
+    output = jnp.concatenate([column_output, output_got], axis=0)
+    row_weights = jnp.concatenate([row_weights, row_got], axis=0)
+    project, keep_other = after((project, keep_other))
+    project = across_plane(project, lon_count)
+    output = doubled(output, PLANE, lon_count)
     far_other = swap_bands(far)
-    normed = call(
-        column_norm_kernel,
-        bf16(2 * tokens, width),
-        "column_normed",
-        (),
-        (keep, keep_other, far, far_other, embed, column_gain),
-    )
-    project = order(pieces, "column_project", True, project_shape)
-    normed, project, second = lax.optimization_barrier((normed, project, second))
-    third, _ = lax.optimization_barrier((third, far))
-    second = across_plane(second, lon_count)
-    if lon_count > 2 * PLANE:
-        third = doubled(third, 2 * PLANE, lon_count)
-
+
+    column_normed = lambda own, other, name: call(
+        column_norm_kernel, bf16(tokens, width), name, (own, other, embed, column_gain)
+    )
+    kept_normed = column_normed(keep, keep_other, "column_normed")
+    far_normed = column_normed(far, far_other, "far_normed")
+    project = call(
+        functools.partial(order_kernel, shard, True), project_shape, "column_project", project
+    )
+    far_normed, project, output = after((far_normed, project, output))
+    row_weights, _ = after((row_weights, far))
+    output = across_plane(output, lon_count)
+    row_weights = doubled(row_weights, PLANE, lon_count)
     mixed_own, mixed_other = call(
         functools.partial(column_kernel, band),
         (bf16(tokens, attend), bf16(tokens, attend)),
         "column_attention",
-        (place, column_slopes),
-        (normed, project),
-        (),
-        [pltpu.VMEM((2 * tokens, 3 * attend), jnp.bfloat16)],
-        cost=1 * 2**18,
+        (kept_normed, far_normed, project),
+        scalars=(column_slopes,),
+        scratch=[pltpu.VMEM((2 * tokens, 3 * attend), jnp.bfloat16)],
+        cost=2**18,
     )
     theirs = swap_bands(mixed_other)
-    second, third, mixed_own = lax.optimization_barrier((second, third, mixed_own))
-    output = order(second, "column_output", False, output_shape)
+    output, row_weights, mixed_own = after((output, row_weights, mixed_own))
+    output = call(functools.partial(order_kernel, shard, False), output_shape, "column_output", output)
     output_far = swap_bands(output)
-    third, late = relayed_plane(third, lon_count)
+
     to_home = jnp.concatenate([mixed_own[tokens // 2 :], theirs[tokens // 2 :]], axis=1)
+    row_weights, late = relayed_plane(row_weights, lon_count)
     row_normed = call(
         functools.partial(middle_kernel, cols),
         bf16(tokens, width),
         "row_normed",
-        (),
         (mixed_own, theirs, output, output_far, keep, far, embed, row_gain),
     )
     spread = lax.all_to_all(row_normed, "lon", split_axis=0, concat_axis=0, tiled=True)
+    to_home, row_weights = after((to_home, row_weights))
     home = antipode(to_home)
-    third = third + late
-    third_far = [swap_bands(piece) for piece in third]
-    spread, home = lax.optimization_barrier((spread, home))
-    sems = pltpu.SemaphoreType.DMA((2, lon_count))
+    row_weights = row_weights + late
+    row_weights += [swap_bands(piece) for piece in row_weights]
+
     row_mixed = call(
         functools.partial(row_kernel, shard, cols, band // lon_count),
         bf16(tokens, 2 * attend),
         "row_attention",
-        (place, row_slopes),
-        (spread,),
-        (*third, *third_far),
-        [pltpu.VMEM((2, *project_shape.shape), jnp.bfloat16), sems],
+        scalars=(row_slopes,),
+        given=(spread, *row_weights),
+        scratch=vmem(spread.reshape(tokens, width))
+        + [pltpu.VMEM((2, *project_shape.shape), jnp.bfloat16)]
+        + sems(2, lon_count)
+        + sems(1),
         room=60,
     )
+    row_mixed, home = after((row_mixed, home))
     back = lax.all_to_all(row_mixed, "lon", split_axis=0, concat_axis=0, tiled=True)
-    given = (*third, *third_far, fields, mask, embed)
+    given = (fields, mask, embed)
     middle, row_out = call(
         functools.partial(home_kernel, shard, lon_count),
         (f32(tokens, width), bf16(2, *output_shape.shape)),
         "middle",
-        (place,),
         (mixed_own, theirs, home, output, output_far),
-        given,
-        [pltpu.VMEM(v.shape, v.dtype) for v in given[-3:]] + [sems, pltpu.SemaphoreType.DMA((3,))],
+        given=(*row_weights, *given),
+        scratch=vmem(*given) + sems(2, lon_count) + sems(3),
         room=56,
     )
     return call(
-        final_kernel, bf16(band, cols, width), "block_output", (), (middle, back, row_out)
+        final_kernel,
+        bf16(band, cols, width),
+        "block_output",
+        given=(back, middle, row_out),
+        scratch=vmem(back, middle, row_out)
+        + [pltpu.VMEM(fields.shape, jnp.bfloat16)]
+        + sems(1 + 3 * CHUNKS)
+        + sems(CHUNKS),
+        room=60,
+        space=pltpu.HBM,
     )
 
 
@@ -617,7 +659,7 @@
 
     def shards(fields, *rest):
         length = lax.axis_size("lon")
-        suits = fields.shape[0] % length == 0 and length in (2 * PLANE, 4 * PLANE)
+        suits = fields.shape[0] % length == 0 and length == 4 * PLANE
         return (fast if suits else general)(fields, *rest)
 
     return jax.shard_map(shards, mesh=mesh, in_specs=in_specs, out_specs=out_specs, check_vma=False)

time: 109 us -> 106 us (0.972)
  starting transfers between devices: 38.3 us -> 37 us
  local copies, waits for them, and re-layouts: 3.13 us -> 1.87 us
    ppermute x2, waiting for transfers between devices: 15.7 us -> 5.4 us  [fast(): lax.ppermute(value, 'lon', at(lambda i: (i + lon_count // 2) % lon_count,...]
    ppermute x4, waiting for transfers between devices: 6.19 us -> 16.2 us  [relayed_plane(): lax.ppermute(value, 'lon', at(lambda i: i ^ k, length))]
    ppermute x0 -> x2, waiting for transfers between devices: none -> 7.37 us  [fast(): lax.ppermute(value, 'lon', at(lambda i: i ^ 2 * PLANE, lon_count))]
    ppermute x0 -> x2, starting transfers between devices: none -> 6.45 us  [fast(): lax.ppermute(value, 'lon', at(lambda i: i ^ 2 * PLANE, lon_count))]
    ppermute x4 -> x2, waiting for transfers between devices: 7.09 us -> 1.16 us  [doubled(): got = lax.ppermute(weight, 'lon', at(lambda i: i ^ step, length))]
    ppermute x4 -> x2, starting transfers between devices: 5.45 us -> 0.68 us  [doubled(): got = lax.ppermute(weight, 'lon', at(lambda i: i ^ step, length))]
    unnamed x40 -> x42, local copies, waits for them, and re-layouts: 3.09 us -> 1.78 us
    ppermute x4, starting transfers between devices: 6.23 us -> 4.97 us  [relayed_plane(): lax.ppermute(value, 'lon', at(lambda i: i ^ k, length))]
  transfers between devices with their start and end apart: 30 -> 30, of which waited for: 13 -> 14; matrix products, arithmetic and copies ran while one was open for 3% -> 3% of each run, Pallas kernels for 13% -> 18%
where the time goes in v4:
time: 106 us; the launch traced here: 105 us
  waiting for transfers between devices  40.9 us (39%)
  starting transfers between devices  37 us (35%)
  Pallas kernels  22.6 us (21%)
  other arithmetic  2.67 us (3%)
  local copies, waits for them, and re-layouts  1.87 us (2%)
    pallas_call x10, Pallas kernels, call(): pl.pallas_call(kernel, out_shape=out, in_specs=[SCALARS] * len(scalars) +...  22.6 us
    ppermute x4, waiting for transfers between devices, relayed_plane(): lax.ppermute(value, 'lon', at(lambda i: i ^ k, length))  16.2 us
    ppermute x2, waiting for transfers between devices, fast(): lax.ppermute(value, 'lon', at(lambda i: i ^ 2 * PLANE, lon_count))  7.37 us
    ppermute x6, starting transfers between devices, across_plane(): lax.ppermute(part, 'lon', at(lambda i: i ^ k, length))  7.11 us
    ppermute x2, starting transfers between devices, fast(): lax.ppermute(value, 'lon', at(lambda i: i ^ 2 * PLANE, lon_count))  6.45 us
    ppermute x2, waiting for transfers between devices, fast(): lax.ppermute(value, 'lon', at(lambda i: (i + lon_count // 2) % lon_count,...  5.4 us
    all_to_all x1, waiting for transfers between devices, fast(): lax.all_to_all(row_mixed, 'lon', split_axis=0, concat_axis=0, tiled=True)  5.03 us
    ppermute x4, starting transfers between devices, relayed_plane(): lax.ppermute(value, 'lon', at(lambda i: i ^ k, length))  4.97 us
  transfers between devices with their start and end apart: 30, of which 14 were waited for; matrix products, arithmetic and copies ran while one was open for 3% of the time, Pallas kernels for 18%

profile of v4, /device:TPU:0, one launch (start us, length us, event | category | flops | bytes accessed | tf_op | source)
XLA Modules:
  0.0 105.4 jit_solution(10475920429400115973)
XLA Ops:
  0.0 4.1 %collective-permute-start.9 = (bf16[64,256]{1,0:T(8,128)(2,1)}, bf16[64,256]{1,0:T(8,128)(2,1)S(1)}, u32[]{:S(2)}, u32[]{:S(2)}) collective-permute-start(bf16[64,256]{1,0:T(8,128)(2,1)} %param.19), channel_id=1, source_target_pairs={{0,16},{2,18},{4,20},{6,22},{8,24},{10,26},{12,28},{14,30},{16,0},... | collective-permute-start | bytes 98312 | tf_op jit(solution)/shard_map/ppermute | solution.py:411
  4.1 1.6 %collective-permute-start = (bf16[64,768]{1,0:T(8,128)(2,1)}, bf16[64,768]{1,0:T(8,128)(2,1)S(1)}, u32[]{:S(2)}, u32[]{:S(2)}) collective-permute-start(bf16[64,768]{1,0:T(8,128)(2,1)} %param.18), channel_id=1, source_target_pairs={{0,8},{2,10},{4,12},{6,14},{8,0},{10,2},{12,4},{14,6},{16,24},{18,... | collective-permute-start | bytes 294920 | tf_op jit(solution)/shard_map/ppermute | solution.py:86
  6.0 2.5 %collective-permute-start.2 = (bf16[64,768]{1,0:T(8,128)(2,1)}, bf16[64,768]{1,0:T(8,128)(2,1)S(1)}, u32[]{:S(2)}, u32[]{:S(2)}) collective-permute-start(bf16[64,768]{1,0:T(8,128)(2,1)} %param.18), channel_id=1, source_target_pairs={{0,24},{2,26},{4,28},{6,30},{8,16},{10,18},{12,20},{14,22},{16,8},... | collective-permute-start | bytes 294920 | tf_op jit(solution)/shard_map/ppermute | solution.py:86
  9.9 2.2 %loop_tokens.1 = (bf16[144,1024]{1,0:T(8,128)(2,1)}, bf16[144,1024]{1,0:T(8,128)(2,1)}, bf16[64,1024]{1,0:T(8,128)(2,1)}) custom-call(bf16[64,4,1024]{2,1,0:T(4,128)(2,1)} %refs_10_.1, s32[4,64]{1,0:T(4,128)} %bitcast.17, bf16[64,768]{1,0:T(8,128)(2,1)} %project.1, bf16[64,256]{1,0:T(8,128)(2,1)} %output.1), custom_call_target="tpu_custom_call" | custom-call | flops 1024 | bytes 1024 | tf_op jit(solution)/shard_map/loop_tokens/pallas_call | solution.py:42
  12.3 2.3 %collective-permute-start.14 = (bf16[64,1024]{1,0:T(8,128)(2,1)}, bf16[64,1024]{1,0:T(8,128)(2,1)S(1)}, u32[]{:S(2)}, u32[]{:S(2)}) collective-permute-start(bf16[64,1024]{1,0:T(8,128)(2,1)} %get-tuple-element.42), channel_id=1, source_target_pairs={{0,16},{2,18},{4,20},{6,22},{8,24},{10,26},{12,28},{14,30},{16,0},... | collective-permute-start | bytes 393224 | tf_op jit(solution)/shard_map/ppermute | solution.py:411
  15.4 2.2 %collective-permute-start.3 = (bf16[144,1024]{1,0:T(8,128)(2,1)}, bf16[144,1024]{1,0:T(8,128)(2,1)S(1)}, u32[]{:S(2)}, u32[]{:S(2)}) collective-permute-start(bf16[144,1024]{1,0:T(8,128)(2,1)} %get-tuple-element.35), channel_id=1, source_target_pairs={{0,16},{2,18},{4,20},{6,22},{8,24},{10,26},{12,28},{14,30},{16,0},... | collective-permute-start | bytes 884744 | tf_op jit(solution)/shard_map/ppermute | solution.py:408
  18.5 1.6 %collective-permute-start.6 = (bf16[256,768]{1,0:T(8,128)(2,1)S(1)}, bf16[256,768]{1,0:T(8,128)(2,1)S(1)}, u32[]{:S(2)}, u32[]{:S(2)}) collective-permute-start(bf16[256,768]{1,0:T(8,128)(2,1)S(1)} %pad_maximum_fusion.1.w0), channel_id=1, source_target_pairs={{0,2},{2,0},{4,6},{6,4},{8,10},{10,8},{12,14},{14,12},{16,18},{18,... | collective-permute-start | bytes 1179656 | tf_op jit(solution)/shard_map/ppermute | solution.py:96
  20.1 1.5 %collective-permute-start.7 = (bf16[256,768]{1,0:T(8,128)(2,1)S(1)}, bf16[256,768]{1,0:T(8,128)(2,1)S(1)}, u32[]{:S(2)}, u32[]{:S(2)}) collective-permute-start(bf16[256,768]{1,0:T(8,128)(2,1)S(1)} %pad_maximum_fusion.1.w0), channel_id=1, source_target_pairs={{0,4},{2,6},{4,0},{6,2},{8,12},{10,14},{12,8},{14,10},{16,20},{18,... | collective-permute-start | bytes 1179656 | tf_op jit(solution)/shard_map/ppermute | solution.py:96
  22.1 7.4 %collective-permute-done.14 = bf16[64,1024]{1,0:T(8,128)(2,1)S(1)} collective-permute-done((bf16[64,1024]{1,0:T(8,128)(2,1)}, bf16[64,1024]{1,0:T(8,128)(2,1)S(1)}, u32[]{:S(2)}, u32[]{:S(2)}) %collective-permute-start.14) | collective-permute-done | bytes 131104 | tf_op jit(solution)/shard_map/ppermute | solution.py:411
  30.4 5.0 %collective-permute-done.3.own.got = bf16[144,1024]{1,0:T(8,128)(2,1)S(1)} collective-permute-done((bf16[144,1024]{1,0:T(8,128)(2,1)}, bf16[144,1024]{1,0:T(8,128)(2,1)S(1)}, u32[]{:S(2)}, u32[]{:S(2)}) %collective-permute-start.3) | collective-permute-done | bytes 294944 | tf_op jit(solution)/shard_map/ppermute | solution.py:408
  43.3 2.5 %column_attention.1 = (bf16[256,256]{1,0:T(8,128)(2,1)S(1)}, bf16[256,256]{1,0:T(8,128)(2,1)S(1)}) custom-call(f32[8]{0:T(128)S(1)} %copy-done.8, bf16[256,1024]{1,0:T(8,128)(2,1)S(1)} %column_normed.1.tokens, bf16[256,1024]{1,0:T(8,128)(2,1)S(1)} %far_normed.1.far_tokens, bf16[1024,768]{1,0:T(8,128)(2,1)S(1)} %column_project.1.weight), custom_call_target="tpu_custom_call" | custom-call | flops 1024 | bytes 262144 | tf_op jit(solution)/shard_map/column_attention/pallas_call | solution.py:42
  45.9 1.8 %collective-permute-done.12.w2 = bf16[256,256]{1,0:T(8,128)(2,1)S(1)} collective-permute-done((bf16[256,256]{1,0:T(8,128)(2,1)S(1)}, bf16[256,256]{1,0:T(8,128)(2,1)S(1)}, u32[]{:S(2)}, u32[]{:S(2)}) %collective-permute-start.12) | collective-permute-done | bytes 131104 | tf_op jit(solution)/shard_map/ppermute | solution.py:96
  51.1 1.8 %row_normed.1 = bf16[256,1024]{1,0:T(8,128)(2,1)} custom-call(bf16[256,256]{1,0:T(8,128)(2,1)S(1)} %get-tuple-element.48.mine, bf16[256,256]{1,0:T(8,128)(2,1)S(1)} %collective-permute-done.16.theirs, bf16[1024,256]{1,0:T(8,128)(2,1)S(1)} %column_output.1.near, bf16[1024,256]{1,0:T(8,128)(2,1)S(1)} %collective-permute-done.17.far, ...), custom_call_target="tpu_custom_call" | custom-call | flops 1024 | bytes 1024 | tf_op jit(solution)/shard_map/row_normed/pallas_call | solution.py:42
  52.9 4.4 %all-to-all-start = ((bf16[16,16,1024]{2,1,0:T(8,128)(2,1)}), bf16[16,16,1024]{2,1,0:T(8,128)(2,1)}, u32[]{:S(2)}, u32[]{:S(2)}) async-start(bf16[16,16,1024]{2,1,0:T(8,128)(2,1)} %bitcast.4), calls=%async_computation | async-start | bytes 1048576 | tf_op jit(solution)/shard_map/all_to_all | solution.py:470
  57.4 5.3 %collective-permute-done.18.refs_1_ = bf16[256,1024]{1,0:T(8,128)(2,1)S(1)} collective-permute-done((bf16[256,1024]{1,0:T(8,128)(2,1)S(1)}, bf16[256,1024]{1,0:T(8,128)(2,1)S(1)}, u32[]{:S(2)}, u32[]{:S(2)}) %collective-permute-start.18) | collective-permute-done | bytes 524320 | tf_op jit(solution)/shard_map/ppermute | solution.py:101
  62.7 3.3 %collective-permute-done.19.refs_2_ = bf16[256,1024]{1,0:T(8,128)(2,1)S(1)} collective-permute-done((bf16[256,1024]{1,0:T(8,128)(2,1)S(1)}, bf16[256,1024]{1,0:T(8,128)(2,1)S(1)}, u32[]{:S(2)}, u32[]{:S(2)}) %collective-permute-start.19) | collective-permute-done | bytes 524320 | tf_op jit(solution)/shard_map/ppermute | solution.py:101
  68.0 1.6 %collective-permute-start.21 = (bf16[128,1024]{1,0:T(8,128)(2,1)S(1)}, bf16[128,1024]{1,0:T(8,128)(2,1)S(1)}, u32[]{:S(2)}, u32[]{:S(2)}) collective-permute-start(bf16[128,1024]{1,0:T(8,128)(2,1)S(1)} %slice.46), channel_id=1, source_target_pairs={{0,4},{2,6},{4,0},{6,2},{8,12},{10,14},{12,8},{14,10},{16,20},{18,... | collective-permute-start | bytes 786440 | tf_op jit(solution)/shard_map/ppermute | solution.py:101
  69.5 6.3 %collective-permute-done.20.refs_3_ = bf16[128,1024]{1,0:T(8,128)(2,1)S(1)} collective-permute-done((bf16[128,1024]{1,0:T(8,128)(2,1)S(1)}, bf16[128,1024]{1,0:T(8,128)(2,1)S(1)}, u32[]{:S(2)}, u32[]{:S(2)}) %collective-permute-start.20) | collective-permute-done | bytes 262176 | tf_op jit(solution)/shard_map/ppermute | solution.py:101
  77.2 1.6 %collective-permute-start.27 = (bf16[128,512]{1,0:T(8,128)(2,1)S(1)}, bf16[128,512]{1,0:T(8,128)(2,1)S(1)}, u32[]{:S(2)}, u32[]{:S(2)}) collective-permute-start(bf16[128,512]{1,0:T(8,128)(2,1)S(1)} %pad_maximum_fusion.4), channel_id=1, source_target_pairs={{0,16},{2,18},{4,20},{6,22},{8,24},{10,26},{12,28},{14,30},{16,0},... | collective-permute-start | bytes 393224 | tf_op jit(solution)/shard_map/ppermute | solution.py:408
  79.9 6.5 %row_attention.1 = bf16[256,512]{1,0:T(8,128)(2,1)} custom-call(f32[8]{0:T(128)} %slopes.3, bf16[256,1024]{1,0:T(8,128)(2,1)} %bitcast.5.spread, bf16[256,1024]{1,0:T(8,128)(2,1)} %copy-done.9, bf16[256,1024]{1,0:T(8,128)(2,1)} %copy-done.10, bf16[256,1024]{1,0:T(8,128)(2,1)} %copy-done.11, bf16[128,1024]{1,0:T(8,128)(2,1)} %copy-done.15, ...), custom_call_target="tpu_custom_call" | custom-call | flops 1024 | bytes 1024 | tf_op jit(solution)/shard_map/row_attention/pallas_call | solution.py:42
  86.8 4.6 %all-to-all-start.1 = ((bf16[16,16,512]{2,1,0:T(8,128)(2,1)}), bf16[16,16,512]{2,1,0:T(8,128)(2,1)S(1)}, u32[]{:S(2)}, u32[]{:S(2)}) async-start(bf16[16,16,512]{2,1,0:T(8,128)(2,1)} %bitcast.15), calls=%async_computation.1 | async-start | bytes 524288 | tf_op jit(solution)/shard_map/all_to_all | solution.py:489
  91.4 5.0 %middle.1 = (f32[256,1024]{1,0:T(8,128)}, bf16[2,1024,256]{2,1,0:T(8,128)(2,1)}) custom-call(bf16[256,256]{1,0:T(8,128)(2,1)} %copy-done.3, bf16[256,256]{1,0:T(8,128)(2,1)} %copy-done.4, bf16[128,512]{1,0:T(8,128)(2,1)} %copy-done.19, bf16[1024,256]{1,0:T(8,128)(2,1)} %copy-done, bf16[1024,256]{1,0:T(8,128)(2,1)} %copy-done.1, bf16[256,1024]{1,0:T(8,128)(2,1)} %copy-done.9, ...), custom_call_target="tpu_custom_call" | custom-call | flops 1024 | bytes 1024 | tf_op jit(solution)/shard_map/middle/pallas_call | solution.py:42
  96.4 5.0 %all-to-all-done.1 = bf16[16,16,512]{2,1,0:T(8,128)(2,1)S(1)} async-done(((bf16[16,16,512]{2,1,0:T(8,128)(2,1)}), bf16[16,16,512]{2,1,0:T(8,128)(2,1)S(1)}, u32[]{:S(2)}, u32[]{:S(2)}) %all-to-all-start.1) | async-done | bytes 262176 | tf_op jit(solution)/shard_map/all_to_all | solution.py:489
  102.1 3.3 %block_output.1 = bf16[64,4,1024]{2,1,0:T(4,128)(2,1)} custom-call(bf16[256,512]{1,0:T(8,128)(2,1)} %bitcast.16, f32[256,1024]{1,0:T(8,128)} %get-tuple-element.61.middle, bf16[2,1024,256]{2,1,0:T(8,128)(2,1)} %get-tuple-element.62.weight), custom_call_target="tpu_custom_call" | custom-call | flops 1024 | bytes 1024 | tf_op jit(solution)/shard_map/block_output/pallas_call | solution.py:42
  (101 shorter events, 21.8 us)
Async XLA Ops:
  0.0 8.5 %collective-permute-start.9 = (bf16[64,256]{1,0:T(8,128)(2,1)}, bf16[64,256]{1,0:T(8,128)(2,1)S(1)}, u32[]{:S(2)}, u32[]{:S(2)}) collective-permute-start(bf16[64,256]{1,0:T(8,128)(2,1)} %param.19), channel_id=1, source_target_pairs={{0,16},{2,18},{4,20},{6,22},{8,24},{10,26},{12,28},{14,30},{16,0},... | collective-permute-start | bytes 98312 | tf_op jit(solution)/shard_map/ppermute | solution.py:411
  4.1 8.2 %collective-permute-start = (bf16[64,768]{1,0:T(8,128)(2,1)}, bf16[64,768]{1,0:T(8,128)(2,1)S(1)}, u32[]{:S(2)}, u32[]{:S(2)}) collective-permute-start(bf16[64,768]{1,0:T(8,128)(2,1)} %param.18), channel_id=1, source_target_pairs={{0,8},{2,10},{4,12},{6,14},{8,0},{10,2},{12,4},{14,6},{16,24},{18,... | collective-permute-start | bytes 294920 | tf_op jit(solution)/shard_map/ppermute | solution.py:86
  5.7 9.7 %collective-permute-start.1 = (bf16[64,768]{1,0:T(8,128)(2,1)}, bf16[64,768]{1,0:T(8,128)(2,1)S(1)}, u32[]{:S(2)}, u32[]{:S(2)}) collective-permute-start(bf16[64,768]{1,0:T(8,128)(2,1)} %param.18), channel_id=1, source_target_pairs={{0,16},{2,18},{4,20},{6,22},{8,24},{10,26},{12,28},{14,30},{16,0},... | collective-permute-start | bytes 294920 | tf_op jit(solution)/shard_map/ppermute | solution.py:86
  6.0 9.4 %collective-permute-start.2 = (bf16[64,768]{1,0:T(8,128)(2,1)}, bf16[64,768]{1,0:T(8,128)(2,1)S(1)}, u32[]{:S(2)}, u32[]{:S(2)}) collective-permute-start(bf16[64,768]{1,0:T(8,128)(2,1)} %param.18), channel_id=1, source_target_pairs={{0,24},{2,26},{4,28},{6,30},{8,16},{10,18},{12,20},{14,22},{16,8},... | collective-permute-start | bytes 294920 | tf_op jit(solution)/shard_map/ppermute | solution.py:86
  9.3 8.3 %collective-permute-start.10 = (bf16[128,256]{1,0:T(8,128)(2,1)S(1)}, bf16[128,256]{1,0:T(8,128)(2,1)S(1)}, u32[]{:S(2)}, u32[]{:S(2)}) collective-permute-start(bf16[128,256]{1,0:T(8,128)(2,1)S(1)} %pad_maximum_fusion.5), channel_id=1, source_target_pairs={{0,8},{2,10},{4,12},{6,14},{8,0},{10,2},{12,4},{14,6},{16,24},{18,... | collective-permute-start | bytes 196616 | tf_op jit(solution)/shard_map/ppermute | solution.py:90
  12.3 17.1 %collective-permute-start.14 = (bf16[64,1024]{1,0:T(8,128)(2,1)}, bf16[64,1024]{1,0:T(8,128)(2,1)S(1)}, u32[]{:S(2)}, u32[]{:S(2)}) collective-permute-start(bf16[64,1024]{1,0:T(8,128)(2,1)} %get-tuple-element.42), channel_id=1, source_target_pairs={{0,16},{2,18},{4,20},{6,22},{8,24},{10,26},{12,28},{14,30},{16,0},... | collective-permute-start | bytes 393224 | tf_op jit(solution)/shard_map/ppermute | solution.py:411
  15.4 19.9 %collective-permute-start.3 = (bf16[144,1024]{1,0:T(8,128)(2,1)}, bf16[144,1024]{1,0:T(8,128)(2,1)S(1)}, u32[]{:S(2)}, u32[]{:S(2)}) collective-permute-start(bf16[144,1024]{1,0:T(8,128)(2,1)} %get-tuple-element.35), channel_id=1, source_target_pairs={{0,16},{2,18},{4,20},{6,22},{8,24},{10,26},{12,28},{14,30},{16,0},... | collective-permute-start | bytes 884744 | tf_op jit(solution)/shard_map/ppermute | solution.py:408
  18.5 18.9 %collective-permute-start.6 = (bf16[256,768]{1,0:T(8,128)(2,1)S(1)}, bf16[256,768]{1,0:T(8,128)(2,1)S(1)}, u32[]{:S(2)}, u32[]{:S(2)}) collective-permute-start(bf16[256,768]{1,0:T(8,128)(2,1)S(1)} %pad_maximum_fusion.1.w0), channel_id=1, source_target_pairs={{0,2},{2,0},{4,6},{6,4},{8,10},{10,8},{12,14},{14,12},{16,18},{18,... | collective-permute-start | bytes 1179656 | tf_op jit(solution)/shard_map/ppermute | solution.py:96
  20.1 18.1 %collective-permute-start.7 = (bf16[256,768]{1,0:T(8,128)(2,1)S(1)}, bf16[256,768]{1,0:T(8,128)(2,1)S(1)}, u32[]{:S(2)}, u32[]{:S(2)}) collective-permute-start(bf16[256,768]{1,0:T(8,128)(2,1)S(1)} %pad_maximum_fusion.1.w0), channel_id=1, source_target_pairs={{0,4},{2,6},{4,0},{6,2},{8,12},{10,14},{12,8},{14,10},{16,20},{18,... | collective-permute-start | bytes 1179656 | tf_op jit(solution)/shard_map/ppermute | solution.py:96
  21.6 16.6 %collective-permute-start.8 = (bf16[256,768]{1,0:T(8,128)(2,1)S(1)}, bf16[256,768]{1,0:T(8,128)(2,1)S(1)}, u32[]{:S(2)}, u32[]{:S(2)}) collective-permute-start(bf16[256,768]{1,0:T(8,128)(2,1)S(1)} %pad_maximum_fusion.1.w0), channel_id=1, source_target_pairs={{0,6},{2,4},{4,2},{6,0},{8,14},{10,12},{12,10},{14,8},{16,22},{18,... | collective-permute-start | bytes 1179656 | tf_op jit(solution)/shard_map/ppermute | solution.py:96
  35.3 7.9 %collective-permute-start.15 = (bf16[128,1024]{1,0:T(8,128)(2,1)S(1)}, bf16[128,1024]{1,0:T(8,128)(2,1)S(1)}, u32[]{:S(2)}, u32[]{:S(2)}) collective-permute-start(bf16[128,1024]{1,0:T(8,128)(2,1)S(1)} %pad_maximum_fusion.2), channel_id=1, source_target_pairs={{0,8},{2,10},{4,12},{6,14},{8,0},{10,2},{12,4},{14,6},{16,24},{18,... | collective-permute-start | bytes 786440 | tf_op jit(solution)/shard_map/ppermute | solution.py:90
  38.5 7.3 %collective-permute-start.11 = (bf16[256,256]{1,0:T(8,128)(2,1)S(1)}, bf16[256,256]{1,0:T(8,128)(2,1)S(1)}, u32[]{:S(2)}, u32[]{:S(2)}) collective-permute-start(bf16[256,256]{1,0:T(8,128)(2,1)S(1)} %pad_maximum_fusion.3.w0), channel_id=1, source_target_pairs={{0,2},{2,0},{4,6},{6,4},{8,10},{10,8},{12,14},{14,12},{16,18},{18,... | collective-permute-start | bytes 393224 | tf_op jit(solution)/shard_map/ppermute | solution.py:96
  39.8 7.8 %collective-permute-start.12 = (bf16[256,256]{1,0:T(8,128)(2,1)S(1)}, bf16[256,256]{1,0:T(8,128)(2,1)S(1)}, u32[]{:S(2)}, u32[]{:S(2)}) collective-permute-start(bf16[256,256]{1,0:T(8,128)(2,1)S(1)} %pad_maximum_fusion.3.w0), channel_id=1, source_target_pairs={{0,4},{2,6},{4,0},{6,2},{8,12},{10,14},{12,8},{14,10},{16,20},{18,... | collective-permute-start | bytes 393224 | tf_op jit(solution)/shard_map/ppermute | solution.py:96
  40.9 6.8 %collective-permute-start.13 = (bf16[256,256]{1,0:T(8,128)(2,1)S(1)}, bf16[256,256]{1,0:T(8,128)(2,1)S(1)}, u32[]{:S(2)}, u32[]{:S(2)}) collective-permute-start(bf16[256,256]{1,0:T(8,128)(2,1)S(1)} %pad_maximum_fusion.3.w0), channel_id=1, source_target_pairs={{0,6},{2,4},{4,2},{6,0},{8,14},{10,12},{12,10},{14,8},{16,22},{18,... | collective-permute-start | bytes 393224 | tf_op jit(solution)/shard_map/ppermute | solution.py:96
  47.8 15.0 %collective-permute-start.18 = (bf16[256,1024]{1,0:T(8,128)(2,1)S(1)}, bf16[256,1024]{1,0:T(8,128)(2,1)S(1)}, u32[]{:S(2)}, u32[]{:S(2)}) collective-permute-start(bf16[256,1024]{1,0:T(8,128)(2,1)S(1)} %pad_maximum_fusion.refs_0_), channel_id=1, source_target_pairs={{0,2},{2,0},{4,6},{6,4},{8,10},{10,8},{12,14},{14,12},{16,18},{18,... | collective-permute-start | bytes 1572872 | tf_op jit(solution)/shard_map/ppermute | solution.py:101
  48.9 17.2 %collective-permute-start.19 = (bf16[256,1024]{1,0:T(8,128)(2,1)S(1)}, bf16[256,1024]{1,0:T(8,128)(2,1)S(1)}, u32[]{:S(2)}, u32[]{:S(2)}) collective-permute-start(bf16[256,1024]{1,0:T(8,128)(2,1)S(1)} %pad_maximum_fusion.refs_0_), channel_id=1, source_target_pairs={{0,4},{2,6},{4,0},{6,2},{8,12},{10,14},{12,8},{14,10},{16,20},{18,... | collective-permute-start | bytes 1572872 | tf_op jit(solution)/shard_map/ppermute | solution.py:101
  52.9 26.6 %all-to-all-start = ((bf16[16,16,1024]{2,1,0:T(8,128)(2,1)}), bf16[16,16,1024]{2,1,0:T(8,128)(2,1)}, u32[]{:S(2)}, u32[]{:S(2)}) async-start(bf16[16,16,1024]{2,1,0:T(8,128)(2,1)} %bitcast.4), calls=%async_computation | async-start | bytes 1048576 | tf_op jit(solution)/shard_map/all_to_all | solution.py:470
  66.0 11.2 %collective-permute-start.22 = (bf16[256,1024]{1,0:T(8,128)(2,1)S(1)}, bf16[256,1024]{1,0:T(8,128)(2,1)S(1)}, u32[]{:S(2)}, u32[]{:S(2)}) collective-permute-start(bf16[256,1024]{1,0:T(8,128)(2,1)S(1)} %pad_maximum_fusion.refs_0_), channel_id=1, source_target_pairs={{0,1},{1,0},{2,3},{3,2},{4,5},{5,4},{6,7},{7,6},{8,9},{9,8},{10,11... | collective-permute-start | bytes 1572872 | tf_op jit(solution)/shard_map/ppermute | solution.py:24
  66.0 9.8 %collective-permute-start.20 = (bf16[128,1024]{1,0:T(8,128)(2,1)S(1)}, bf16[128,1024]{1,0:T(8,128)(2,1)S(1)}, u32[]{:S(2)}, u32[]{:S(2)}) collective-permute-start(bf16[128,1024]{1,0:T(8,128)(2,1)S(1)} %slice.45), channel_id=1, source_target_pairs={{0,2},{2,0},{4,6},{6,4},{8,10},{10,8},{12,14},{14,12},{16,18},{18,... | collective-permute-start | bytes 786440 | tf_op jit(solution)/shard_map/ppermute | solution.py:101
  67.4 11.3 %collective-permute-start.23 = (bf16[256,1024]{1,0:T(8,128)(2,1)S(1)}, bf16[256,1024]{1,0:T(8,128)(2,1)S(1)}, u32[]{:S(2)}, u32[]{:S(2)}) collective-permute-start(bf16[256,1024]{1,0:T(8,128)(2,1)S(1)} %collective-permute-done.18.refs_1_), channel_id=1, source_target_pairs={{0,1},{1,0},{2,3},{3,2},{4,5},{5,4},{6,7},{7,6},{8,9},{9,8},{10,11... | collective-permute-start | bytes 1572872 | tf_op jit(solution)/shard_map/ppermute | solution.py:24
  67.7 11.1 %collective-permute-start.24 = (bf16[256,1024]{1,0:T(8,128)(2,1)S(1)}, bf16[256,1024]{1,0:T(8,128)(2,1)S(1)}, u32[]{:S(2)}, u32[]{:S(2)}) collective-permute-start(bf16[256,1024]{1,0:T(8,128)(2,1)S(1)} %collective-permute-done.19.refs_2_), channel_id=1, source_target_pairs={{0,1},{1,0},{2,3},{3,2},{4,5},{5,4},{6,7},{7,6},{8,9},{9,8},{10,11... | collective-permute-start | bytes 1572872 | tf_op jit(solution)/shard_map/ppermute | solution.py:24
  68.0 9.2 %collective-permute-start.21 = (bf16[128,1024]{1,0:T(8,128)(2,1)S(1)}, bf16[128,1024]{1,0:T(8,128)(2,1)S(1)}, u32[]{:S(2)}, u32[]{:S(2)}) collective-permute-start(bf16[128,1024]{1,0:T(8,128)(2,1)S(1)} %slice.46), channel_id=1, source_target_pairs={{0,4},{2,6},{4,0},{6,2},{8,12},{10,14},{12,8},{14,10},{16,20},{18,... | collective-permute-start | bytes 786440 | tf_op jit(solution)/shard_map/ppermute | solution.py:101
  77.2 9.6 %collective-permute-start.27 = (bf16[128,512]{1,0:T(8,128)(2,1)S(1)}, bf16[128,512]{1,0:T(8,128)(2,1)S(1)}, u32[]{:S(2)}, u32[]{:S(2)}) collective-permute-start(bf16[128,512]{1,0:T(8,128)(2,1)S(1)} %pad_maximum_fusion.4), channel_id=1, source_target_pairs={{0,16},{2,18},{4,20},{6,22},{8,24},{10,26},{12,28},{14,30},{16,0},... | collective-permute-start | bytes 393224 | tf_op jit(solution)/shard_map/ppermute | solution.py:408
  86.8 14.6 %all-to-all-start.1 = ((bf16[16,16,512]{2,1,0:T(8,128)(2,1)}), bf16[16,16,512]{2,1,0:T(8,128)(2,1)S(1)}, u32[]{:S(2)}, u32[]{:S(2)}) async-start(bf16[16,16,512]{2,1,0:T(8,128)(2,1)} %bitcast.15), calls=%async_computation.1 | async-start | bytes 524288 | tf_op jit(solution)/shard_map/all_to_all | solution.py:489
  (27 other events, 253.6 us)

commit v5 on v4

--- a/solution.py
+++ b/solution.py
@@ -13,7 +13,6 @@
 PLANE = 4
 NEVER = -1e30
 EXTRA = 16
-CHUNKS = 4
 
 
 def at(place, length):
@@ -355,27 +354,16 @@
             out[:, start : start + PAIR] = dot(homeward, mixed).astype(jnp.bfloat16)
 
 
-def final_kernel(mixed, middle, weight, out, mixed_held, total, held, staged, sems, out_sems):
-    width = held.shape[2]
-    step = total.shape[1] // CHUNKS
-    cut = [slice(i * step, (i + 1) * step) for i in range(CHUNKS)]
-    pairs = [(mixed, mixed_held)]
-    for at_cols in cut:
-        pairs += [(weight.at[half, at_cols, :], held.at[half, at_cols, :]) for half in range(2)]
-        pairs += [(middle.at[:, at_cols], total.at[:, at_cols])]
-    coming = bring(pairs, sems)
-    coming[0].wait()
-    going = []
-    for i, at_cols in enumerate(cut):
-        wait(coming[1 + 3 * i : 4 + 3 * i])
-        update = total[:, at_cols]
-        for half in range(2):
-            update += dot_t(mixed_held[:, half * width : (half + 1) * width], held[half, at_cols, :])
-        staged[:, :, at_cols] = update.reshape(*out.shape[:2], step).astype(jnp.bfloat16)
-        copy = pltpu.make_async_copy(staged.at[:, :, at_cols], out.at[:, :, at_cols], out_sems.at[i])
-        copy.start()
-        going.append(copy)
-    wait(going)
+def final_kernel(mixed, middle, weight, out, *refs):
+    *held, staged, sems = refs
+    coming = bring(zip((mixed, weight, middle), held), sems)
+    mixed, weight, middle = held
+    width = weight.shape[2]
+    wait(coming[:2])
+    update = dot_t(mixed[:, :width], weight[0]) + dot_t(mixed[:, width:], weight[1])
+    wait(coming[2:])
+    staged[...] = (middle[...] + update).reshape(out.shape).astype(jnp.bfloat16)
+    wait(bring([(staged, out)], sems))
 
 
 def fast(
@@ -438,10 +426,10 @@
     )
     kept_normed = column_normed(keep, keep_other, "column_normed")
     far_normed = column_normed(far, far_other, "far_normed")
+    far_normed, project, output = after((far_normed, project, output))
     project = call(
         functools.partial(order_kernel, shard, True), project_shape, "column_project", project
     )
-    far_normed, project, output = after((far_normed, project, output))
     row_weights, _ = after((row_weights, far))
     output = across_plane(output, lon_count)
     row_weights = doubled(row_weights, PLANE, lon_count)
@@ -466,6 +454,7 @@
         bf16(tokens, width),
         "row_normed",
         (mixed_own, theirs, output, output_far, keep, far, embed, row_gain),
+        cost=2**20,
     )
     spread = lax.all_to_all(row_normed, "lon", split_axis=0, concat_axis=0, tiled=True)
     to_home, row_weights = after((to_home, row_weights))
@@ -502,10 +491,7 @@
         bf16(band, cols, width),
         "block_output",
         given=(back, middle, row_out),
-        scratch=vmem(back, middle, row_out)
-        + [pltpu.VMEM(fields.shape, jnp.bfloat16)]
-        + sems(1 + 3 * CHUNKS)
-        + sems(CHUNKS),
+        scratch=vmem(back, row_out, middle) + [pltpu.VMEM(fields.shape, jnp.bfloat16)] + sems(3),
         room=60,
         space=pltpu.HBM,
     )

time: 106 us -> 105 us (level)
  waiting for transfers between devices: 40.9 us -> 39.2 us
    ppermute x6, waiting for transfers between devices: 2.54 us -> 1.46 us  [across_plane(): lax.ppermute(part, 'lon', at(lambda i: i ^ k, length))]
where the time goes in v5:
time: 105 us
  waiting for transfers between devices  39.2 us (37%)
  starting transfers between devices  38 us (36%)
  Pallas kernels  22.1 us (21%)
  other arithmetic  2.67 us (3%)
  local copies, waits for them, and re-layouts  2.2 us (2%)
    pallas_call x10, Pallas kernels, call(): pl.pallas_call(kernel, out_shape=out, in_specs=[SCALARS] * len(scalars) +...  22.1 us
    ppermute x4, waiting for transfers between devices, relayed_plane(): lax.ppermute(value, 'lon', at(lambda i: i ^ k, length))  15.5 us
    ppermute x2, waiting for transfers between devices, fast(): lax.ppermute(value, 'lon', at(lambda i: i ^ 2 * PLANE, lon_count))  7.37 us
    ppermute x6, starting transfers between devices, across_plane(): lax.ppermute(part, 'lon', at(lambda i: i ^ k, length))  7.04 us
    ppermute x2, starting transfers between devices, fast(): lax.ppermute(value, 'lon', at(lambda i: i ^ 2 * PLANE, lon_count))  6.45 us
    ppermute x4, starting transfers between devices, relayed_plane(): lax.ppermute(value, 'lon', at(lambda i: i ^ k, length))  5.7 us
    ppermute x2, waiting for transfers between devices, fast(): lax.ppermute(value, 'lon', at(lambda i: (i + lon_count // 2) % lon_count,...  5.23 us
    all_to_all x1, starting transfers between devices, fast(): lax.all_to_all(row_mixed, 'lon', split_axis=0, concat_axis=0, tiled=True)  4.95 us
  transfers between devices with their start and end apart: 30, of which 14 were waited for; matrix products, arithmetic and copies ran while one was open for 3% of the time, Pallas kernels for 18%

profile of v5, /device:TPU:0, one launch (start us, length us, event | category | flops | bytes accessed | tf_op | source)
XLA Modules:
  0.0 104.6 jit_solution(2832242283680365908)
XLA Ops:
  0.0 4.1 %collective-permute-start.9 = (bf16[64,256]{1,0:T(8,128)(2,1)}, bf16[64,256]{1,0:T(8,128)(2,1)S(1)}, u32[]{:S(2)}, u32[]{:S(2)}) collective-permute-start(bf16[64,256]{1,0:T(8,128)(2,1)} %param.19), channel_id=1, source_target_pairs={{0,16},{2,18},{4,20},{6,22},{8,24},{10,26},{12,28},{14,30},{16,0},... | collective-permute-start | bytes 98312 | tf_op jit(solution)/shard_map/ppermute | solution.py:399
  4.1 1.6 %collective-permute-start = (bf16[64,768]{1,0:T(8,128)(2,1)}, bf16[64,768]{1,0:T(8,128)(2,1)S(1)}, u32[]{:S(2)}, u32[]{:S(2)}) collective-permute-start(bf16[64,768]{1,0:T(8,128)(2,1)} %param.18), channel_id=1, source_target_pairs={{0,8},{2,10},{4,12},{6,14},{8,0},{10,2},{12,4},{14,6},{16,24},{18,... | collective-permute-start | bytes 294920 | tf_op jit(solution)/shard_map/ppermute | solution.py:85
  6.0 2.5 %collective-permute-start.2 = (bf16[64,768]{1,0:T(8,128)(2,1)}, bf16[64,768]{1,0:T(8,128)(2,1)S(1)}, u32[]{:S(2)}, u32[]{:S(2)}) collective-permute-start(bf16[64,768]{1,0:T(8,128)(2,1)} %param.18), channel_id=1, source_target_pairs={{0,24},{2,26},{4,28},{6,30},{8,16},{10,18},{12,20},{14,22},{16,8},... | collective-permute-start | bytes 294920 | tf_op jit(solution)/shard_map/ppermute | solution.py:85
  9.9 2.2 %loop_tokens.1 = (bf16[144,1024]{1,0:T(8,128)(2,1)}, bf16[144,1024]{1,0:T(8,128)(2,1)}, bf16[64,1024]{1,0:T(8,128)(2,1)}) custom-call(bf16[64,4,1024]{2,1,0:T(4,128)(2,1)} %refs_10_.1, s32[4,64]{1,0:T(4,128)} %bitcast.17, bf16[64,768]{1,0:T(8,128)(2,1)} %project.1, bf16[64,256]{1,0:T(8,128)(2,1)} %output.1), custom_call_target="tpu_custom_call" | custom-call | flops 1024 | bytes 1024 | tf_op jit(solution)/shard_map/loop_tokens/pallas_call | solution.py:41
  12.3 2.3 %collective-permute-start.14 = (bf16[64,1024]{1,0:T(8,128)(2,1)}, bf16[64,1024]{1,0:T(8,128)(2,1)S(1)}, u32[]{:S(2)}, u32[]{:S(2)}) collective-permute-start(bf16[64,1024]{1,0:T(8,128)(2,1)} %get-tuple-element.45), channel_id=1, source_target_pairs={{0,16},{2,18},{4,20},{6,22},{8,24},{10,26},{12,28},{14,30},{16,0},... | collective-permute-start | bytes 393224 | tf_op jit(solution)/shard_map/ppermute | solution.py:399
  15.4 2.2 %collective-permute-start.3 = (bf16[144,1024]{1,0:T(8,128)(2,1)}, bf16[144,1024]{1,0:T(8,128)(2,1)S(1)}, u32[]{:S(2)}, u32[]{:S(2)}) collective-permute-start(bf16[144,1024]{1,0:T(8,128)(2,1)} %get-tuple-element.38), channel_id=1, source_target_pairs={{0,16},{2,18},{4,20},{6,22},{8,24},{10,26},{12,28},{14,30},{16,0},... | collective-permute-start | bytes 884744 | tf_op jit(solution)/shard_map/ppermute | solution.py:396
  18.5 1.6 %collective-permute-start.6 = (bf16[256,768]{1,0:T(8,128)(2,1)S(1)}, bf16[256,768]{1,0:T(8,128)(2,1)S(1)}, u32[]{:S(2)}, u32[]{:S(2)}) collective-permute-start(bf16[256,768]{1,0:T(8,128)(2,1)S(1)} %pad_maximum_fusion.1.w0), channel_id=1, source_target_pairs={{0,2},{2,0},{4,6},{6,4},{8,10},{10,8},{12,14},{14,12},{16,18},{18,... | collective-permute-start | bytes 1179656 | tf_op jit(solution)/shard_map/ppermute | solution.py:95
  20.1 1.5 %collective-permute-start.7 = (bf16[256,768]{1,0:T(8,128)(2,1)S(1)}, bf16[256,768]{1,0:T(8,128)(2,1)S(1)}, u32[]{:S(2)}, u32[]{:S(2)}) collective-permute-start(bf16[256,768]{1,0:T(8,128)(2,1)S(1)} %pad_maximum_fusion.1.w0), channel_id=1, source_target_pairs={{0,4},{2,6},{4,0},{6,2},{8,12},{10,14},{12,8},{14,10},{16,20},{18,... | collective-permute-start | bytes 1179656 | tf_op jit(solution)/shard_map/ppermute | solution.py:95
  22.1 7.4 %collective-permute-done.14 = bf16[64,1024]{1,0:T(8,128)(2,1)S(1)} collective-permute-done((bf16[64,1024]{1,0:T(8,128)(2,1)}, bf16[64,1024]{1,0:T(8,128)(2,1)S(1)}, u32[]{:S(2)}, u32[]{:S(2)}) %collective-permute-start.14) | collective-permute-done | bytes 131104 | tf_op jit(solution)/shard_map/ppermute | solution.py:399
  30.4 5.0 %collective-permute-done.3.own.got = bf16[144,1024]{1,0:T(8,128)(2,1)S(1)} collective-permute-done((bf16[144,1024]{1,0:T(8,128)(2,1)}, bf16[144,1024]{1,0:T(8,128)(2,1)S(1)}, u32[]{:S(2)}, u32[]{:S(2)}) %collective-permute-start.3) | collective-permute-done | bytes 294944 | tf_op jit(solution)/shard_map/ppermute | solution.py:396
  41.7 1.6 %collective-permute-done.15 = bf16[128,1024]{1,0:T(8,128)(2,1)S(1)} collective-permute-done((bf16[128,1024]{1,0:T(8,128)(2,1)S(1)}, bf16[128,1024]{1,0:T(8,128)(2,1)S(1)}, u32[]{:S(2)}, u32[]{:S(2)}) %collective-permute-start.15) | collective-permute-done | bytes 262176 | tf_op jit(solution)/shard_map/ppermute | solution.py:89
  44.0 2.5 %column_attention.1 = (bf16[256,256]{1,0:T(8,128)(2,1)S(1)}, bf16[256,256]{1,0:T(8,128)(2,1)S(1)}) custom-call(f32[8]{0:T(128)S(1)} %copy-done.8, bf16[256,1024]{1,0:T(8,128)(2,1)S(1)} %column_normed.1.tokens, bf16[256,1024]{1,0:T(8,128)(2,1)S(1)} %far_normed.1.far_tokens, bf16[1024,768]{1,0:T(8,128)(2,1)S(1)} %column_project.1.weight), custom_call_target="tpu_custom_call" | custom-call | flops 1024 | bytes 262144 | tf_op jit(solution)/shard_map/column_attention/pallas_call | solution.py:41
  51.1 1.8 %row_normed.1 = bf16[256,1024]{1,0:T(8,128)(2,1)} custom-call(bf16[256,256]{1,0:T(8,128)(2,1)S(1)} %get-tuple-element.54.mine, bf16[256,256]{1,0:T(8,128)(2,1)S(1)} %collective-permute-done.16.theirs, bf16[1024,256]{1,0:T(8,128)(2,1)S(1)} %column_output.1.near, bf16[1024,256]{1,0:T(8,128)(2,1)S(1)} %collective-permute-done.17.far, ...), custom_call_target="tpu_custom_call" | custom-call | flops 1024 | bytes 1048576 | tf_op jit(solution)/shard_map/row_normed/pallas_call | solution.py:41
  52.9 4.2 %all-to-all-start = ((bf16[16,16,1024]{2,1,0:T(8,128)(2,1)}), bf16[16,16,1024]{2,1,0:T(8,128)(2,1)}, u32[]{:S(2)}, u32[]{:S(2)}) async-start(bf16[16,16,1024]{2,1,0:T(8,128)(2,1)} %bitcast.4), calls=%async_computation | async-start | bytes 1048576 | tf_op jit(solution)/shard_map/all_to_all | solution.py:459
  57.2 5.1 %collective-permute-done.18.refs_1_ = bf16[256,1024]{1,0:T(8,128)(2,1)S(1)} collective-permute-done((bf16[256,1024]{1,0:T(8,128)(2,1)S(1)}, bf16[256,1024]{1,0:T(8,128)(2,1)S(1)}, u32[]{:S(2)}, u32[]{:S(2)}) %collective-permute-start.18) | collective-permute-done | bytes 524320 | tf_op jit(solution)/shard_map/ppermute | solution.py:100
  62.3 3.0 %collective-permute-done.19.refs_2_ = bf16[256,1024]{1,0:T(8,128)(2,1)S(1)} collective-permute-done((bf16[256,1024]{1,0:T(8,128)(2,1)S(1)}, bf16[256,1024]{1,0:T(8,128)(2,1)S(1)}, u32[]{:S(2)}, u32[]{:S(2)}) %collective-permute-start.19) | collective-permute-done | bytes 524320 | tf_op jit(solution)/shard_map/ppermute | solution.py:100
  67.2 1.9 %collective-permute-start.21 = (bf16[128,1024]{1,0:T(8,128)(2,1)S(1)}, bf16[128,1024]{1,0:T(8,128)(2,1)S(1)}, u32[]{:S(2)}, u32[]{:S(2)}) collective-permute-start(bf16[128,1024]{1,0:T(8,128)(2,1)S(1)} %slice.46), channel_id=1, source_target_pairs={{0,4},{2,6},{4,0},{6,2},{8,12},{10,14},{12,8},{14,10},{16,20},{18,... | collective-permute-start | bytes 786440 | tf_op jit(solution)/shard_map/ppermute | solution.py:100
  69.2 6.5 %collective-permute-done.20.refs_3_ = bf16[128,1024]{1,0:T(8,128)(2,1)S(1)} collective-permute-done((bf16[128,1024]{1,0:T(8,128)(2,1)S(1)}, bf16[128,1024]{1,0:T(8,128)(2,1)S(1)}, u32[]{:S(2)}, u32[]{:S(2)}) %collective-permute-start.20) | collective-permute-done | bytes 262176 | tf_op jit(solution)/shard_map/ppermute | solution.py:100
  76.6 1.8 %collective-permute-start.27 = (bf16[128,512]{1,0:T(8,128)(2,1)S(1)}, bf16[128,512]{1,0:T(8,128)(2,1)S(1)}, u32[]{:S(2)}, u32[]{:S(2)}) collective-permute-start(bf16[128,512]{1,0:T(8,128)(2,1)S(1)} %pad_maximum_fusion.4), channel_id=1, source_target_pairs={{0,16},{2,18},{4,20},{6,22},{8,24},{10,26},{12,28},{14,30},{16,0},... | collective-permute-start | bytes 393224 | tf_op jit(solution)/shard_map/ppermute | solution.py:396
  79.5 6.5 %row_attention.1 = bf16[256,512]{1,0:T(8,128)(2,1)} custom-call(f32[8]{0:T(128)} %slopes.3, bf16[256,1024]{1,0:T(8,128)(2,1)} %bitcast.5.spread, bf16[256,1024]{1,0:T(8,128)(2,1)} %copy-done.9, bf16[256,1024]{1,0:T(8,128)(2,1)} %copy-done.10, bf16[256,1024]{1,0:T(8,128)(2,1)} %copy-done.11, bf16[128,1024]{1,0:T(8,128)(2,1)} %copy-done.15, ...), custom_call_target="tpu_custom_call" | custom-call | flops 1024 | bytes 1024 | tf_op jit(solution)/shard_map/row_attention/pallas_call | solution.py:41
  86.2 4.9 %all-to-all-start.1 = ((bf16[16,16,512]{2,1,0:T(8,128)(2,1)}), bf16[16,16,512]{2,1,0:T(8,128)(2,1)S(1)}, u32[]{:S(2)}, u32[]{:S(2)}) async-start(bf16[16,16,512]{2,1,0:T(8,128)(2,1)} %bitcast.15), calls=%async_computation.1 | async-start | bytes 524288 | tf_op jit(solution)/shard_map/all_to_all | solution.py:478
  91.2 5.0 %middle.1 = (f32[256,1024]{1,0:T(8,128)}, bf16[2,1024,256]{2,1,0:T(8,128)(2,1)}) custom-call(bf16[256,256]{1,0:T(8,128)(2,1)} %copy-done.3, bf16[256,256]{1,0:T(8,128)(2,1)} %copy-done.4, bf16[128,512]{1,0:T(8,128)(2,1)} %copy-done.19, bf16[1024,256]{1,0:T(8,128)(2,1)} %copy-done, bf16[1024,256]{1,0:T(8,128)(2,1)} %copy-done.1, bf16[256,1024]{1,0:T(8,128)(2,1)} %copy-done.9, ...), custom_call_target="tpu_custom_call" | custom-call | flops 1024 | bytes 1024 | tf_op jit(solution)/shard_map/middle/pallas_call | solution.py:41
  96.2 4.9 %all-to-all-done.1 = bf16[16,16,512]{2,1,0:T(8,128)(2,1)S(1)} async-done(((bf16[16,16,512]{2,1,0:T(8,128)(2,1)}), bf16[16,16,512]{2,1,0:T(8,128)(2,1)S(1)}, u32[]{:S(2)}, u32[]{:S(2)}) %all-to-all-start.1) | async-done | bytes 262176 | tf_op jit(solution)/shard_map/all_to_all | solution.py:478
  101.8 2.8 %block_output.1 = bf16[64,4,1024]{2,1,0:T(4,128)(2,1)} custom-call(bf16[256,512]{1,0:T(8,128)(2,1)} %bitcast.16, f32[256,1024]{1,0:T(8,128)} %get-tuple-element.67.middle, bf16[2,1024,256]{2,1,0:T(8,128)(2,1)} %get-tuple-element.68.weight), custom_call_target="tpu_custom_call" | custom-call | flops 1024 | bytes 1024 | tf_op jit(solution)/shard_map/block_output/pallas_call | solution.py:41
  (101 shorter events, 21.4 us)
Async XLA Ops:
  0.0 8.5 %collective-permute-start.9 = (bf16[64,256]{1,0:T(8,128)(2,1)}, bf16[64,256]{1,0:T(8,128)(2,1)S(1)}, u32[]{:S(2)}, u32[]{:S(2)}) collective-permute-start(bf16[64,256]{1,0:T(8,128)(2,1)} %param.19), channel_id=1, source_target_pairs={{0,16},{2,18},{4,20},{6,22},{8,24},{10,26},{12,28},{14,30},{16,0},... | collective-permute-start | bytes 98312 | tf_op jit(solution)/shard_map/ppermute | solution.py:399
  4.1 8.2 %collective-permute-start = (bf16[64,768]{1,0:T(8,128)(2,1)}, bf16[64,768]{1,0:T(8,128)(2,1)S(1)}, u32[]{:S(2)}, u32[]{:S(2)}) collective-permute-start(bf16[64,768]{1,0:T(8,128)(2,1)} %param.18), channel_id=1, source_target_pairs={{0,8},{2,10},{4,12},{6,14},{8,0},{10,2},{12,4},{14,6},{16,24},{18,... | collective-permute-start | bytes 294920 | tf_op jit(solution)/shard_map/ppermute | solution.py:85
  5.7 9.7 %collective-permute-start.1 = (bf16[64,768]{1,0:T(8,128)(2,1)}, bf16[64,768]{1,0:T(8,128)(2,1)S(1)}, u32[]{:S(2)}, u32[]{:S(2)}) collective-permute-start(bf16[64,768]{1,0:T(8,128)(2,1)} %param.18), channel_id=1, source_target_pairs={{0,16},{2,18},{4,20},{6,22},{8,24},{10,26},{12,28},{14,30},{16,0},... | collective-permute-start | bytes 294920 | tf_op jit(solution)/shard_map/ppermute | solution.py:85
  6.0 9.4 %collective-permute-start.2 = (bf16[64,768]{1,0:T(8,128)(2,1)}, bf16[64,768]{1,0:T(8,128)(2,1)S(1)}, u32[]{:S(2)}, u32[]{:S(2)}) collective-permute-start(bf16[64,768]{1,0:T(8,128)(2,1)} %param.18), channel_id=1, source_target_pairs={{0,24},{2,26},{4,28},{6,30},{8,16},{10,18},{12,20},{14,22},{16,8},... | collective-permute-start | bytes 294920 | tf_op jit(solution)/shard_map/ppermute | solution.py:85
  9.3 8.3 %collective-permute-start.10 = (bf16[128,256]{1,0:T(8,128)(2,1)S(1)}, bf16[128,256]{1,0:T(8,128)(2,1)S(1)}, u32[]{:S(2)}, u32[]{:S(2)}) collective-permute-start(bf16[128,256]{1,0:T(8,128)(2,1)S(1)} %pad_maximum_fusion.5), channel_id=1, source_target_pairs={{0,8},{2,10},{4,12},{6,14},{8,0},{10,2},{12,4},{14,6},{16,24},{18,... | collective-permute-start | bytes 196616 | tf_op jit(solution)/shard_map/ppermute | solution.py:89
  12.3 17.1 %collective-permute-start.14 = (bf16[64,1024]{1,0:T(8,128)(2,1)}, bf16[64,1024]{1,0:T(8,128)(2,1)S(1)}, u32[]{:S(2)}, u32[]{:S(2)}) collective-permute-start(bf16[64,1024]{1,0:T(8,128)(2,1)} %get-tuple-element.45), channel_id=1, source_target_pairs={{0,16},{2,18},{4,20},{6,22},{8,24},{10,26},{12,28},{14,30},{16,0},... | collective-permute-start | bytes 393224 | tf_op jit(solution)/shard_map/ppermute | solution.py:399
  15.4 19.9 %collective-permute-start.3 = (bf16[144,1024]{1,0:T(8,128)(2,1)}, bf16[144,1024]{1,0:T(8,128)(2,1)S(1)}, u32[]{:S(2)}, u32[]{:S(2)}) collective-permute-start(bf16[144,1024]{1,0:T(8,128)(2,1)} %get-tuple-element.38), channel_id=1, source_target_pairs={{0,16},{2,18},{4,20},{6,22},{8,24},{10,26},{12,28},{14,30},{16,0},... | collective-permute-start | bytes 884744 | tf_op jit(solution)/shard_map/ppermute | solution.py:396
  18.5 18.9 %collective-permute-start.6 = (bf16[256,768]{1,0:T(8,128)(2,1)S(1)}, bf16[256,768]{1,0:T(8,128)(2,1)S(1)}, u32[]{:S(2)}, u32[]{:S(2)}) collective-permute-start(bf16[256,768]{1,0:T(8,128)(2,1)S(1)} %pad_maximum_fusion.1.w0), channel_id=1, source_target_pairs={{0,2},{2,0},{4,6},{6,4},{8,10},{10,8},{12,14},{14,12},{16,18},{18,... | collective-permute-start | bytes 1179656 | tf_op jit(solution)/shard_map/ppermute | solution.py:95
  20.1 18.1 %collective-permute-start.7 = (bf16[256,768]{1,0:T(8,128)(2,1)S(1)}, bf16[256,768]{1,0:T(8,128)(2,1)S(1)}, u32[]{:S(2)}, u32[]{:S(2)}) collective-permute-start(bf16[256,768]{1,0:T(8,128)(2,1)S(1)} %pad_maximum_fusion.1.w0), channel_id=1, source_target_pairs={{0,4},{2,6},{4,0},{6,2},{8,12},{10,14},{12,8},{14,10},{16,20},{18,... | collective-permute-start | bytes 1179656 | tf_op jit(solution)/shard_map/ppermute | solution.py:95
  21.6 16.6 %collective-permute-start.8 = (bf16[256,768]{1,0:T(8,128)(2,1)S(1)}, bf16[256,768]{1,0:T(8,128)(2,1)S(1)}, u32[]{:S(2)}, u32[]{:S(2)}) collective-permute-start(bf16[256,768]{1,0:T(8,128)(2,1)S(1)} %pad_maximum_fusion.1.w0), channel_id=1, source_target_pairs={{0,6},{2,4},{4,2},{6,0},{8,14},{10,12},{12,10},{14,8},{16,22},{18,... | collective-permute-start | bytes 1179656 | tf_op jit(solution)/shard_map/ppermute | solution.py:95
  35.3 7.9 %collective-permute-start.15 = (bf16[128,1024]{1,0:T(8,128)(2,1)S(1)}, bf16[128,1024]{1,0:T(8,128)(2,1)S(1)}, u32[]{:S(2)}, u32[]{:S(2)}) collective-permute-start(bf16[128,1024]{1,0:T(8,128)(2,1)S(1)} %pad_maximum_fusion.2), channel_id=1, source_target_pairs={{0,8},{2,10},{4,12},{6,14},{8,0},{10,2},{12,4},{14,6},{16,24},{18,... | collective-permute-start | bytes 786440 | tf_op jit(solution)/shard_map/ppermute | solution.py:89
  38.2 8.3 %collective-permute-start.11 = (bf16[256,256]{1,0:T(8,128)(2,1)S(1)}, bf16[256,256]{1,0:T(8,128)(2,1)S(1)}, u32[]{:S(2)}, u32[]{:S(2)}) collective-permute-start(bf16[256,256]{1,0:T(8,128)(2,1)S(1)} %pad_maximum_fusion.3.w0), channel_id=1, source_target_pairs={{0,2},{2,0},{4,6},{6,4},{8,10},{10,8},{12,14},{14,12},{16,18},{18,... | collective-permute-start | bytes 393224 | tf_op jit(solution)/shard_map/ppermute | solution.py:95
  39.4 7.8 %collective-permute-start.12 = (bf16[256,256]{1,0:T(8,128)(2,1)S(1)}, bf16[256,256]{1,0:T(8,128)(2,1)S(1)}, u32[]{:S(2)}, u32[]{:S(2)}) collective-permute-start(bf16[256,256]{1,0:T(8,128)(2,1)S(1)} %pad_maximum_fusion.3.w0), channel_id=1, source_target_pairs={{0,4},{2,6},{4,0},{6,2},{8,12},{10,14},{12,8},{14,10},{16,20},{18,... | collective-permute-start | bytes 393224 | tf_op jit(solution)/shard_map/ppermute | solution.py:95
  40.5 6.7 %collective-permute-start.13 = (bf16[256,256]{1,0:T(8,128)(2,1)S(1)}, bf16[256,256]{1,0:T(8,128)(2,1)S(1)}, u32[]{:S(2)}, u32[]{:S(2)}) collective-permute-start(bf16[256,256]{1,0:T(8,128)(2,1)S(1)} %pad_maximum_fusion.3.w0), channel_id=1, source_target_pairs={{0,6},{2,4},{4,2},{6,0},{8,14},{10,12},{12,10},{14,8},{16,22},{18,... | collective-permute-start | bytes 393224 | tf_op jit(solution)/shard_map/ppermute | solution.py:95
  47.3 15.0 %collective-permute-start.18 = (bf16[256,1024]{1,0:T(8,128)(2,1)S(1)}, bf16[256,1024]{1,0:T(8,128)(2,1)S(1)}, u32[]{:S(2)}, u32[]{:S(2)}) collective-permute-start(bf16[256,1024]{1,0:T(8,128)(2,1)S(1)} %pad_maximum_fusion.refs_0_), channel_id=1, source_target_pairs={{0,2},{2,0},{4,6},{6,4},{8,10},{10,8},{12,14},{14,12},{16,18},{18,... | collective-permute-start | bytes 1572872 | tf_op jit(solution)/shard_map/ppermute | solution.py:100
  48.5 16.8 %collective-permute-start.19 = (bf16[256,1024]{1,0:T(8,128)(2,1)S(1)}, bf16[256,1024]{1,0:T(8,128)(2,1)S(1)}, u32[]{:S(2)}, u32[]{:S(2)}) collective-permute-start(bf16[256,1024]{1,0:T(8,128)(2,1)S(1)} %pad_maximum_fusion.refs_0_), channel_id=1, source_target_pairs={{0,4},{2,6},{4,0},{6,2},{8,12},{10,14},{12,8},{14,10},{16,20},{18,... | collective-permute-start | bytes 1572872 | tf_op jit(solution)/shard_map/ppermute | solution.py:100
  52.9 26.2 %all-to-all-start = ((bf16[16,16,1024]{2,1,0:T(8,128)(2,1)}), bf16[16,16,1024]{2,1,0:T(8,128)(2,1)}, u32[]{:S(2)}, u32[]{:S(2)}) async-start(bf16[16,16,1024]{2,1,0:T(8,128)(2,1)} %bitcast.4), calls=%async_computation | async-start | bytes 1048576 | tf_op jit(solution)/shard_map/all_to_all | solution.py:459
  65.3 11.3 %collective-permute-start.22 = (bf16[256,1024]{1,0:T(8,128)(2,1)S(1)}, bf16[256,1024]{1,0:T(8,128)(2,1)S(1)}, u32[]{:S(2)}, u32[]{:S(2)}) collective-permute-start(bf16[256,1024]{1,0:T(8,128)(2,1)S(1)} %pad_maximum_fusion.refs_0_), channel_id=1, source_target_pairs={{0,1},{1,0},{2,3},{3,2},{4,5},{5,4},{6,7},{7,6},{8,9},{9,8},{10,11... | collective-permute-start | bytes 1572872 | tf_op jit(solution)/shard_map/ppermute | solution.py:23
  65.3 10.3 %collective-permute-start.20 = (bf16[128,1024]{1,0:T(8,128)(2,1)S(1)}, bf16[128,1024]{1,0:T(8,128)(2,1)S(1)}, u32[]{:S(2)}, u32[]{:S(2)}) collective-permute-start(bf16[128,1024]{1,0:T(8,128)(2,1)S(1)} %slice.45), channel_id=1, source_target_pairs={{0,2},{2,0},{4,6},{6,4},{8,10},{10,8},{12,14},{14,12},{16,18},{18,... | collective-permute-start | bytes 786440 | tf_op jit(solution)/shard_map/ppermute | solution.py:100
  66.7 11.7 %collective-permute-start.23 = (bf16[256,1024]{1,0:T(8,128)(2,1)S(1)}, bf16[256,1024]{1,0:T(8,128)(2,1)S(1)}, u32[]{:S(2)}, u32[]{:S(2)}) collective-permute-start(bf16[256,1024]{1,0:T(8,128)(2,1)S(1)} %collective-permute-done.18.refs_1_), channel_id=1, source_target_pairs={{0,1},{1,0},{2,3},{3,2},{4,5},{5,4},{6,7},{7,6},{8,9},{9,8},{10,11... | collective-permute-start | bytes 1572872 | tf_op jit(solution)/shard_map/ppermute | solution.py:23
  66.9 11.5 %collective-permute-start.24 = (bf16[256,1024]{1,0:T(8,128)(2,1)S(1)}, bf16[256,1024]{1,0:T(8,128)(2,1)S(1)}, u32[]{:S(2)}, u32[]{:S(2)}) collective-permute-start(bf16[256,1024]{1,0:T(8,128)(2,1)S(1)} %collective-permute-done.19.refs_2_), channel_id=1, source_target_pairs={{0,1},{1,0},{2,3},{3,2},{4,5},{5,4},{6,7},{7,6},{8,9},{9,8},{10,11... | collective-permute-start | bytes 1572872 | tf_op jit(solution)/shard_map/ppermute | solution.py:23
  67.2 9.4 %collective-permute-start.21 = (bf16[128,1024]{1,0:T(8,128)(2,1)S(1)}, bf16[128,1024]{1,0:T(8,128)(2,1)S(1)}, u32[]{:S(2)}, u32[]{:S(2)}) collective-permute-start(bf16[128,1024]{1,0:T(8,128)(2,1)S(1)} %slice.46), channel_id=1, source_target_pairs={{0,4},{2,6},{4,0},{6,2},{8,12},{10,14},{12,8},{14,10},{16,20},{18,... | collective-permute-start | bytes 786440 | tf_op jit(solution)/shard_map/ppermute | solution.py:100
  76.6 9.6 %collective-permute-start.27 = (bf16[128,512]{1,0:T(8,128)(2,1)S(1)}, bf16[128,512]{1,0:T(8,128)(2,1)S(1)}, u32[]{:S(2)}, u32[]{:S(2)}) collective-permute-start(bf16[128,512]{1,0:T(8,128)(2,1)S(1)} %pad_maximum_fusion.4), channel_id=1, source_target_pairs={{0,16},{2,18},{4,20},{6,22},{8,24},{10,26},{12,28},{14,30},{16,0},... | collective-permute-start | bytes 393224 | tf_op jit(solution)/shard_map/ppermute | solution.py:396
  86.2 14.9 %all-to-all-start.1 = ((bf16[16,16,512]{2,1,0:T(8,128)(2,1)}), bf16[16,16,512]{2,1,0:T(8,128)(2,1)S(1)}, u32[]{:S(2)}, u32[]{:S(2)}) async-start(bf16[16,16,512]{2,1,0:T(8,128)(2,1)} %bitcast.15), calls=%async_computation.1 | async-start | bytes 524288 | tf_op jit(solution)/shard_map/all_to_all | solution.py:478
  (27 other events, 248.7 us)

commit v6 on v5

--- a/solution.py
+++ b/solution.py
@@ -37,13 +37,14 @@
     cost=2**10,
     room=24,
     space=pltpu.VMEM,
+    given_space=pltpu.HBM,
 ):
     return pl.pallas_call(
         kernel,
         out_shape=out,
         in_specs=[SCALARS] * len(scalars)
         + [pl.BlockSpec(memory_space=pltpu.VMEM)] * len(arrays)
-        + [pl.BlockSpec(memory_space=pltpu.HBM)] * len(given),
+        + [pl.BlockSpec(memory_space=given_space)] * len(given),
         out_specs=jax.tree.map(lambda _: pl.BlockSpec(memory_space=space), out),
         scratch_shapes=scratch,
         compiler_params=pltpu.CompilerParams(vmem_limit_bytes=room * 2**20),
@@ -306,7 +307,6 @@
     )
     first_copy = bring([(spread, tokens)], token_sem)
     coming = fetch(0)
-    wait(first_copy)
     total = tokens.shape[0]
     block = cols * rows
     lon_count = total // block
@@ -331,6 +331,7 @@
     same = row_of(spot_q) == row_of(spot_k)
     width = weight.shape[2] // 3
     heads = width // HS
+    wait(first_copy)
     for half in range(2):
         first = lax.rem(place[1] + half, 2) * heads
         wait(coming)
@@ -340,6 +341,7 @@
         query = unit_heads(projected[:, :width], 1.0 / math.sqrt(HS))
         keyed = unit_heads(projected[:, width : 2 * width])
         valued = projected[:, 2 * width :].astype(jnp.bfloat16)
+        mixed = []
         for pair in range(width // PAIR):
             lanes = slice(pair * PAIR, (pair + 1) * PAIR)
             bias = jnp.concatenate(
@@ -349,9 +351,9 @@
                 ],
                 axis=0,
             )
-            mixed = two_heads(query[:, lanes], keyed[:, lanes], valued[:, lanes], bias)
-            start = half * width + pair * PAIR
-            out[:, start : start + PAIR] = dot(homeward, mixed).astype(jnp.bfloat16)
+            mixed.append(two_heads(query[:, lanes], keyed[:, lanes], valued[:, lanes], bias))
+        mixed = jnp.concatenate(mixed, axis=1)
+        out[:, half * width : (half + 1) * width] = dot(homeward, mixed).astype(jnp.bfloat16)
 
 
 def final_kernel(mixed, middle, weight, out, *refs):
@@ -472,7 +474,8 @@
         + [pltpu.VMEM((2, *project_shape.shape), jnp.bfloat16)]
         + sems(2, lon_count)
         + sems(1),
-        room=60,
+        room=51,
+        given_space=pl.ANY,
     )
     row_mixed, home = after((row_mixed, home))
     back = lax.all_to_all(row_mixed, "lon", split_axis=0, concat_axis=0, tiled=True)

time: 105 us -> 105 us (level)
  waiting for transfers between devices: 39.2 us -> 40.7 us
  starting transfers between devices: 38 us -> 36.9 us
    unnamed x42 -> x46, local copies, waits for them, and re-layouts: 2.11 us -> 2.08 us
where the time goes in v6:
time: 105 us; the launch traced here: 104 us
  waiting for transfers between devices  40.7 us (39%)
  starting transfers between devices  36.9 us (35%)
  Pallas kernels  21.2 us (20%)
  other arithmetic  2.67 us (3%)
  local copies, waits for them, and re-layouts  2.17 us (2%)
    pallas_call x10, Pallas kernels, call(): pl.pallas_call(kernel, out_shape=out, in_specs=[SCALARS] * len(scalars) +...  21.2 us
    ppermute x4, waiting for transfers between devices, relayed_plane(): lax.ppermute(value, 'lon', at(lambda i: i ^ k, length))  16.1 us
    ppermute x2, waiting for transfers between devices, fast(): lax.ppermute(value, 'lon', at(lambda i: i ^ 2 * PLANE, lon_count))  7.38 us
    ppermute x6, starting transfers between devices, across_plane(): lax.ppermute(part, 'lon', at(lambda i: i ^ k, length))  7.04 us
    ppermute x2, starting transfers between devices, fast(): lax.ppermute(value, 'lon', at(lambda i: i ^ 2 * PLANE, lon_count))  6.45 us
    ppermute x2, waiting for transfers between devices, fast(): lax.ppermute(value, 'lon', at(lambda i: (i + lon_count // 2) % lon_count,...  6.11 us
    ppermute x4, starting transfers between devices, relayed_plane(): lax.ppermute(value, 'lon', at(lambda i: i ^ k, length))  5.32 us
    all_to_all x1, waiting for transfers between devices, fast(): lax.all_to_all(row_mixed, 'lon', split_axis=0, concat_axis=0, tiled=True)  4.94 us
  transfers between devices with their start and end apart: 30, of which 14 were waited for; matrix products, arithmetic and copies ran while one was open for 3% of the time, Pallas kernels for 18%

profile of v6, /device:TPU:0, one launch (start us, length us, event | category | flops | bytes accessed | tf_op | source)
XLA Modules:
  0.0 104.1 jit_solution(6109052014965415197)
XLA Ops:
  0.0 4.1 %collective-permute-start.9 = (bf16[64,256]{1,0:T(8,128)(2,1)}, bf16[64,256]{1,0:T(8,128)(2,1)S(1)}, u32[]{:S(2)}, u32[]{:S(2)}) collective-permute-start(bf16[64,256]{1,0:T(8,128)(2,1)} %param.19), channel_id=1, source_target_pairs={{0,16},{2,18},{4,20},{6,22},{8,24},{10,26},{12,28},{14,30},{16,0},... | collective-permute-start | bytes 98312 | tf_op jit(solution)/shard_map/ppermute | solution.py:401
  4.1 1.6 %collective-permute-start = (bf16[64,768]{1,0:T(8,128)(2,1)}, bf16[64,768]{1,0:T(8,128)(2,1)S(1)}, u32[]{:S(2)}, u32[]{:S(2)}) collective-permute-start(bf16[64,768]{1,0:T(8,128)(2,1)} %param.18), channel_id=1, source_target_pairs={{0,8},{2,10},{4,12},{6,14},{8,0},{10,2},{12,4},{14,6},{16,24},{18,... | collective-permute-start | bytes 294920 | tf_op jit(solution)/shard_map/ppermute | solution.py:86
  6.0 2.5 %collective-permute-start.2 = (bf16[64,768]{1,0:T(8,128)(2,1)}, bf16[64,768]{1,0:T(8,128)(2,1)S(1)}, u32[]{:S(2)}, u32[]{:S(2)}) collective-permute-start(bf16[64,768]{1,0:T(8,128)(2,1)} %param.18), channel_id=1, source_target_pairs={{0,24},{2,26},{4,28},{6,30},{8,16},{10,18},{12,20},{14,22},{16,8},... | collective-permute-start | bytes 294920 | tf_op jit(solution)/shard_map/ppermute | solution.py:86
  9.9 2.3 %loop_tokens.1 = (bf16[144,1024]{1,0:T(8,128)(2,1)}, bf16[144,1024]{1,0:T(8,128)(2,1)}, bf16[64,1024]{1,0:T(8,128)(2,1)}) custom-call(bf16[64,4,1024]{2,1,0:T(4,128)(2,1)} %refs_10_.1, s32[4,64]{1,0:T(4,128)} %bitcast.17, bf16[64,768]{1,0:T(8,128)(2,1)} %project.1, bf16[64,256]{1,0:T(8,128)(2,1)} %output.1), custom_call_target="tpu_custom_call" | custom-call | flops 1024 | bytes 1024 | tf_op jit(solution)/shard_map/loop_tokens/pallas_call | solution.py:42
  12.3 2.3 %collective-permute-start.14 = (bf16[64,1024]{1,0:T(8,128)(2,1)}, bf16[64,1024]{1,0:T(8,128)(2,1)S(1)}, u32[]{:S(2)}, u32[]{:S(2)}) collective-permute-start(bf16[64,1024]{1,0:T(8,128)(2,1)} %get-tuple-element.45), channel_id=1, source_target_pairs={{0,16},{2,18},{4,20},{6,22},{8,24},{10,26},{12,28},{14,30},{16,0},... | collective-permute-start | bytes 393224 | tf_op jit(solution)/shard_map/ppermute | solution.py:401
  15.4 2.2 %collective-permute-start.3 = (bf16[144,1024]{1,0:T(8,128)(2,1)}, bf16[144,1024]{1,0:T(8,128)(2,1)S(1)}, u32[]{:S(2)}, u32[]{:S(2)}) collective-permute-start(bf16[144,1024]{1,0:T(8,128)(2,1)} %get-tuple-element.38), channel_id=1, source_target_pairs={{0,16},{2,18},{4,20},{6,22},{8,24},{10,26},{12,28},{14,30},{16,0},... | collective-permute-start | bytes 884744 | tf_op jit(solution)/shard_map/ppermute | solution.py:398
  18.5 1.6 %collective-permute-start.6 = (bf16[256,768]{1,0:T(8,128)(2,1)S(1)}, bf16[256,768]{1,0:T(8,128)(2,1)S(1)}, u32[]{:S(2)}, u32[]{:S(2)}) collective-permute-start(bf16[256,768]{1,0:T(8,128)(2,1)S(1)} %pad_maximum_fusion.1.w0), channel_id=1, source_target_pairs={{0,2},{2,0},{4,6},{6,4},{8,10},{10,8},{12,14},{14,12},{16,18},{18,... | collective-permute-start | bytes 1179656 | tf_op jit(solution)/shard_map/ppermute | solution.py:96
  20.1 1.5 %collective-permute-start.7 = (bf16[256,768]{1,0:T(8,128)(2,1)S(1)}, bf16[256,768]{1,0:T(8,128)(2,1)S(1)}, u32[]{:S(2)}, u32[]{:S(2)}) collective-permute-start(bf16[256,768]{1,0:T(8,128)(2,1)S(1)} %pad_maximum_fusion.1.w0), channel_id=1, source_target_pairs={{0,4},{2,6},{4,0},{6,2},{8,12},{10,14},{12,8},{14,10},{16,20},{18,... | collective-permute-start | bytes 1179656 | tf_op jit(solution)/shard_map/ppermute | solution.py:96
  22.1 7.4 %collective-permute-done.14 = bf16[64,1024]{1,0:T(8,128)(2,1)S(1)} collective-permute-done((bf16[64,1024]{1,0:T(8,128)(2,1)}, bf16[64,1024]{1,0:T(8,128)(2,1)S(1)}, u32[]{:S(2)}, u32[]{:S(2)}) %collective-permute-start.14) | collective-permute-done | bytes 131104 | tf_op jit(solution)/shard_map/ppermute | solution.py:401
  30.4 5.0 %collective-permute-done.3.own.got = bf16[144,1024]{1,0:T(8,128)(2,1)S(1)} collective-permute-done((bf16[144,1024]{1,0:T(8,128)(2,1)}, bf16[144,1024]{1,0:T(8,128)(2,1)S(1)}, u32[]{:S(2)}, u32[]{:S(2)}) %collective-permute-start.3) | collective-permute-done | bytes 294944 | tf_op jit(solution)/shard_map/ppermute | solution.py:398
  41.7 1.6 %collective-permute-done.15 = bf16[128,1024]{1,0:T(8,128)(2,1)S(1)} collective-permute-done((bf16[128,1024]{1,0:T(8,128)(2,1)S(1)}, bf16[128,1024]{1,0:T(8,128)(2,1)S(1)}, u32[]{:S(2)}, u32[]{:S(2)}) %collective-permute-start.15) | collective-permute-done | bytes 262176 | tf_op jit(solution)/shard_map/ppermute | solution.py:90
  44.0 2.5 %column_attention.1 = (bf16[256,256]{1,0:T(8,128)(2,1)S(1)}, bf16[256,256]{1,0:T(8,128)(2,1)S(1)}) custom-call(f32[8]{0:T(128)S(1)} %copy-done.15, bf16[256,1024]{1,0:T(8,128)(2,1)S(1)} %column_normed.1.tokens, bf16[256,1024]{1,0:T(8,128)(2,1)S(1)} %far_normed.1.far_tokens, bf16[1024,768]{1,0:T(8,128)(2,1)S(1)} %column_project.1.weight), custom_call_target="tpu_custom_call" | custom-call | flops 1024 | bytes 262144 | tf_op jit(solution)/shard_map/column_attention/pallas_call | solution.py:42
  51.2 1.8 %row_normed.1 = bf16[256,1024]{1,0:T(8,128)(2,1)} custom-call(bf16[256,256]{1,0:T(8,128)(2,1)S(1)} %get-tuple-element.54.mine, bf16[256,256]{1,0:T(8,128)(2,1)S(1)} %collective-permute-done.16.theirs, bf16[1024,256]{1,0:T(8,128)(2,1)S(1)} %column_output.1.near, bf16[1024,256]{1,0:T(8,128)(2,1)S(1)} %collective-permute-done.17.far, ...), custom_call_target="tpu_custom_call" | custom-call | flops 1024 | bytes 1048576 | tf_op jit(solution)/shard_map/row_normed/pallas_call | solution.py:42
  53.0 4.1 %all-to-all-start = ((bf16[16,16,1024]{2,1,0:T(8,128)(2,1)}), bf16[16,16,1024]{2,1,0:T(8,128)(2,1)S(1)}, u32[]{:S(2)}, u32[]{:S(2)}) async-start(bf16[16,16,1024]{2,1,0:T(8,128)(2,1)} %bitcast.4), calls=%async_computation | async-start | bytes 1048576 | tf_op jit(solution)/shard_map/all_to_all | solution.py:461
  57.1 5.4 %collective-permute-done.18.refs_1_ = bf16[256,1024]{1,0:T(8,128)(2,1)S(1)} collective-permute-done((bf16[256,1024]{1,0:T(8,128)(2,1)S(1)}, bf16[256,1024]{1,0:T(8,128)(2,1)S(1)}, u32[]{:S(2)}, u32[]{:S(2)}) %collective-permute-start.18) | collective-permute-done | bytes 524320 | tf_op jit(solution)/shard_map/ppermute | solution.py:101
  62.5 3.1 %collective-permute-done.19.refs_2_ = bf16[256,1024]{1,0:T(8,128)(2,1)S(1)} collective-permute-done((bf16[256,1024]{1,0:T(8,128)(2,1)S(1)}, bf16[256,1024]{1,0:T(8,128)(2,1)S(1)}, u32[]{:S(2)}, u32[]{:S(2)}) %collective-permute-start.19) | collective-permute-done | bytes 524320 | tf_op jit(solution)/shard_map/ppermute | solution.py:101
  67.5 1.6 %collective-permute-start.21 = (bf16[128,1024]{1,0:T(8,128)(2,1)S(1)}, bf16[128,1024]{1,0:T(8,128)(2,1)S(1)}, u32[]{:S(2)}, u32[]{:S(2)}) collective-permute-start(bf16[128,1024]{1,0:T(8,128)(2,1)S(1)} %slice.46), channel_id=1, source_target_pairs={{0,4},{2,6},{4,0},{6,2},{8,12},{10,14},{12,8},{14,10},{16,20},{18,... | collective-permute-start | bytes 786440 | tf_op jit(solution)/shard_map/ppermute | solution.py:101
  69.1 6.5 %collective-permute-done.20.refs_3_ = bf16[128,1024]{1,0:T(8,128)(2,1)S(1)} collective-permute-done((bf16[128,1024]{1,0:T(8,128)(2,1)S(1)}, bf16[128,1024]{1,0:T(8,128)(2,1)S(1)}, u32[]{:S(2)}, u32[]{:S(2)}) %collective-permute-start.20) | collective-permute-done | bytes 262176 | tf_op jit(solution)/shard_map/ppermute | solution.py:101
  76.7 1.8 %collective-permute-start.27 = (bf16[128,512]{1,0:T(8,128)(2,1)S(1)}, bf16[128,512]{1,0:T(8,128)(2,1)S(1)}, u32[]{:S(2)}, u32[]{:S(2)}) collective-permute-start(bf16[128,512]{1,0:T(8,128)(2,1)S(1)} %pad_maximum_fusion.4), channel_id=1, source_target_pairs={{0,16},{2,18},{4,20},{6,22},{8,24},{10,26},{12,28},{14,30},{16,0},... | collective-permute-start | bytes 393224 | tf_op jit(solution)/shard_map/ppermute | solution.py:398
  79.5 5.6 %row_attention.1 = bf16[256,512]{1,0:T(8,128)(2,1)} custom-call(f32[8]{0:T(128)S(1)} %copy-done.14, bf16[256,1024]{1,0:T(8,128)(2,1)S(1)} %bitcast.8, bf16[256,1024]{1,0:T(8,128)(2,1)S(1)} %pad_maximum_fusion.refs_0_, bf16[256,1024]{1,0:T(8,128)(2,1)S(1)} %collective-permute-done.18.refs_1_, bf16[256,1024]{1,0:T(8,128)(2,1)} %copy-done.16, ...), custom_call_target="tpu_custom_call" | custom-call | flops 1024 | bytes 1024 | tf_op jit(solution)/shard_map/row_attention/pallas_call | solution.py:42
  86.3 4.3 %all-to-all-start.1 = ((bf16[16,16,512]{2,1,0:T(8,128)(2,1)}), bf16[16,16,512]{2,1,0:T(8,128)(2,1)S(1)}, u32[]{:S(2)}, u32[]{:S(2)}) async-start(bf16[16,16,512]{2,1,0:T(8,128)(2,1)} %bitcast.6), calls=%async_computation.1 | async-start | bytes 524288 | tf_op jit(solution)/shard_map/all_to_all | solution.py:481
  90.6 5.0 %middle.1 = (f32[256,1024]{1,0:T(8,128)}, bf16[2,1024,256]{2,1,0:T(8,128)(2,1)}) custom-call(bf16[256,256]{1,0:T(8,128)(2,1)} %copy-done.9, bf16[256,256]{1,0:T(8,128)(2,1)} %copy-done.10, bf16[128,512]{1,0:T(8,128)(2,1)} %copy-done.21, bf16[1024,256]{1,0:T(8,128)(2,1)} %copy-done.1, bf16[1024,256]{1,0:T(8,128)(2,1)} %copy-done.3, ...), custom_call_target="tpu_custom_call" | custom-call | flops 1024 | bytes 1024 | tf_op jit(solution)/shard_map/middle/pallas_call | solution.py:42
  95.7 4.9 %all-to-all-done.1 = bf16[16,16,512]{2,1,0:T(8,128)(2,1)S(1)} async-done(((bf16[16,16,512]{2,1,0:T(8,128)(2,1)}), bf16[16,16,512]{2,1,0:T(8,128)(2,1)S(1)}, u32[]{:S(2)}, u32[]{:S(2)}) %all-to-all-start.1) | async-done | bytes 262176 | tf_op jit(solution)/shard_map/all_to_all | solution.py:481
  101.3 2.8 %block_output.1 = bf16[64,4,1024]{2,1,0:T(4,128)(2,1)} custom-call(bf16[256,512]{1,0:T(8,128)(2,1)} %bitcast.16, f32[256,1024]{1,0:T(8,128)} %get-tuple-element.67.middle, bf16[2,1024,256]{2,1,0:T(8,128)(2,1)} %get-tuple-element.68.weight), custom_call_target="tpu_custom_call" | custom-call | flops 1024 | bytes 1024 | tf_op jit(solution)/shard_map/block_output/pallas_call | solution.py:42
  (105 shorter events, 22.3 us)
Async XLA Ops:
  0.0 8.5 %collective-permute-start.9 = (bf16[64,256]{1,0:T(8,128)(2,1)}, bf16[64,256]{1,0:T(8,128)(2,1)S(1)}, u32[]{:S(2)}, u32[]{:S(2)}) collective-permute-start(bf16[64,256]{1,0:T(8,128)(2,1)} %param.19), channel_id=1, source_target_pairs={{0,16},{2,18},{4,20},{6,22},{8,24},{10,26},{12,28},{14,30},{16,0},... | collective-permute-start | bytes 98312 | tf_op jit(solution)/shard_map/ppermute | solution.py:401
  4.1 8.2 %collective-permute-start = (bf16[64,768]{1,0:T(8,128)(2,1)}, bf16[64,768]{1,0:T(8,128)(2,1)S(1)}, u32[]{:S(2)}, u32[]{:S(2)}) collective-permute-start(bf16[64,768]{1,0:T(8,128)(2,1)} %param.18), channel_id=1, source_target_pairs={{0,8},{2,10},{4,12},{6,14},{8,0},{10,2},{12,4},{14,6},{16,24},{18,... | collective-permute-start | bytes 294920 | tf_op jit(solution)/shard_map/ppermute | solution.py:86
  5.7 9.7 %collective-permute-start.1 = (bf16[64,768]{1,0:T(8,128)(2,1)}, bf16[64,768]{1,0:T(8,128)(2,1)S(1)}, u32[]{:S(2)}, u32[]{:S(2)}) collective-permute-start(bf16[64,768]{1,0:T(8,128)(2,1)} %param.18), channel_id=1, source_target_pairs={{0,16},{2,18},{4,20},{6,22},{8,24},{10,26},{12,28},{14,30},{16,0},... | collective-permute-start | bytes 294920 | tf_op jit(solution)/shard_map/ppermute | solution.py:86
  6.0 9.4 %collective-permute-start.2 = (bf16[64,768]{1,0:T(8,128)(2,1)}, bf16[64,768]{1,0:T(8,128)(2,1)S(1)}, u32[]{:S(2)}, u32[]{:S(2)}) collective-permute-start(bf16[64,768]{1,0:T(8,128)(2,1)} %param.18), channel_id=1, source_target_pairs={{0,24},{2,26},{4,28},{6,30},{8,16},{10,18},{12,20},{14,22},{16,8},... | collective-permute-start | bytes 294920 | tf_op jit(solution)/shard_map/ppermute | solution.py:86
  9.3 8.3 %collective-permute-start.10 = (bf16[128,256]{1,0:T(8,128)(2,1)S(1)}, bf16[128,256]{1,0:T(8,128)(2,1)S(1)}, u32[]{:S(2)}, u32[]{:S(2)}) collective-permute-start(bf16[128,256]{1,0:T(8,128)(2,1)S(1)} %pad_maximum_fusion.5), channel_id=1, source_target_pairs={{0,8},{2,10},{4,12},{6,14},{8,0},{10,2},{12,4},{14,6},{16,24},{18,... | collective-permute-start | bytes 196616 | tf_op jit(solution)/shard_map/ppermute | solution.py:90
  12.3 17.1 %collective-permute-start.14 = (bf16[64,1024]{1,0:T(8,128)(2,1)}, bf16[64,1024]{1,0:T(8,128)(2,1)S(1)}, u32[]{:S(2)}, u32[]{:S(2)}) collective-permute-start(bf16[64,1024]{1,0:T(8,128)(2,1)} %get-tuple-element.45), channel_id=1, source_target_pairs={{0,16},{2,18},{4,20},{6,22},{8,24},{10,26},{12,28},{14,30},{16,0},... | collective-permute-start | bytes 393224 | tf_op jit(solution)/shard_map/ppermute | solution.py:401
  15.4 19.9 %collective-permute-start.3 = (bf16[144,1024]{1,0:T(8,128)(2,1)}, bf16[144,1024]{1,0:T(8,128)(2,1)S(1)}, u32[]{:S(2)}, u32[]{:S(2)}) collective-permute-start(bf16[144,1024]{1,0:T(8,128)(2,1)} %get-tuple-element.38), channel_id=1, source_target_pairs={{0,16},{2,18},{4,20},{6,22},{8,24},{10,26},{12,28},{14,30},{16,0},... | collective-permute-start | bytes 884744 | tf_op jit(solution)/shard_map/ppermute | solution.py:398
  18.5 18.9 %collective-permute-start.6 = (bf16[256,768]{1,0:T(8,128)(2,1)S(1)}, bf16[256,768]{1,0:T(8,128)(2,1)S(1)}, u32[]{:S(2)}, u32[]{:S(2)}) collective-permute-start(bf16[256,768]{1,0:T(8,128)(2,1)S(1)} %pad_maximum_fusion.1.w0), channel_id=1, source_target_pairs={{0,2},{2,0},{4,6},{6,4},{8,10},{10,8},{12,14},{14,12},{16,18},{18,... | collective-permute-start | bytes 1179656 | tf_op jit(solution)/shard_map/ppermute | solution.py:96
  20.1 18.1 %collective-permute-start.7 = (bf16[256,768]{1,0:T(8,128)(2,1)S(1)}, bf16[256,768]{1,0:T(8,128)(2,1)S(1)}, u32[]{:S(2)}, u32[]{:S(2)}) collective-permute-start(bf16[256,768]{1,0:T(8,128)(2,1)S(1)} %pad_maximum_fusion.1.w0), channel_id=1, source_target_pairs={{0,4},{2,6},{4,0},{6,2},{8,12},{10,14},{12,8},{14,10},{16,20},{18,... | collective-permute-start | bytes 1179656 | tf_op jit(solution)/shard_map/ppermute | solution.py:96
  21.6 16.6 %collective-permute-start.8 = (bf16[256,768]{1,0:T(8,128)(2,1)S(1)}, bf16[256,768]{1,0:T(8,128)(2,1)S(1)}, u32[]{:S(2)}, u32[]{:S(2)}) collective-permute-start(bf16[256,768]{1,0:T(8,128)(2,1)S(1)} %pad_maximum_fusion.1.w0), channel_id=1, source_target_pairs={{0,6},{2,4},{4,2},{6,0},{8,14},{10,12},{12,10},{14,8},{16,22},{18,... | collective-permute-start | bytes 1179656 | tf_op jit(solution)/shard_map/ppermute | solution.py:96
  35.3 7.9 %collective-permute-start.15 = (bf16[128,1024]{1,0:T(8,128)(2,1)S(1)}, bf16[128,1024]{1,0:T(8,128)(2,1)S(1)}, u32[]{:S(2)}, u32[]{:S(2)}) collective-permute-start(bf16[128,1024]{1,0:T(8,128)(2,1)S(1)} %pad_maximum_fusion.2), channel_id=1, source_target_pairs={{0,8},{2,10},{4,12},{6,14},{8,0},{10,2},{12,4},{14,6},{16,24},{18,... | collective-permute-start | bytes 786440 | tf_op jit(solution)/shard_map/ppermute | solution.py:90
  38.2 8.4 %collective-permute-start.11 = (bf16[256,256]{1,0:T(8,128)(2,1)S(1)}, bf16[256,256]{1,0:T(8,128)(2,1)S(1)}, u32[]{:S(2)}, u32[]{:S(2)}) collective-permute-start(bf16[256,256]{1,0:T(8,128)(2,1)S(1)} %pad_maximum_fusion.3.w0), channel_id=1, source_target_pairs={{0,2},{2,0},{4,6},{6,4},{8,10},{10,8},{12,14},{14,12},{16,18},{18,... | collective-permute-start | bytes 393224 | tf_op jit(solution)/shard_map/ppermute | solution.py:96
  39.4 7.8 %collective-permute-start.12 = (bf16[256,256]{1,0:T(8,128)(2,1)S(1)}, bf16[256,256]{1,0:T(8,128)(2,1)S(1)}, u32[]{:S(2)}, u32[]{:S(2)}) collective-permute-start(bf16[256,256]{1,0:T(8,128)(2,1)S(1)} %pad_maximum_fusion.3.w0), channel_id=1, source_target_pairs={{0,4},{2,6},{4,0},{6,2},{8,12},{10,14},{12,8},{14,10},{16,20},{18,... | collective-permute-start | bytes 393224 | tf_op jit(solution)/shard_map/ppermute | solution.py:96
  40.5 6.7 %collective-permute-start.13 = (bf16[256,256]{1,0:T(8,128)(2,1)S(1)}, bf16[256,256]{1,0:T(8,128)(2,1)S(1)}, u32[]{:S(2)}, u32[]{:S(2)}) collective-permute-start(bf16[256,256]{1,0:T(8,128)(2,1)S(1)} %pad_maximum_fusion.3.w0), channel_id=1, source_target_pairs={{0,6},{2,4},{4,2},{6,0},{8,14},{10,12},{12,10},{14,8},{16,22},{18,... | collective-permute-start | bytes 393224 | tf_op jit(solution)/shard_map/ppermute | solution.py:96
  47.3 15.2 %collective-permute-start.18 = (bf16[256,1024]{1,0:T(8,128)(2,1)S(1)}, bf16[256,1024]{1,0:T(8,128)(2,1)S(1)}, u32[]{:S(2)}, u32[]{:S(2)}) collective-permute-start(bf16[256,1024]{1,0:T(8,128)(2,1)S(1)} %pad_maximum_fusion.refs_0_), channel_id=1, source_target_pairs={{0,2},{2,0},{4,6},{6,4},{8,10},{10,8},{12,14},{14,12},{16,18},{18,... | collective-permute-start | bytes 1572872 | tf_op jit(solution)/shard_map/ppermute | solution.py:101
  48.5 17.1 %collective-permute-start.19 = (bf16[256,1024]{1,0:T(8,128)(2,1)S(1)}, bf16[256,1024]{1,0:T(8,128)(2,1)S(1)}, u32[]{:S(2)}, u32[]{:S(2)}) collective-permute-start(bf16[256,1024]{1,0:T(8,128)(2,1)S(1)} %pad_maximum_fusion.refs_0_), channel_id=1, source_target_pairs={{0,4},{2,6},{4,0},{6,2},{8,12},{10,14},{12,8},{14,10},{16,20},{18,... | collective-permute-start | bytes 1572872 | tf_op jit(solution)/shard_map/ppermute | solution.py:101
  53.0 26.5 %all-to-all-start = ((bf16[16,16,1024]{2,1,0:T(8,128)(2,1)}), bf16[16,16,1024]{2,1,0:T(8,128)(2,1)S(1)}, u32[]{:S(2)}, u32[]{:S(2)}) async-start(bf16[16,16,1024]{2,1,0:T(8,128)(2,1)} %bitcast.4), calls=%async_computation | async-start | bytes 1048576 | tf_op jit(solution)/shard_map/all_to_all | solution.py:461
  65.7 11.0 %collective-permute-start.22 = (bf16[256,1024]{1,0:T(8,128)(2,1)S(1)}, bf16[256,1024]{1,0:T(8,128)(2,1)S(1)}, u32[]{:S(2)}, u32[]{:S(2)}) collective-permute-start(bf16[256,1024]{1,0:T(8,128)(2,1)S(1)} %pad_maximum_fusion.refs_0_), channel_id=1, source_target_pairs={{0,1},{1,0},{2,3},{3,2},{4,5},{5,4},{6,7},{7,6},{8,9},{9,8},{10,11... | collective-permute-start | bytes 1572872 | tf_op jit(solution)/shard_map/ppermute | solution.py:23
  65.7 9.9 %collective-permute-start.20 = (bf16[128,1024]{1,0:T(8,128)(2,1)S(1)}, bf16[128,1024]{1,0:T(8,128)(2,1)S(1)}, u32[]{:S(2)}, u32[]{:S(2)}) collective-permute-start(bf16[128,1024]{1,0:T(8,128)(2,1)S(1)} %slice.45), channel_id=1, source_target_pairs={{0,2},{2,0},{4,6},{6,4},{8,10},{10,8},{12,14},{14,12},{16,18},{18,... | collective-permute-start | bytes 786440 | tf_op jit(solution)/shard_map/ppermute | solution.py:101
  66.9 11.6 %collective-permute-start.23 = (bf16[256,1024]{1,0:T(8,128)(2,1)S(1)}, bf16[256,1024]{1,0:T(8,128)(2,1)S(1)}, u32[]{:S(2)}, u32[]{:S(2)}) collective-permute-start(bf16[256,1024]{1,0:T(8,128)(2,1)S(1)} %collective-permute-done.18.refs_1_), channel_id=1, source_target_pairs={{0,1},{1,0},{2,3},{3,2},{4,5},{5,4},{6,7},{7,6},{8,9},{9,8},{10,11... | collective-permute-start | bytes 1572872 | tf_op jit(solution)/shard_map/ppermute | solution.py:23
  67.2 11.3 %collective-permute-start.24 = (bf16[256,1024]{1,0:T(8,128)(2,1)S(1)}, bf16[256,1024]{1,0:T(8,128)(2,1)S(1)}, u32[]{:S(2)}, u32[]{:S(2)}) collective-permute-start(bf16[256,1024]{1,0:T(8,128)(2,1)S(1)} %collective-permute-done.19.refs_2_), channel_id=1, source_target_pairs={{0,1},{1,0},{2,3},{3,2},{4,5},{5,4},{6,7},{7,6},{8,9},{9,8},{10,11... | collective-permute-start | bytes 1572872 | tf_op jit(solution)/shard_map/ppermute | solution.py:23
  67.5 9.2 %collective-permute-start.21 = (bf16[128,1024]{1,0:T(8,128)(2,1)S(1)}, bf16[128,1024]{1,0:T(8,128)(2,1)S(1)}, u32[]{:S(2)}, u32[]{:S(2)}) collective-permute-start(bf16[128,1024]{1,0:T(8,128)(2,1)S(1)} %slice.46), channel_id=1, source_target_pairs={{0,4},{2,6},{4,0},{6,2},{8,12},{10,14},{12,8},{14,10},{16,20},{18,... | collective-permute-start | bytes 786440 | tf_op jit(solution)/shard_map/ppermute | solution.py:101
  76.7 9.6 %collective-permute-start.27 = (bf16[128,512]{1,0:T(8,128)(2,1)S(1)}, bf16[128,512]{1,0:T(8,128)(2,1)S(1)}, u32[]{:S(2)}, u32[]{:S(2)}) collective-permute-start(bf16[128,512]{1,0:T(8,128)(2,1)S(1)} %pad_maximum_fusion.4), channel_id=1, source_target_pairs={{0,16},{2,18},{4,20},{6,22},{8,24},{10,26},{12,28},{14,30},{16,0},... | collective-permute-start | bytes 393224 | tf_op jit(solution)/shard_map/ppermute | solution.py:398
  86.3 14.3 %all-to-all-start.1 = ((bf16[16,16,512]{2,1,0:T(8,128)(2,1)}), bf16[16,16,512]{2,1,0:T(8,128)(2,1)S(1)}, u32[]{:S(2)}, u32[]{:S(2)}) async-start(bf16[16,16,512]{2,1,0:T(8,128)(2,1)} %bitcast.6), calls=%async_computation.1 | async-start | bytes 524288 | tf_op jit(solution)/shard_map/all_to_all | solution.py:481
  (29 other events, 317.2 us)

commit v7 on v6

--- a/solution.py
+++ b/solution.py
@@ -358,12 +358,16 @@
 
 def final_kernel(mixed, middle, weight, out, *refs):
     *held, staged, sems = refs
-    coming = bring(zip((mixed, weight, middle), held), sems)
+    mixed_held, weight_held, middle_held = held
+    halves = [(weight.at[half], weight_held.at[half]) for half in range(2)]
+    coming = bring([(mixed, mixed_held), *halves, (middle, middle_held)], sems)
     mixed, weight, middle = held
     width = weight.shape[2]
     wait(coming[:2])
-    update = dot_t(mixed[:, :width], weight[0]) + dot_t(mixed[:, width:], weight[1])
-    wait(coming[2:])
+    update = dot_t(mixed[:, :width], weight[0])
+    wait(coming[2:3])
+    update += dot_t(mixed[:, width:], weight[1])
+    wait(coming[3:])
     staged[...] = (middle[...] + update).reshape(out.shape).astype(jnp.bfloat16)
     wait(bring([(staged, out)], sems))
 
@@ -494,7 +498,7 @@
         bf16(band, cols, width),
         "block_output",
         given=(back, middle, row_out),
-        scratch=vmem(back, row_out, middle) + [pltpu.VMEM(fields.shape, jnp.bfloat16)] + sems(3),
+        scratch=vmem(back, row_out, middle) + [pltpu.VMEM(fields.shape, jnp.bfloat16)] + sems(4),
         room=60,
         space=pltpu.HBM,
     )

time: 105 us -> 105 us (level)
  no operation moved by 1% of the time
where the time goes in v7:
time: 105 us; the launch traced here: 104 us
  waiting for transfers between devices  40.7 us (39%)
  starting transfers between devices  36.9 us (35%)
  Pallas kernels  21.2 us (20%)
  other arithmetic  2.67 us (3%)
  local copies, waits for them, and re-layouts  2.17 us (2%)
    pallas_call x10, Pallas kernels, call(): pl.pallas_call(kernel, out_shape=out, in_specs=[SCALARS] * len(scalars) +...  21.2 us
    ppermute x4, waiting for transfers between devices, relayed_plane(): lax.ppermute(value, 'lon', at(lambda i: i ^ k, length))  16.1 us
    ppermute x2, waiting for transfers between devices, fast(): lax.ppermute(value, 'lon', at(lambda i: i ^ 2 * PLANE, lon_count))  7.38 us
    ppermute x6, starting transfers between devices, across_plane(): lax.ppermute(part, 'lon', at(lambda i: i ^ k, length))  7.04 us
    ppermute x2, starting transfers between devices, fast(): lax.ppermute(value, 'lon', at(lambda i: i ^ 2 * PLANE, lon_count))  6.45 us
    ppermute x2, waiting for transfers between devices, fast(): lax.ppermute(value, 'lon', at(lambda i: (i + lon_count // 2) % lon_count,...  6.11 us
    ppermute x4, starting transfers between devices, relayed_plane(): lax.ppermute(value, 'lon', at(lambda i: i ^ k, length))  5.32 us
    all_to_all x1, waiting for transfers between devices, fast(): lax.all_to_all(row_mixed, 'lon', split_axis=0, concat_axis=0, tiled=True)  4.94 us
  transfers between devices with their start and end apart: 30, of which 14 were waited for; matrix products, arithmetic and copies ran while one was open for 3% of the time, Pallas kernels for 18%

profile of v7, /device:TPU:0, one launch (start us, length us, event | category | flops | bytes accessed | tf_op | source)
XLA Modules:
  0.0 104.1 jit_solution(10975197846985945632)
XLA Ops:
  0.0 4.1 %collective-permute-start.9 = (bf16[64,256]{1,0:T(8,128)(2,1)}, bf16[64,256]{1,0:T(8,128)(2,1)S(1)}, u32[]{:S(2)}, u32[]{:S(2)}) collective-permute-start(bf16[64,256]{1,0:T(8,128)(2,1)} %param.19), channel_id=1, source_target_pairs={{0,16},{2,18},{4,20},{6,22},{8,24},{10,26},{12,28},{14,30},{16,0},... | collective-permute-start | bytes 98312 | tf_op jit(solution)/shard_map/ppermute | solution.py:405
  4.1 1.6 %collective-permute-start = (bf16[64,768]{1,0:T(8,128)(2,1)}, bf16[64,768]{1,0:T(8,128)(2,1)S(1)}, u32[]{:S(2)}, u32[]{:S(2)}) collective-permute-start(bf16[64,768]{1,0:T(8,128)(2,1)} %param.18), channel_id=1, source_target_pairs={{0,8},{2,10},{4,12},{6,14},{8,0},{10,2},{12,4},{14,6},{16,24},{18,... | collective-permute-start | bytes 294920 | tf_op jit(solution)/shard_map/ppermute | solution.py:86
  6.0 2.5 %collective-permute-start.2 = (bf16[64,768]{1,0:T(8,128)(2,1)}, bf16[64,768]{1,0:T(8,128)(2,1)S(1)}, u32[]{:S(2)}, u32[]{:S(2)}) collective-permute-start(bf16[64,768]{1,0:T(8,128)(2,1)} %param.18), channel_id=1, source_target_pairs={{0,24},{2,26},{4,28},{6,30},{8,16},{10,18},{12,20},{14,22},{16,8},... | collective-permute-start | bytes 294920 | tf_op jit(solution)/shard_map/ppermute | solution.py:86
  9.9 2.3 %loop_tokens.1 = (bf16[144,1024]{1,0:T(8,128)(2,1)}, bf16[144,1024]{1,0:T(8,128)(2,1)}, bf16[64,1024]{1,0:T(8,128)(2,1)}) custom-call(bf16[64,4,1024]{2,1,0:T(4,128)(2,1)} %refs_10_.1, s32[4,64]{1,0:T(4,128)} %bitcast.17, bf16[64,768]{1,0:T(8,128)(2,1)} %project.1, bf16[64,256]{1,0:T(8,128)(2,1)} %output.1), custom_call_target="tpu_custom_call" | custom-call | flops 1024 | bytes 1024 | tf_op jit(solution)/shard_map/loop_tokens/pallas_call | solution.py:42
  12.3 2.3 %collective-permute-start.14 = (bf16[64,1024]{1,0:T(8,128)(2,1)}, bf16[64,1024]{1,0:T(8,128)(2,1)S(1)}, u32[]{:S(2)}, u32[]{:S(2)}) collective-permute-start(bf16[64,1024]{1,0:T(8,128)(2,1)} %get-tuple-element.45), channel_id=1, source_target_pairs={{0,16},{2,18},{4,20},{6,22},{8,24},{10,26},{12,28},{14,30},{16,0},... | collective-permute-start | bytes 393224 | tf_op jit(solution)/shard_map/ppermute | solution.py:405
  15.4 2.2 %collective-permute-start.3 = (bf16[144,1024]{1,0:T(8,128)(2,1)}, bf16[144,1024]{1,0:T(8,128)(2,1)S(1)}, u32[]{:S(2)}, u32[]{:S(2)}) collective-permute-start(bf16[144,1024]{1,0:T(8,128)(2,1)} %get-tuple-element.38), channel_id=1, source_target_pairs={{0,16},{2,18},{4,20},{6,22},{8,24},{10,26},{12,28},{14,30},{16,0},... | collective-permute-start | bytes 884744 | tf_op jit(solution)/shard_map/ppermute | solution.py:402
  18.5 1.6 %collective-permute-start.6 = (bf16[256,768]{1,0:T(8,128)(2,1)S(1)}, bf16[256,768]{1,0:T(8,128)(2,1)S(1)}, u32[]{:S(2)}, u32[]{:S(2)}) collective-permute-start(bf16[256,768]{1,0:T(8,128)(2,1)S(1)} %pad_maximum_fusion.1.w0), channel_id=1, source_target_pairs={{0,2},{2,0},{4,6},{6,4},{8,10},{10,8},{12,14},{14,12},{16,18},{18,... | collective-permute-start | bytes 1179656 | tf_op jit(solution)/shard_map/ppermute | solution.py:96
  20.1 1.5 %collective-permute-start.7 = (bf16[256,768]{1,0:T(8,128)(2,1)S(1)}, bf16[256,768]{1,0:T(8,128)(2,1)S(1)}, u32[]{:S(2)}, u32[]{:S(2)}) collective-permute-start(bf16[256,768]{1,0:T(8,128)(2,1)S(1)} %pad_maximum_fusion.1.w0), channel_id=1, source_target_pairs={{0,4},{2,6},{4,0},{6,2},{8,12},{10,14},{12,8},{14,10},{16,20},{18,... | collective-permute-start | bytes 1179656 | tf_op jit(solution)/shard_map/ppermute | solution.py:96
  22.1 7.4 %collective-permute-done.14 = bf16[64,1024]{1,0:T(8,128)(2,1)S(1)} collective-permute-done((bf16[64,1024]{1,0:T(8,128)(2,1)}, bf16[64,1024]{1,0:T(8,128)(2,1)S(1)}, u32[]{:S(2)}, u32[]{:S(2)}) %collective-permute-start.14) | collective-permute-done | bytes 131104 | tf_op jit(solution)/shard_map/ppermute | solution.py:405
  30.4 5.0 %collective-permute-done.3.own.got = bf16[144,1024]{1,0:T(8,128)(2,1)S(1)} collective-permute-done((bf16[144,1024]{1,0:T(8,128)(2,1)}, bf16[144,1024]{1,0:T(8,128)(2,1)S(1)}, u32[]{:S(2)}, u32[]{:S(2)}) %collective-permute-start.3) | collective-permute-done | bytes 294944 | tf_op jit(solution)/shard_map/ppermute | solution.py:402
  41.7 1.6 %collective-permute-done.15 = bf16[128,1024]{1,0:T(8,128)(2,1)S(1)} collective-permute-done((bf16[128,1024]{1,0:T(8,128)(2,1)S(1)}, bf16[128,1024]{1,0:T(8,128)(2,1)S(1)}, u32[]{:S(2)}, u32[]{:S(2)}) %collective-permute-start.15) | collective-permute-done | bytes 262176 | tf_op jit(solution)/shard_map/ppermute | solution.py:90
  44.0 2.5 %column_attention.1 = (bf16[256,256]{1,0:T(8,128)(2,1)S(1)}, bf16[256,256]{1,0:T(8,128)(2,1)S(1)}) custom-call(f32[8]{0:T(128)S(1)} %copy-done.15, bf16[256,1024]{1,0:T(8,128)(2,1)S(1)} %column_normed.1.tokens, bf16[256,1024]{1,0:T(8,128)(2,1)S(1)} %far_normed.1.far_tokens, bf16[1024,768]{1,0:T(8,128)(2,1)S(1)} %column_project.1.weight), custom_call_target="tpu_custom_call" | custom-call | flops 1024 | bytes 262144 | tf_op jit(solution)/shard_map/column_attention/pallas_call | solution.py:42
  51.2 1.8 %row_normed.1 = bf16[256,1024]{1,0:T(8,128)(2,1)} custom-call(bf16[256,256]{1,0:T(8,128)(2,1)S(1)} %get-tuple-element.54.mine, bf16[256,256]{1,0:T(8,128)(2,1)S(1)} %collective-permute-done.16.theirs, bf16[1024,256]{1,0:T(8,128)(2,1)S(1)} %column_output.1.near, bf16[1024,256]{1,0:T(8,128)(2,1)S(1)} %collective-permute-done.17.far, ...), custom_call_target="tpu_custom_call" | custom-call | flops 1024 | bytes 1048576 | tf_op jit(solution)/shard_map/row_normed/pallas_call | solution.py:42
  53.0 4.1 %all-to-all-start = ((bf16[16,16,1024]{2,1,0:T(8,128)(2,1)}), bf16[16,16,1024]{2,1,0:T(8,128)(2,1)S(1)}, u32[]{:S(2)}, u32[]{:S(2)}) async-start(bf16[16,16,1024]{2,1,0:T(8,128)(2,1)} %bitcast.4), calls=%async_computation | async-start | bytes 1048576 | tf_op jit(solution)/shard_map/all_to_all | solution.py:465
  57.1 5.4 %collective-permute-done.18.refs_1_ = bf16[256,1024]{1,0:T(8,128)(2,1)S(1)} collective-permute-done((bf16[256,1024]{1,0:T(8,128)(2,1)S(1)}, bf16[256,1024]{1,0:T(8,128)(2,1)S(1)}, u32[]{:S(2)}, u32[]{:S(2)}) %collective-permute-start.18) | collective-permute-done | bytes 524320 | tf_op jit(solution)/shard_map/ppermute | solution.py:101
  62.5 3.1 %collective-permute-done.19.refs_2_ = bf16[256,1024]{1,0:T(8,128)(2,1)S(1)} collective-permute-done((bf16[256,1024]{1,0:T(8,128)(2,1)S(1)}, bf16[256,1024]{1,0:T(8,128)(2,1)S(1)}, u32[]{:S(2)}, u32[]{:S(2)}) %collective-permute-start.19) | collective-permute-done | bytes 524320 | tf_op jit(solution)/shard_map/ppermute | solution.py:101
  67.5 1.6 %collective-permute-start.21 = (bf16[128,1024]{1,0:T(8,128)(2,1)S(1)}, bf16[128,1024]{1,0:T(8,128)(2,1)S(1)}, u32[]{:S(2)}, u32[]{:S(2)}) collective-permute-start(bf16[128,1024]{1,0:T(8,128)(2,1)S(1)} %slice.46), channel_id=1, source_target_pairs={{0,4},{2,6},{4,0},{6,2},{8,12},{10,14},{12,8},{14,10},{16,20},{18,... | collective-permute-start | bytes 786440 | tf_op jit(solution)/shard_map/ppermute | solution.py:101
  69.1 6.5 %collective-permute-done.20.refs_3_ = bf16[128,1024]{1,0:T(8,128)(2,1)S(1)} collective-permute-done((bf16[128,1024]{1,0:T(8,128)(2,1)S(1)}, bf16[128,1024]{1,0:T(8,128)(2,1)S(1)}, u32[]{:S(2)}, u32[]{:S(2)}) %collective-permute-start.20) | collective-permute-done | bytes 262176 | tf_op jit(solution)/shard_map/ppermute | solution.py:101
  76.7 1.8 %collective-permute-start.27 = (bf16[128,512]{1,0:T(8,128)(2,1)S(1)}, bf16[128,512]{1,0:T(8,128)(2,1)S(1)}, u32[]{:S(2)}, u32[]{:S(2)}) collective-permute-start(bf16[128,512]{1,0:T(8,128)(2,1)S(1)} %pad_maximum_fusion.4), channel_id=1, source_target_pairs={{0,16},{2,18},{4,20},{6,22},{8,24},{10,26},{12,28},{14,30},{16,0},... | collective-permute-start | bytes 393224 | tf_op jit(solution)/shard_map/ppermute | solution.py:402
  79.5 5.6 %row_attention.1 = bf16[256,512]{1,0:T(8,128)(2,1)} custom-call(f32[8]{0:T(128)S(1)} %copy-done.14, bf16[256,1024]{1,0:T(8,128)(2,1)S(1)} %bitcast.8, bf16[256,1024]{1,0:T(8,128)(2,1)S(1)} %pad_maximum_fusion.refs_0_, bf16[256,1024]{1,0:T(8,128)(2,1)S(1)} %collective-permute-done.18.refs_1_, bf16[256,1024]{1,0:T(8,128)(2,1)} %copy-done.16, ...), custom_call_target="tpu_custom_call" | custom-call | flops 1024 | bytes 1024 | tf_op jit(solution)/shard_map/row_attention/pallas_call | solution.py:42
  86.3 4.3 %all-to-all-start.1 = ((bf16[16,16,512]{2,1,0:T(8,128)(2,1)}), bf16[16,16,512]{2,1,0:T(8,128)(2,1)S(1)}, u32[]{:S(2)}, u32[]{:S(2)}) async-start(bf16[16,16,512]{2,1,0:T(8,128)(2,1)} %bitcast.6), calls=%async_computation.1 | async-start | bytes 524288 | tf_op jit(solution)/shard_map/all_to_all | solution.py:485
  90.6 5.0 %middle.1 = (f32[256,1024]{1,0:T(8,128)}, bf16[2,1024,256]{2,1,0:T(8,128)(2,1)}) custom-call(bf16[256,256]{1,0:T(8,128)(2,1)} %copy-done.9, bf16[256,256]{1,0:T(8,128)(2,1)} %copy-done.10, bf16[128,512]{1,0:T(8,128)(2,1)} %copy-done.21, bf16[1024,256]{1,0:T(8,128)(2,1)} %copy-done.1, bf16[1024,256]{1,0:T(8,128)(2,1)} %copy-done.3, ...), custom_call_target="tpu_custom_call" | custom-call | flops 1024 | bytes 1024 | tf_op jit(solution)/shard_map/middle/pallas_call | solution.py:42
  95.7 4.9 %all-to-all-done.1 = bf16[16,16,512]{2,1,0:T(8,128)(2,1)S(1)} async-done(((bf16[16,16,512]{2,1,0:T(8,128)(2,1)}), bf16[16,16,512]{2,1,0:T(8,128)(2,1)S(1)}, u32[]{:S(2)}, u32[]{:S(2)}) %all-to-all-start.1) | async-done | bytes 262176 | tf_op jit(solution)/shard_map/all_to_all | solution.py:485
  101.3 2.8 %block_output.1 = bf16[64,4,1024]{2,1,0:T(4,128)(2,1)} custom-call(bf16[256,512]{1,0:T(8,128)(2,1)} %bitcast.16, f32[256,1024]{1,0:T(8,128)} %get-tuple-element.67.middle, bf16[2,1024,256]{2,1,0:T(8,128)(2,1)} %get-tuple-element.68.weight), custom_call_target="tpu_custom_call" | custom-call | flops 1024 | bytes 1024 | tf_op jit(solution)/shard_map/block_output/pallas_call | solution.py:42
  (105 shorter events, 22.3 us)
Async XLA Ops:
  0.0 8.5 %collective-permute-start.9 = (bf16[64,256]{1,0:T(8,128)(2,1)}, bf16[64,256]{1,0:T(8,128)(2,1)S(1)}, u32[]{:S(2)}, u32[]{:S(2)}) collective-permute-start(bf16[64,256]{1,0:T(8,128)(2,1)} %param.19), channel_id=1, source_target_pairs={{0,16},{2,18},{4,20},{6,22},{8,24},{10,26},{12,28},{14,30},{16,0},... | collective-permute-start | bytes 98312 | tf_op jit(solution)/shard_map/ppermute | solution.py:405
  4.1 8.2 %collective-permute-start = (bf16[64,768]{1,0:T(8,128)(2,1)}, bf16[64,768]{1,0:T(8,128)(2,1)S(1)}, u32[]{:S(2)}, u32[]{:S(2)}) collective-permute-start(bf16[64,768]{1,0:T(8,128)(2,1)} %param.18), channel_id=1, source_target_pairs={{0,8},{2,10},{4,12},{6,14},{8,0},{10,2},{12,4},{14,6},{16,24},{18,... | collective-permute-start | bytes 294920 | tf_op jit(solution)/shard_map/ppermute | solution.py:86
  5.7 9.7 %collective-permute-start.1 = (bf16[64,768]{1,0:T(8,128)(2,1)}, bf16[64,768]{1,0:T(8,128)(2,1)S(1)}, u32[]{:S(2)}, u32[]{:S(2)}) collective-permute-start(bf16[64,768]{1,0:T(8,128)(2,1)} %param.18), channel_id=1, source_target_pairs={{0,16},{2,18},{4,20},{6,22},{8,24},{10,26},{12,28},{14,30},{16,0},... | collective-permute-start | bytes 294920 | tf_op jit(solution)/shard_map/ppermute | solution.py:86
  6.0 9.4 %collective-permute-start.2 = (bf16[64,768]{1,0:T(8,128)(2,1)}, bf16[64,768]{1,0:T(8,128)(2,1)S(1)}, u32[]{:S(2)}, u32[]{:S(2)}) collective-permute-start(bf16[64,768]{1,0:T(8,128)(2,1)} %param.18), channel_id=1, source_target_pairs={{0,24},{2,26},{4,28},{6,30},{8,16},{10,18},{12,20},{14,22},{16,8},... | collective-permute-start | bytes 294920 | tf_op jit(solution)/shard_map/ppermute | solution.py:86
  9.3 8.3 %collective-permute-start.10 = (bf16[128,256]{1,0:T(8,128)(2,1)S(1)}, bf16[128,256]{1,0:T(8,128)(2,1)S(1)}, u32[]{:S(2)}, u32[]{:S(2)}) collective-permute-start(bf16[128,256]{1,0:T(8,128)(2,1)S(1)} %pad_maximum_fusion.5), channel_id=1, source_target_pairs={{0,8},{2,10},{4,12},{6,14},{8,0},{10,2},{12,4},{14,6},{16,24},{18,... | collective-permute-start | bytes 196616 | tf_op jit(solution)/shard_map/ppermute | solution.py:90
  12.3 17.1 %collective-permute-start.14 = (bf16[64,1024]{1,0:T(8,128)(2,1)}, bf16[64,1024]{1,0:T(8,128)(2,1)S(1)}, u32[]{:S(2)}, u32[]{:S(2)}) collective-permute-start(bf16[64,1024]{1,0:T(8,128)(2,1)} %get-tuple-element.45), channel_id=1, source_target_pairs={{0,16},{2,18},{4,20},{6,22},{8,24},{10,26},{12,28},{14,30},{16,0},... | collective-permute-start | bytes 393224 | tf_op jit(solution)/shard_map/ppermute | solution.py:405
  15.4 19.9 %collective-permute-start.3 = (bf16[144,1024]{1,0:T(8,128)(2,1)}, bf16[144,1024]{1,0:T(8,128)(2,1)S(1)}, u32[]{:S(2)}, u32[]{:S(2)}) collective-permute-start(bf16[144,1024]{1,0:T(8,128)(2,1)} %get-tuple-element.38), channel_id=1, source_target_pairs={{0,16},{2,18},{4,20},{6,22},{8,24},{10,26},{12,28},{14,30},{16,0},... | collective-permute-start | bytes 884744 | tf_op jit(solution)/shard_map/ppermute | solution.py:402
  18.5 18.9 %collective-permute-start.6 = (bf16[256,768]{1,0:T(8,128)(2,1)S(1)}, bf16[256,768]{1,0:T(8,128)(2,1)S(1)}, u32[]{:S(2)}, u32[]{:S(2)}) collective-permute-start(bf16[256,768]{1,0:T(8,128)(2,1)S(1)} %pad_maximum_fusion.1.w0), channel_id=1, source_target_pairs={{0,2},{2,0},{4,6},{6,4},{8,10},{10,8},{12,14},{14,12},{16,18},{18,... | collective-permute-start | bytes 1179656 | tf_op jit(solution)/shard_map/ppermute | solution.py:96
  20.1 18.1 %collective-permute-start.7 = (bf16[256,768]{1,0:T(8,128)(2,1)S(1)}, bf16[256,768]{1,0:T(8,128)(2,1)S(1)}, u32[]{:S(2)}, u32[]{:S(2)}) collective-permute-start(bf16[256,768]{1,0:T(8,128)(2,1)S(1)} %pad_maximum_fusion.1.w0), channel_id=1, source_target_pairs={{0,4},{2,6},{4,0},{6,2},{8,12},{10,14},{12,8},{14,10},{16,20},{18,... | collective-permute-start | bytes 1179656 | tf_op jit(solution)/shard_map/ppermute | solution.py:96
  21.6 16.6 %collective-permute-start.8 = (bf16[256,768]{1,0:T(8,128)(2,1)S(1)}, bf16[256,768]{1,0:T(8,128)(2,1)S(1)}, u32[]{:S(2)}, u32[]{:S(2)}) collective-permute-start(bf16[256,768]{1,0:T(8,128)(2,1)S(1)} %pad_maximum_fusion.1.w0), channel_id=1, source_target_pairs={{0,6},{2,4},{4,2},{6,0},{8,14},{10,12},{12,10},{14,8},{16,22},{18,... | collective-permute-start | bytes 1179656 | tf_op jit(solution)/shard_map/ppermute | solution.py:96
  35.3 7.9 %collective-permute-start.15 = (bf16[128,1024]{1,0:T(8,128)(2,1)S(1)}, bf16[128,1024]{1,0:T(8,128)(2,1)S(1)}, u32[]{:S(2)}, u32[]{:S(2)}) collective-permute-start(bf16[128,1024]{1,0:T(8,128)(2,1)S(1)} %pad_maximum_fusion.2), channel_id=1, source_target_pairs={{0,8},{2,10},{4,12},{6,14},{8,0},{10,2},{12,4},{14,6},{16,24},{18,... | collective-permute-start | bytes 786440 | tf_op jit(solution)/shard_map/ppermute | solution.py:90
  38.2 8.4 %collective-permute-start.11 = (bf16[256,256]{1,0:T(8,128)(2,1)S(1)}, bf16[256,256]{1,0:T(8,128)(2,1)S(1)}, u32[]{:S(2)}, u32[]{:S(2)}) collective-permute-start(bf16[256,256]{1,0:T(8,128)(2,1)S(1)} %pad_maximum_fusion.3.w0), channel_id=1, source_target_pairs={{0,2},{2,0},{4,6},{6,4},{8,10},{10,8},{12,14},{14,12},{16,18},{18,... | collective-permute-start | bytes 393224 | tf_op jit(solution)/shard_map/ppermute | solution.py:96
  39.4 7.8 %collective-permute-start.12 = (bf16[256,256]{1,0:T(8,128)(2,1)S(1)}, bf16[256,256]{1,0:T(8,128)(2,1)S(1)}, u32[]{:S(2)}, u32[]{:S(2)}) collective-permute-start(bf16[256,256]{1,0:T(8,128)(2,1)S(1)} %pad_maximum_fusion.3.w0), channel_id=1, source_target_pairs={{0,4},{2,6},{4,0},{6,2},{8,12},{10,14},{12,8},{14,10},{16,20},{18,... | collective-permute-start | bytes 393224 | tf_op jit(solution)/shard_map/ppermute | solution.py:96
  40.5 6.7 %collective-permute-start.13 = (bf16[256,256]{1,0:T(8,128)(2,1)S(1)}, bf16[256,256]{1,0:T(8,128)(2,1)S(1)}, u32[]{:S(2)}, u32[]{:S(2)}) collective-permute-start(bf16[256,256]{1,0:T(8,128)(2,1)S(1)} %pad_maximum_fusion.3.w0), channel_id=1, source_target_pairs={{0,6},{2,4},{4,2},{6,0},{8,14},{10,12},{12,10},{14,8},{16,22},{18,... | collective-permute-start | bytes 393224 | tf_op jit(solution)/shard_map/ppermute | solution.py:96
  47.3 15.2 %collective-permute-start.18 = (bf16[256,1024]{1,0:T(8,128)(2,1)S(1)}, bf16[256,1024]{1,0:T(8,128)(2,1)S(1)}, u32[]{:S(2)}, u32[]{:S(2)}) collective-permute-start(bf16[256,1024]{1,0:T(8,128)(2,1)S(1)} %pad_maximum_fusion.refs_0_), channel_id=1, source_target_pairs={{0,2},{2,0},{4,6},{6,4},{8,10},{10,8},{12,14},{14,12},{16,18},{18,... | collective-permute-start | bytes 1572872 | tf_op jit(solution)/shard_map/ppermute | solution.py:101
  48.5 17.1 %collective-permute-start.19 = (bf16[256,1024]{1,0:T(8,128)(2,1)S(1)}, bf16[256,1024]{1,0:T(8,128)(2,1)S(1)}, u32[]{:S(2)}, u32[]{:S(2)}) collective-permute-start(bf16[256,1024]{1,0:T(8,128)(2,1)S(1)} %pad_maximum_fusion.refs_0_), channel_id=1, source_target_pairs={{0,4},{2,6},{4,0},{6,2},{8,12},{10,14},{12,8},{14,10},{16,20},{18,... | collective-permute-start | bytes 1572872 | tf_op jit(solution)/shard_map/ppermute | solution.py:101
  53.0 26.5 %all-to-all-start = ((bf16[16,16,1024]{2,1,0:T(8,128)(2,1)}), bf16[16,16,1024]{2,1,0:T(8,128)(2,1)S(1)}, u32[]{:S(2)}, u32[]{:S(2)}) async-start(bf16[16,16,1024]{2,1,0:T(8,128)(2,1)} %bitcast.4), calls=%async_computation | async-start | bytes 1048576 | tf_op jit(solution)/shard_map/all_to_all | solution.py:465
  65.7 11.0 %collective-permute-start.22 = (bf16[256,1024]{1,0:T(8,128)(2,1)S(1)}, bf16[256,1024]{1,0:T(8,128)(2,1)S(1)}, u32[]{:S(2)}, u32[]{:S(2)}) collective-permute-start(bf16[256,1024]{1,0:T(8,128)(2,1)S(1)} %pad_maximum_fusion.refs_0_), channel_id=1, source_target_pairs={{0,1},{1,0},{2,3},{3,2},{4,5},{5,4},{6,7},{7,6},{8,9},{9,8},{10,11... | collective-permute-start | bytes 1572872 | tf_op jit(solution)/shard_map/ppermute | solution.py:23
  65.7 9.9 %collective-permute-start.20 = (bf16[128,1024]{1,0:T(8,128)(2,1)S(1)}, bf16[128,1024]{1,0:T(8,128)(2,1)S(1)}, u32[]{:S(2)}, u32[]{:S(2)}) collective-permute-start(bf16[128,1024]{1,0:T(8,128)(2,1)S(1)} %slice.45), channel_id=1, source_target_pairs={{0,2},{2,0},{4,6},{6,4},{8,10},{10,8},{12,14},{14,12},{16,18},{18,... | collective-permute-start | bytes 786440 | tf_op jit(solution)/shard_map/ppermute | solution.py:101
  66.9 11.6 %collective-permute-start.23 = (bf16[256,1024]{1,0:T(8,128)(2,1)S(1)}, bf16[256,1024]{1,0:T(8,128)(2,1)S(1)}, u32[]{:S(2)}, u32[]{:S(2)}) collective-permute-start(bf16[256,1024]{1,0:T(8,128)(2,1)S(1)} %collective-permute-done.18.refs_1_), channel_id=1, source_target_pairs={{0,1},{1,0},{2,3},{3,2},{4,5},{5,4},{6,7},{7,6},{8,9},{9,8},{10,11... | collective-permute-start | bytes 1572872 | tf_op jit(solution)/shard_map/ppermute | solution.py:23
  67.2 11.3 %collective-permute-start.24 = (bf16[256,1024]{1,0:T(8,128)(2,1)S(1)}, bf16[256,1024]{1,0:T(8,128)(2,1)S(1)}, u32[]{:S(2)}, u32[]{:S(2)}) collective-permute-start(bf16[256,1024]{1,0:T(8,128)(2,1)S(1)} %collective-permute-done.19.refs_2_), channel_id=1, source_target_pairs={{0,1},{1,0},{2,3},{3,2},{4,5},{5,4},{6,7},{7,6},{8,9},{9,8},{10,11... | collective-permute-start | bytes 1572872 | tf_op jit(solution)/shard_map/ppermute | solution.py:23
  67.5 9.2 %collective-permute-start.21 = (bf16[128,1024]{1,0:T(8,128)(2,1)S(1)}, bf16[128,1024]{1,0:T(8,128)(2,1)S(1)}, u32[]{:S(2)}, u32[]{:S(2)}) collective-permute-start(bf16[128,1024]{1,0:T(8,128)(2,1)S(1)} %slice.46), channel_id=1, source_target_pairs={{0,4},{2,6},{4,0},{6,2},{8,12},{10,14},{12,8},{14,10},{16,20},{18,... | collective-permute-start | bytes 786440 | tf_op jit(solution)/shard_map/ppermute | solution.py:101
  76.7 9.6 %collective-permute-start.27 = (bf16[128,512]{1,0:T(8,128)(2,1)S(1)}, bf16[128,512]{1,0:T(8,128)(2,1)S(1)}, u32[]{:S(2)}, u32[]{:S(2)}) collective-permute-start(bf16[128,512]{1,0:T(8,128)(2,1)S(1)} %pad_maximum_fusion.4), channel_id=1, source_target_pairs={{0,16},{2,18},{4,20},{6,22},{8,24},{10,26},{12,28},{14,30},{16,0},... | collective-permute-start | bytes 393224 | tf_op jit(solution)/shard_map/ppermute | solution.py:402
  86.3 14.3 %all-to-all-start.1 = ((bf16[16,16,512]{2,1,0:T(8,128)(2,1)}), bf16[16,16,512]{2,1,0:T(8,128)(2,1)S(1)}, u32[]{:S(2)}, u32[]{:S(2)}) async-start(bf16[16,16,512]{2,1,0:T(8,128)(2,1)} %bitcast.6), calls=%async_computation.1 | async-start | bytes 524288 | tf_op jit(solution)/shard_map/all_to_all | solution.py:485
  (29 other events, 317.2 us)
